TPU v7x, 32 devices: a whole 2x2x4 slice. The times are simulated.
32 devices in a mesh: dp: 8 (over z, x), shard: 4 (over y, core).
Axes of the slice: x: 2, y: 2, z: 4, core: 2. Of those that a mesh axis runs over, the one named last changes fastest.
Arguments:
- tokens: bfloat16 [32768, 1024], P(('dp', 'shard')), may hold values from -6 to 6
- cotangent: bfloat16 [32768, 1024], P(('dp', 'shard')), may hold values from -6 to 6
- segment_ids: int32 [32768], P(('dp', 'shard')), may hold values from 0 to 5, as said below
- group_counts: int32 [8], replicated, may hold values from 50 to 400
- master_qkv: float32 [1024, 3072], P('dp', 'shard'), may hold values from -0.1875 to 0.1875
- master_out: float32 [1024, 1024], P('dp', 'shard'), may hold values from -1 to 1
- master_up: float32 [1024, 4096], P('dp', 'shard'), may hold values from -0.1875 to 0.1875
- master_down: float32 [4096, 1024], P('dp', 'shard'), may hold values from -0.09375 to 0.09375
- moment_qkv: float32 [1024, 3072], P('dp', 'shard')
- moment_out: float32 [1024, 1024], P('dp', 'shard')
- moment_up: float32 [1024, 4096], P('dp', 'shard')
- moment_down: float32 [4096, 1024], P('dp', 'shard')
- square_qkv: float32 [1024, 3072], P('dp', 'shard'), as said below
- square_out: float32 [1024, 1024], P('dp', 'shard'), as said below
- square_up: float32 [1024, 4096], P('dp', 'shard'), as said below
- square_down: float32 [4096, 1024], P('dp', 'shard'), as said below
- norm_params: float32 [4, 1024], replicated, as said below
- norm_moment: float32 [4, 1024], replicated
- norm_square: float32 [4, 1024], replicated, as said below
Outputs:
- block_out: bfloat16 [32768, 1024], P(('dp', 'shard'))
- input_grad: float32 [32768, 1024], P(('dp', 'shard'))
- grad_qkv: float32 [1024, 3072], P('dp', 'shard')
- grad_out: float32 [1024, 1024], P('dp', 'shard')
- grad_up: float32 [1024, 4096], P('dp', 'shard')
- grad_down: float32 [4096, 1024], P('dp', 'shard')
- new_qkv: float32 [1024, 3072], P('dp', 'shard')
- new_out: float32 [1024, 1024], P('dp', 'shard')
- new_up: float32 [1024, 4096], P('dp', 'shard')
- new_down: float32 [4096, 1024], P('dp', 'shard')
- new_moment_qkv: float32 [1024, 3072], P('dp', 'shard')
- new_moment_out: float32 [1024, 1024], P('dp', 'shard')
- new_moment_up: float32 [1024, 4096], P('dp', 'shard')
- new_moment_down: float32 [4096, 1024], P('dp', 'shard')
- new_square_qkv: float32 [1024, 3072], P('dp', 'shard')
- new_square_out: float32 [1024, 1024], P('dp', 'shard')
- new_square_up: float32 [1024, 4096], P('dp', 'shard')
- new_square_down: float32 [4096, 1024], P('dp', 'shard')
- copy_qkv: bfloat16 [1024, 3072], P('dp', 'shard')
- copy_out: bfloat16 [1024, 1024], P('dp', 'shard')
- copy_up: bfloat16 [1024, 4096], P('dp', 'shard')
- copy_down: bfloat16 [4096, 1024], P('dp', 'shard')
- norm_grad: float32 [4, 1024], replicated
- new_norm: float32 [4, 1024], replicated
- new_norm_moment: float32 [4, 1024], replicated
- new_norm_square: float32 [4, 1024], replicated
Inputs may be any that keep to these rules, and one draw needn't show every extreme that they name: `segment_ids`: in each packed row of 256 tokens the ids number whole images in order, with the padding tokens as one more id placed before, between or after whole images; every row of one group holds images of 50 tokens or every row holds images of 145 tokens, and both kinds of group occur. `norm_params`: gains near one, shifts near zero. `norm_square`: every entry positive. `square_qkv`: every entry positive. `square_out`: every entry positive. `square_up`: every entry positive. `square_down`: every entry positive.
All inputs are finite; a program needn't handle non-finite values.
Results may differ from a plain program's by a relative error of at most 0.012.
Values may be sent and summed in bfloat16 or wider, within the bound.
No kernel may reach another device: no remote copies, remote signals or barrier semaphores. Data moves between devices by JAX's collectives and lax.ppermute only.
A program may use at most 256 MiB of HBM per device.

v0:
```python
import functools
import math

import jax
import jax.numpy as jnp
from jax import lax
from jax.experimental import pallas as pl
from jax.experimental.pallas import tpu as pltpu
from jax.sharding import PartitionSpec as P

HEADS = 16
HD = 64
SEQ = 256
STEP = 3

NORM_EPSILON = 1e-06
BETA_FIRST = 0.5
BETA_SECOND = 0.5
ADAM_EPSILON = 1e-08
RATE_MATRIX = 0.02
RATE_OUTPUT = 0.1
RATE_NORMS = 0.3
WEIGHT_DECAY = 0.01
MASK_FILL = -1000000000.0
SCALING = 1.0 / math.sqrt(HD)
PLAIN = (((1,), (0,)), ((), ()))
TRANSPOSED = (((1,), (1,)), ((), ()))
LEADING = (((0,), (0,)), ((), ()))

F32 = jnp.float32
BF16 = jnp.bfloat16
MIB = 2**20


def dot(left, right, dims=PLAIN):
    return lax.dot_general(left, right, dims, preferred_element_type=F32)


def wide(values):
    return values.astype(F32)


def thin(values):
    return values.astype(BF16)


def shape_of(dims, dtype):
    return jax.ShapeDtypeStruct(dims, dtype)


def limits(mib):
    return pltpu.CompilerParams(vmem_limit_bytes=mib * MIB)


def cost(flops, moved, transcendentals=0):
    return pl.CostEstimate(flops=flops, bytes_accessed=moved, transcendentals=transcendentals)


def entire(array):
    return pl.BlockSpec(array.shape, lambda *_: (0,) * array.ndim)


class Grid:
    def __init__(self, dp, shard):
        self.dp, self.shard, self.depth = dp, shard, dp // 2

    def core_swap(self, values):
        return lax.ppermute(values, "shard", [(i, i ^ 1) for i in range(self.shard)])

    def cross(self, values, turned):
        pairs = []
        for d in range(self.dp):
            for s in range(self.shard):
                along_x = (s % 2 == 0) != turned
                other = (d ^ 1, s) if along_x else (d, s ^ 2)
                pairs.append((d * self.shard + s, other[0] * self.shard + other[1]))
        return lax.ppermute(values, ("dp", "shard"), pairs)

    def z_exchange(self, values):
        groups = [[z * 2 + x for z in range(self.depth)] for x in range(2)]
        return lax.all_to_all(values, "dp", 0, 0, axis_index_groups=groups, tiled=True)

    def total(self, values, axis):
        size = self.shard if axis == "shard" else self.dp
        for bit in range((size - 1).bit_length()):
            pairs = [(i, i ^ (1 << bit)) for i in range(size)]
            values = values + lax.ppermute(values, axis, pairs)
        return values


    def copies(self, piece):
        return jnp.broadcast_to(piece, (self.depth, *piece.shape))

    def gather_z(self, piece):
        parts = [piece]
        for k in range(1, self.depth):
            shift = [((i // 2 + k) % self.depth * 2 + i % 2, i) for i in range(self.dp)]
            parts.append(lax.ppermute(piece, "dp", shift))
        return jnp.stack(parts)

    def both(self, near):
        return near, self.core_swap(near)

    def gather_xy(self, near):
        return [self.cross(values, False) for values in near]

    def gather_far(self, over):
        return self.cross(over[0], True)

    def gather_end(self, near, over, far):
        mine = [*over, far]
        return [*near, *mine, *[self.core_swap(values) for values in mine]]


    def gather_xy_joined(self, near):
        return self.cross(jnp.concatenate(near), False)

    def gather_far_joined(self, over):
        return self.cross(over[: self.depth], True)

    def gather_end_joined(self, near, over, far):
        return [*near, over, far, self.core_swap(over), self.core_swap(far)]

    def owner(self, z, dx, dy, dc):
        index_dp, index_shard = lax.axis_index("dp"), lax.axis_index("shard")
        x, y, c = index_dp % 2, index_shard // 2, index_shard % 2
        row = z * 2 + lax.rem(x + dx, 2)
        column = lax.rem(y + dy, 2) * 2 + lax.rem(c + dc, 2)
        return row, column

    def gathered_places(self, turned, joined):
        where = (2, 2, 4, 4, 3, 5) if joined else (2, 3, 5, 6, 4, 7)
        skip = self.depth if joined else 0
        core = lax.rem(lax.axis_index("shard"), 2)
        own = lax.axis_index("dp") // 2
        places = []
        for k in range(self.depth):
            z = lax.rem(own + k, self.depth) if turned else k
            for side in range(2):
                places.append((side, k, self.owner(z, 0, 0, side)))
                beyond = side * skip + k
                places.append((where[side], beyond, self.owner(z, 1 - core, core, side)))
                places.append((where[2 + side], beyond, self.owner(z, core, 1 - core, 1 - side)))
            places.append((where[4], k, self.owner(z, 1, 1, 0)))
            places.append((where[5], k, self.owner(z, 1, 1, 1)))
        return places

    def region(self, other):
        core = lax.rem(lax.axis_index("shard"), 2)
        role = 1 - core if other else core
        flip = 1 if other else 0
        depth = range(self.depth)
        blocks = [self.owner(k, 1 - role, role, (flip + side) % 2) for side in range(2) for k in depth]
        blocks += [self.owner(k, 1, 1, flip) for k in depth]
        return blocks + [self.owner(k, 0, 0, flip) for k in depth]


    def scatter_core(self, far):
        return self.core_swap(far)

    def scatter_far(self, near, other):
        corner = slice(2 * self.depth, 3 * self.depth)
        return self.cross(thin(wide(near[corner]) + wide(other[corner])), True)

    def scatter_xy(self, near, other, far):
        d = self.depth
        first = wide(near[:d]) + wide(other[:d]) + wide(far)
        second = wide(near[d : 2 * d]) + wide(other[d : 2 * d])
        return [self.cross(thin(second), False), self.cross(thin(first), False)][::-1]

    def scatter_home(self, over):
        return self.core_swap(over[1])

    def scatter_z(self, near, other, over, passed):
        d = self.depth
        home = slice(3 * d, 4 * d)
        here = wide(near[home]) + wide(other[home]) + wide(over[0]) + wide(passed)
        return self.z_exchange(thin(here))

    def scatter_end(self, sent):
        return jnp.sum(wide(sent), axis=0)


def tie(*values):
    return lax.optimization_barrier(values)


def block(ref, row, rows, column, columns):
    return ref.at[
        pl.ds(pl.multiple_of(row, rows), rows), pl.ds(pl.multiple_of(column, columns), columns)
    ]


def start_copies(pairs, sems):
    copies = [pltpu.make_async_copy(a, b, sems.at[n]) for n, (a, b) in enumerate(pairs)]
    for copy in copies:
        copy.start()
    return copies


def run_copies(pairs, sems):
    for copy in start_copies(pairs, sems):
        copy.wait()


def piece_loads(grid, refs, lane, target, lanes, across, offset, turned=True):
    rows = target.shape[0] // grid.dp
    pairs = []
    for i, place, (row, column) in grid.gathered_places(turned, len(refs) == 6):
        source = refs[i].at[place, :, pl.ds(lane, lanes)]
        pairs.append((source, block(target, row * rows, rows, column * across + offset, lanes)))
    return pairs


def block_stores(grid, source, lanes, near, far, lane):
    rows = source.shape[0] // grid.dp
    pairs = []
    for other in (1, 0):
        for n, (row, column) in enumerate(grid.region(other)):
            taken = block(source, row * rows, rows, column * lanes, lanes)
            pairs.append((taken, (near, far)[other].at[n, :, pl.ds(lane, lanes)]))
    return pairs


ANYWHERE = pl.BlockSpec(memory_space=pl.ANY)
SCALAR = pl.BlockSpec(memory_space=pltpu.SMEM)
HELD = pl.BlockSpec(memory_space=pltpu.VMEM)


def standardised(values):
    centred = values - jnp.mean(values, axis=-1, keepdims=True)
    inverse = lax.rsqrt(jnp.mean(centred * centred, axis=-1, keepdims=True) + NORM_EPSILON)
    return centred * inverse, inverse


def norm_back(grad, values, gain):
    n, inverse = standardised(values)
    scaled = grad * gain
    mean_scaled = jnp.mean(scaled, axis=-1, keepdims=True)
    mean_product = jnp.mean(scaled * n, axis=-1, keepdims=True)
    grad_values = inverse * (scaled - mean_scaled - n * mean_product)
    return (
        grad_values,
        jnp.sum(grad * n, axis=0, keepdims=True),
        jnp.sum(grad, axis=0, keepdims=True),
    )


def first_projection(grid, sets, cuts, tokens, norms):
    count, width = tokens.shape
    halves = len(sets)
    each = len(sets[0])
    across = sum(cuts)
    columns = across * grid.shard
    owners = grid.dp * grid.shard
    tile = width

    def kernel(x_ref, p_ref, *refs):
        sources, rest = refs[: halves * each], refs[halves * each :]
        turned_ref, joined_hbm, weight_hbm, weight, first, joined, sems, out_sems = rest
        pairs = []
        for n in range(halves):
            pieces = sources[n * each : (n + 1) * each]
            pairs += piece_loads(grid, pieces, 0, weight, cuts[n], across, sum(cuts[:n]))
        loads = start_copies(pairs, sems)

        @pl.loop(0, count, step=SEQ)
        def _(i):
            rows = pl.ds(pl.multiple_of(i, SEQ), SEQ)
            n, _ = standardised(wide(x_ref[rows, :]))
            value = thin(n * p_ref[0:1, :] + p_ref[1:2, :])
            first[rows, :] = value
            turned_ref[:, rows] = value.T

        for load in loads:
            load.wait()
        leaving = start_copies([(weight, weight_hbm)], out_sems)
        for n in range(columns // tile):
            own = slice(n * tile, (n + 1) * tile)
            joined[:, own] = thin(dot(first[...], weight[:, own]))
            pair = (joined.at[:, own], joined_hbm.at[:, own])
            leaving += start_copies([pair], out_sems.at[pl.ds(1 + n, 1)])
        for copy in leaving:
            copy.wait()

    return pl.pallas_call(
        kernel,
        out_shape=(
            shape_of((width, count), BF16),
            shape_of((count, columns), BF16),
            shape_of((width, columns), BF16),
        ),
        in_specs=[HELD, HELD] + [ANYWHERE] * (halves * each),
        out_specs=(HELD, ANYWHERE, ANYWHERE),
        scratch_shapes=[
            pltpu.VMEM((width, columns), BF16),
            pltpu.VMEM((count, width), BF16),
            pltpu.VMEM((count, columns), BF16),
            pltpu.SemaphoreType.DMA((halves * owners,)),
            pltpu.SemaphoreType.DMA((1 + columns // tile,)),
        ],
        compiler_params=limits(60),
        cost_estimate=cost(2 * count * width * columns, 4 * (width + count) * columns),
    )(tokens, norms, *[array for pieces in sets for array in pieces])


def attention(grid, pieces, lane, joined, seg_column, seg_row, tokens, norms):
    count, width = tokens.shape

    def kernel(
        j_ref, sc_ref, sr_ref, x_ref, p_ref, *refs,
    ):
        sources, rest = refs[: len(pieces)], refs[len(pieces) :]
        turned_ref, log_ref, res_ref, second_ref, second_turned_ref, mixed, weight, sems = rest
        lanes = width // grid.shard
        step = pl.program_id(0)

        @pl.when(step == 0)
        def _():
            start_copies(piece_loads(grid, sources, lane, weight, lanes, lanes, 0), sems)

        same = sc_ref[...] == sr_ref[0]
        left = lax.broadcasted_iota(jnp.int32, (SEQ, 2 * HD), 1) < HD
        for pair in range(HEADS // 2):
            a, b = pair * 2 * HD, (pair + 1) * 2 * HD
            query, key = j_ref[:, a:b], j_ref[:, width + a : width + b]
            value = j_ref[:, 2 * width + a : 2 * width + b]
            results = []
            for side in range(2):
                own_key = jnp.where(left == (side == 0), key, jnp.zeros_like(key))
                scores = jnp.where(same, dot(own_key, query, TRANSPOSED) * SCALING, MASK_FILL)
                top = jnp.max(scores, axis=0, keepdims=True)
                raised = jnp.exp(scores - top)
                total = jnp.sum(raised, axis=0, keepdims=True)
                head = 2 * pair + side
                log_ref[0, head : head + 1, :] = top + jnp.log(total)
                results.append(dot(thin(raised * (1.0 / total)), value, LEADING))
            mixed[:, a:b] = thin(jnp.where(left, results[0], results[1]))
        turned_ref[...] = mixed[...].T

        @pl.when(step == 0)
        def _():
            for n, (a, b) in enumerate(piece_loads(grid, sources, lane, weight, lanes, lanes, 0)):
                pltpu.make_async_copy(a, b, sems.at[n]).wait()

        residual = wide(x_ref[...]) + dot(mixed[...], weight[...])
        res_ref[...] = residual
        n, _ = standardised(residual)
        second = thin(n * p_ref[2:3, :] + p_ref[3:4, :])
        second_ref[...] = second
        second_turned_ref[...] = second.T

    blocks = count // SEQ

    def rows(columns):
        return pl.BlockSpec((SEQ, columns), lambda r: (r, 0))

    turned = pl.BlockSpec((width, SEQ), lambda r: (0, r))
    return pl.pallas_call(
        kernel,
        grid=(blocks,),
        out_shape=(
            shape_of((width, count), BF16),
            shape_of((blocks, HEADS, SEQ), F32),
            shape_of((count, width), F32),
            shape_of((count, width), BF16),
            shape_of((width, count), BF16),
        ),
        in_specs=[
            rows(3 * width),
            rows(1),
            pl.BlockSpec((1, 1, SEQ), lambda r: (r, 0, 0)),
            rows(width),
            entire(norms),
        ]
        + [ANYWHERE] * len(pieces),
        out_specs=(
            turned,
            pl.BlockSpec((1, HEADS, SEQ), lambda r: (r, 0, 0)),
            rows(width),
            rows(width),
            turned,
        ),
        scratch_shapes=[
            pltpu.VMEM((SEQ, width), BF16),
            pltpu.VMEM((width, width), BF16),
            pltpu.SemaphoreType.DMA((grid.dp * grid.shard,)),
        ],
        compiler_params=limits(60),
        cost_estimate=cost(
            4 * count * width * width + 16 * count * SEQ * width,
            20 * count * width,
            count * SEQ * HEADS,
        ),
    )(joined, seg_column, seg_row, tokens, norms, *pieces)


def gelu_and_slope(values):
    below = 0.5 * (1.0 + lax.erf(values * (1.0 / math.sqrt(2.0))))
    density = jnp.exp(-0.5 * values * values) * (1.0 / math.sqrt(2.0 * math.pi))
    return values * below, below + values * density


def feed_forward(grid, pieces, second, second_turned, cotangent, factor, sums, regions,
                 region_lane, region_lanes, up_lanes, down_lanes, turned):
    count, width = second.shape
    columns = up_lanes * grid.shard
    rows = width // grid.dp
    owners = grid.dp * grid.shard
    region = shape_of((4 * grid.depth, rows, region_lanes), BF16)
    used = len(pieces)

    def kernel(f_ref, s_hbm, st_hbm, c_hbm, *refs):
        sources, rest = refs[:used], refs[used:]
        if sums:
            out_in, back_in = rest[:2]
        (
            out_hbm, back_hbm, near, far, s_ref, st_ref, c_ref, up, down, out_sum, back_sum, hidden, grads,
            gu, gd, sems, sum_sems, row_sems,
        ) = rest[len(sums) + len(regions) :]
        up_sems, down_sems = sems.at[pl.ds(0, owners)], sems.at[pl.ds(owners, owners)]
        up_loads = start_copies([(s_hbm, s_ref)], row_sems.at[pl.ds(0, 1)])
        up_loads += start_copies(piece_loads(grid, sources, 0, up, up_lanes, up_lanes, 0, turned), up_sems)
        down_loads = start_copies([(c_hbm, c_ref)], row_sems.at[pl.ds(1, 1)])
        down_loads += start_copies(
            piece_loads(grid, sources, up_lanes, down, down_lanes, down_lanes, 0, turned), down_sems
        )
        if sums:
            arriving = start_copies([(out_in, out_sum), (back_in, back_sum)], sum_sems)
        turned_load = start_copies([(st_hbm, st_ref)], row_sems.at[pl.ds(2, 1)])
        for load in up_loads:
            load.wait()
        value, slope = gelu_and_slope(dot(s_ref[...], up[...]))
        for load in down_loads:
            load.wait()
        hidden[...] = thin(value)
        grads[...] = thin(dot(c_ref[...], down[...], TRANSPOSED) * slope)
        if sums:
            for copy in arriving:
                copy.wait()
            out_sum[...] += dot(hidden[...], down[...])
            back_sum[...] += dot(grads[...], up[...], TRANSPOSED)
        else:
            out_sum[...] = dot(hidden[...], down[...])
            back_sum[...] = dot(grads[...], up[...], TRANSPOSED)
        leaving = start_copies([(out_sum, out_hbm), (back_sum, back_hbm)], sum_sems)
        turned_load[0].wait()
        gu[...] = thin(dot(st_ref[...], grads[...]) * f_ref[0, 0])
        leaving += start_copies(block_stores(grid, gu, up_lanes, near, far, region_lane), up_sems)
        gd[...] = thin(dot(hidden[...], c_ref[...], LEADING) * f_ref[0, 0])
        leaving += start_copies(
            block_stores(grid, gd, down_lanes, near, far, region_lane + up_lanes), down_sems
        )
        for copy in leaving:
            copy.wait()

    aliases = {4 + used + n: n for n in range(len(sums))}
    aliases |= {4 + used + len(sums) + n: 2 + n for n in range(len(regions))}
    return pl.pallas_call(
        kernel,
        out_shape=(shape_of((count, width), F32),) * 2 + (region, region),
        in_specs=[SCALAR] + [ANYWHERE] * (3 + used + len(sums) + len(regions)),
        out_specs=(ANYWHERE,) * 4,
        scratch_shapes=[
            pltpu.VMEM((count, width), BF16),
            pltpu.VMEM((width, count), BF16),
            pltpu.VMEM((count, width), BF16),
            pltpu.VMEM((width, columns), BF16),
            pltpu.VMEM((columns, width), BF16),
            pltpu.VMEM((count, width), F32),
            pltpu.VMEM((count, width), F32),
            pltpu.VMEM((count, columns), BF16),
            pltpu.VMEM((count, columns), BF16),
            pltpu.VMEM((width, columns), BF16),
            pltpu.VMEM((columns, width), BF16),
            pltpu.SemaphoreType.DMA((2 * owners,)),
            pltpu.SemaphoreType.DMA((2,)),
            pltpu.SemaphoreType.DMA((3,)),
        ],
        input_output_aliases=aliases,
        compiler_params=limits(60),
        cost_estimate=cost(
            12 * count * width * columns,
            8 * width * columns + 22 * count * width,
            2 * count * columns,
        ),
    )(factor, second, second_turned, cotangent, *pieces, *sums, *regions)


def second_norm_back(grid, pieces, lane, sums, residual, cotangent, norms):
    out_sum, back_sum = sums
    count, width = residual.shape

    def kernel(o_ref, b_ref, res_ref, c_ref, p_ref, *refs):
        sources, rest = refs[: len(pieces)], refs[len(pieces) :]
        out_ref, grad_ref, ga_ref, gm_ref, terms_ref, weight, sems = rest
        lanes = width // grid.shard

        @pl.when(pl.program_id(0) == 0)
        def _():
            terms_ref[...] = jnp.zeros_like(terms_ref)
            run_copies(piece_loads(grid, sources, lane, weight, lanes, lanes, 0), sems)

        residual = res_ref[...]
        out_ref[...] = thin(residual + o_ref[...])
        part, gain, shift = norm_back(b_ref[...], residual, p_ref[2:3, :])
        terms_ref[0:1, :] += gain
        terms_ref[1:2, :] += shift
        grad = wide(c_ref[...]) + part
        grad_ref[...] = grad
        ga_ref[...] = thin(grad)
        gm_ref[...] = thin(dot(ga_ref[...], weight[...], TRANSPOSED))

    rows = pl.BlockSpec((SEQ, width), lambda r: (r, 0))
    return pl.pallas_call(
        kernel,
        grid=(count // SEQ,),
        out_shape=(
            shape_of((count, width), BF16),
            shape_of((count, width), F32),
            shape_of((count, width), BF16),
            shape_of((count, width), BF16),
            shape_of((2, width), F32),
        ),
        in_specs=[rows, rows, rows, rows, entire(norms)] + [ANYWHERE] * len(pieces),
        out_specs=(rows, rows, rows, rows, pl.BlockSpec((2, width), lambda r: (0, 0))),
        scratch_shapes=[
            pltpu.VMEM((width, width), BF16),
            pltpu.SemaphoreType.DMA((grid.dp * grid.shard,)),
        ],
        compiler_params=limits(60),
        cost_estimate=cost(2 * count * width * width, 24 * count * width),
    )(out_sum, back_sum, residual, cotangent, norms, *pieces)


def attention_back(first, blocks, joined, grad_mixed, logs, seg_column, seg_row):
    width = grad_mixed.shape[1]
    count = blocks * SEQ

    def kernel(j_ref, gm_ref, log_ref, sc_ref, sr_ref, gj_ref):
        same = sc_ref[...] == sr_ref[0]
        left = lax.broadcasted_iota(jnp.int32, (SEQ, 2 * HD), 1) < HD
        for pair in range(HEADS // 2):
            a, b = pair * 2 * HD, (pair + 1) * 2 * HD
            query, key = j_ref[:, a:b], j_ref[:, width + a : width + b]
            value, grad = j_ref[:, 2 * width + a : 2 * width + b], gm_ref[:, a:b]
            turned_key = key.T
            grad_query, results = [], []
            for side in range(2):
                chosen = left == (side == 0)
                own_key = jnp.where(chosen, key, jnp.zeros_like(key))
                own_value = jnp.where(chosen, value, jnp.zeros_like(value))
                scores = jnp.where(same, dot(own_key, query, TRANSPOSED) * SCALING, MASK_FILL)
                head = 2 * pair + side
                probs = jnp.exp(scores - log_ref[0, head : head + 1, :])
                grad_probs = dot(own_value, grad, TRANSPOSED)
                delta = jnp.sum(probs * grad_probs, axis=0, keepdims=True)
                grad_scores = thin(probs * (grad_probs - delta))
                grad_query.append(dot(turned_key[side * HD : (side + 1) * HD], grad_scores))
                results.append((dot(grad_scores, query) * SCALING, dot(thin(probs), grad)))
            gj_ref[:, a:b] = thin(jnp.concatenate(grad_query).T * SCALING)
            for n, (even, odd) in enumerate(zip(*results), 1):
                gj_ref[:, n * width + a : n * width + b] = thin(jnp.where(left, even, odd))

    def rows(columns):
        return pl.BlockSpec((SEQ, columns), lambda r: (r + first, 0))

    return pl.pallas_call(
        kernel,
        grid=(blocks,),
        out_shape=shape_of((count, 3 * width), BF16),
        in_specs=[
            rows(3 * width),
            rows(width),
            pl.BlockSpec((1, HEADS, SEQ), lambda r: (r + first, 0, 0)),
            rows(1),
            pl.BlockSpec((1, 1, SEQ), lambda r: (r + first, 0, 0)),
        ],
        out_specs=pl.BlockSpec((SEQ, 3 * width), lambda r: (r, 0)),
        compiler_params=limits(60),
        cost_estimate=cost(40 * count * SEQ * width, 14 * count * width, count * SEQ * HEADS),
    )(joined, grad_mixed, logs, seg_column, seg_row)


def first_norm_back(grad_joined, grad_residual, tokens, norms, weight):
    count, width = tokens.shape
    parts = len(grad_joined)
    blocks = count // SEQ // parts

    def kernel(*refs):
        gj_refs, (g_ref, x_ref, p_ref, w_ref, out_ref, terms_ref) = refs[:parts], refs[parts:]
        step = pl.program_id(0)

        @pl.when(step == 0)
        def _():
            terms_ref[...] = jnp.zeros_like(terms_ref)

        for n in range(parts):

            @pl.when(lax.div(step, blocks) == n)
            def _(n=n):
                grad_first = dot(gj_refs[n][...], w_ref[...], TRANSPOSED)
                part, gain, shift = norm_back(grad_first, wide(x_ref[...]), p_ref[0:1, :])
                terms_ref[0:1, :] += gain
                terms_ref[1:2, :] += shift
                out_ref[...] = g_ref[...] + part

    rows = pl.BlockSpec((SEQ, width), lambda r: (r, 0))

    def part_rows(n):
        return pl.BlockSpec(
            (SEQ, 3 * width), lambda r: (jnp.clip(r - n * blocks, 0, blocks - 1), 0)
        )

    return pl.pallas_call(
        kernel,
        grid=(count // SEQ,),
        out_shape=(shape_of((count, width), F32), shape_of((2, width), F32)),
        in_specs=[part_rows(n) for n in range(parts)] + [rows, rows, entire(norms), entire(weight)],
        out_specs=(rows, pl.BlockSpec((2, width), lambda r: (0, 0))),
        compiler_params=limits(60),
        cost_estimate=cost(6 * count * width * width, 16 * count * width + 6 * width * width),
    )(*grad_joined, grad_residual, tokens, norms, weight)


def weight_grad(grid, turned, grads, factor, lanes, across, offset, regions, region_lane, region_lanes):
    width, count = turned.shape
    parts = len(grads)
    share = count // parts
    columns = lanes * grid.shard
    region = shape_of((4 * grid.depth, width // grid.dp, region_lanes), BF16)

    def kernel(f_ref, t_ref, *refs):
        near, far, grad, whole, sems, load_sems = refs[parts + len(regions) :]
        pairs = []
        for n in range(parts):
            for s in range(grid.shard):
                source = refs[n].at[:, pl.ds(s * across + offset, lanes)]
                rows = pl.ds(n * share, share)
                pairs.append((source, grad.at[rows, pl.ds(s * lanes, lanes)]))
        run_copies(pairs, load_sems)
        whole[...] = thin(dot(t_ref[...], grad[...]) * f_ref[0, 0])
        run_copies(block_stores(grid, whole, lanes, near, far, region_lane), sems)

    return pl.pallas_call(
        kernel,
        out_shape=(region, region),
        in_specs=[SCALAR, HELD] + [ANYWHERE] * (parts + len(regions)),
        out_specs=(ANYWHERE,) * 2,
        scratch_shapes=[
            pltpu.VMEM((count, columns), BF16),
            pltpu.VMEM((width, columns), BF16),
            pltpu.SemaphoreType.DMA((grid.dp * grid.shard,)),
            pltpu.SemaphoreType.DMA((parts * grid.shard,)),
        ],
        input_output_aliases={2 + parts + n: n for n in range(len(regions))},
        compiler_params=limits(60),
        cost_estimate=cost(
            2 * count * width * columns, 2 * (width * count + (width + count) * columns)
        ),
    )(factor, turned, *grads, *regions)


def adam_update(master, moment, square, gradient, rate):
    new_moment = BETA_FIRST * moment + (1.0 - BETA_FIRST) * gradient
    new_square = BETA_SECOND * square + (1.0 - BETA_SECOND) * gradient * gradient
    bias_first = 1.0 - BETA_FIRST**STEP
    bias_second = 1.0 - BETA_SECOND**STEP
    update = new_moment / bias_first / (jnp.sqrt(new_square / bias_second) + ADAM_EPSILON)
    new_master = master - rate * (update + WEIGHT_DECAY * master)
    return (new_master, new_moment, new_square)


def local(
    grid,
    tokens,
    cotangent,
    segment_ids,
    group_counts,
    master_qkv,
    master_out,
    master_up,
    master_down,
    moment_qkv,
    moment_out,
    moment_up,
    moment_down,
    square_qkv,
    square_out,
    square_up,
    square_down,
    norm_params,
    norm_moment,
    norm_square,
):
    rows, out_lanes = master_up.shape[0], master_out.shape[1]
    qkv_lanes = master_qkv.shape[1]
    chunks = master_down.shape[0] // rows
    up_lanes = master_up.shape[1] // chunks
    down_lanes = master_down.shape[1]
    per_shard = grid.dp // grid.shard
    blocks = tokens.shape[0] // SEQ
    both_lanes = up_lanes + down_lanes

    up_cut = thin(master_up).reshape(rows, per_shard, chunks, up_lanes // per_shard)
    down_cut = thin(master_down).reshape(chunks, rows, down_lanes)
    cuts = (qkv_lanes - out_lanes, out_lanes)

    def large(*members):
        parts = []
        for n in members:
            parts += [up_cut[:, :, n].reshape(rows, up_lanes), down_cut[n]]
        return jnp.concatenate(parts, axis=1)

    counts = group_counts.astype(F32)
    own_count = jnp.sum(jnp.where(jnp.arange(counts.shape[0]) == lax.axis_index("dp"), counts, 0.0))
    factor = own_count * counts.shape[0] / jnp.sum(counts)
    factor_cell = factor.reshape(1, 1)
    seg_column = segment_ids[:, None]
    seg_row = segment_ids.reshape(blocks, 1, SEQ)

    piece = jnp.concatenate([thin(master_qkv[:, cuts[0] :]), thin(master_out)], axis=1)
    q0 = grid.gather_z(thin(master_qkv[:, : cuts[0]]))
    q0, piece = tie(grid.both(q0), piece)
    q0_over = grid.gather_xy(q0)
    q1 = grid.gather_z(piece)
    q0_over, q1, piece = tie(q0_over, grid.both(q1), large(0, 1))
    q1_over = grid.gather_xy(q1)
    q0_far = grid.gather_far(q0_over)
    m01 = grid.gather_z(piece)
    q1_over, q0_far, m01 = tie(q1_over, q0_far, m01)
    q0_pieces = grid.gather_end(q0, q0_over, q0_far)
    q1_far = grid.gather_far(q1_over)
    m01 = grid.both(m01)
    q1_far, m01 = tie(q1_far, m01)
    q1_pieces = grid.gather_end(q1, q1_over, q1_far)

    def halves(pair):
        lanes = [slice(n * both_lanes, (n + 1) * both_lanes) for n in range(2)]
        return [[values[:, :, own] for values in pair] for own in lanes]

    m0, m1 = halves(m01)

    q0_pieces, q1_pieces, m0, piece = tie(q0_pieces, q1_pieces, m0, large(2, 3))
    first_turned, joined, qkv_weight = first_projection(
        grid, [q0_pieces, q1_pieces], cuts, tokens, norm_params
    )
    m0_over = grid.gather_xy_joined(m0)
    m23 = grid.z_exchange(grid.copies(piece))

    joined, m0_over, m1 = tie(joined, m0_over, m1)
    mixed_turned, logs, residual, second, second_turned = attention(
        grid, q1_pieces, cuts[1], joined, seg_column, seg_row, tokens, norm_params
    )
    m0_far = grid.gather_far_joined(m0_over)
    m1_over = grid.gather_xy_joined(m1)
    second, m0_far, m1_over, m23 = tie(second, m0_far, m1_over, m23)
    m0_pieces = grid.gather_end_joined(m0, m0_over, m0_far)
    m2, m3 = halves(grid.both(m23))

    def chunk(weights, sums, regions, place, turned):
        out_sum, back_sum, near, far = feed_forward(
            grid, weights, second, second_turned, cotangent, factor_cell, sums, regions,
            place * both_lanes, 2 * both_lanes, up_lanes, down_lanes, turned,
        )
        return (out_sum, back_sum), (near, far)

    second, m0_pieces, m1_over, m2 = tie(second, m0_pieces, m1_over, m2)
    sums, r0 = chunk(m0_pieces, (), (), 0, True)
    m1_far = grid.gather_far_joined(m1_over)
    m2_over = grid.gather_xy_joined(m2)
    sums, m1_far, m2_over = tie(sums, m1_far, m2_over)
    m1_pieces = grid.gather_end_joined(m1, m1_over, m1_far)

    sums, m1_pieces, m2_over, m3 = tie(sums, m1_pieces, m2_over, m3)
    sums, r0 = chunk(m1_pieces, sums, r0, 1, True)
    m2_far = grid.gather_far_joined(m2_over)
    m3_over = grid.gather_xy_joined(m3)
    sums, m2_far, m3_over = tie(sums, m2_far, m3_over)
    m2_pieces = grid.gather_end_joined(m2, m2_over, m2_far)

    sums, m2_pieces, r0, m3_over = tie(sums, m2_pieces, r0, m3_over)
    sums, r1 = chunk(m2_pieces, sums, (), 0, False)
    r0_other = grid.scatter_core(r0[1])
    m3_far = grid.gather_far_joined(m3_over)
    sums, m3_far, r0_other = tie(sums, m3_far, r0_other)
    m3_pieces = grid.gather_end_joined(m3, m3_over, m3_far)

    sums, r0_other, m3_pieces = tie(sums, r0_other, m3_pieces)
    sums, r1 = chunk(m3_pieces, sums, r1, 1, False)
    r0_far = grid.scatter_far(r0[0], r0_other)

    sums, r0_far, r1 = tie(sums, r0_far, r1)
    block_out, grad_residual, grad_attention, grad_mixed, second_terms = second_norm_back(
        grid, q1_pieces, cuts[1], sums, residual, cotangent, norm_params
    )
    r0_over = grid.scatter_xy(r0[0], r0_other, r0_far)
    r1_other = grid.scatter_core(r1[1])
    q1 = weight_grad(
        grid, mixed_turned, [grad_attention], factor_cell, out_lanes, out_lanes, 0,
        (), cuts[1], cuts[1] + out_lanes,
    )

    grad_mixed, r0_over, r1_other, q1 = tie(grad_mixed, r0_over, r1_other, q1)
    grad_joined = [attention_back(0, blocks // 2, joined, grad_mixed, logs, seg_column, seg_row)]
    r1_far = grid.scatter_far(r1[0], r1_other)
    r0_passed = grid.scatter_home(r0_over)
    grad_mixed, grad_joined, r1_far, r0_passed = tie(grad_mixed, grad_joined, r1_far, r0_passed)
    grad_joined.append(
        attention_back(blocks // 2, blocks // 2, joined, grad_mixed, logs, seg_column, seg_row)
    )
    r1_over = grid.scatter_xy(r1[0], r1_other, r1_far)
    r0_sent = grid.scatter_z(r0[0], r0_other, r0_over, r0_passed)
    q0 = weight_grad(
        grid, first_turned, grad_joined, factor_cell, cuts[0], qkv_lanes, 0, (), 0, cuts[0]
    )
    grad_joined, q0, r1_over, r0_sent = tie(grad_joined, q0, r1_over, r0_sent)
    q0_other = grid.scatter_core(q0[1])
    r1_passed = grid.scatter_home(r1_over)
    q1 = weight_grad(
        grid, first_turned, grad_joined, factor_cell, cuts[1], qkv_lanes, cuts[0],
        q1, 0, cuts[1] + out_lanes,
    )

    grad_joined, q0_other, q1, r1_passed = tie(grad_joined, q0_other, q1, r1_passed)
    q0_far = grid.scatter_far(q0[0], q0_other)
    q1_other = grid.scatter_core(q1[1])
    q0_far, q1_other = tie(q0_far, q1_other)
    q0_over = grid.scatter_xy(q0[0], q0_other, q0_far)
    q1_far = grid.scatter_far(q1[0], q1_other)
    r1_sent = grid.scatter_z(r1[0], r1_other, r1_over, r1_passed)
    input_grad, first_terms = first_norm_back(
        grad_joined, grad_residual, tokens, norm_params, qkv_weight
    )
    first_terms, q0_over, q1_far = tie(first_terms, q0_over, q1_far)
    q0_passed = grid.scatter_home(q0_over)
    q1_over = grid.scatter_xy(q1[0], q1_other, q1_far)
    q0_sent = grid.scatter_z(q0[0], q0_other, q0_over, q0_passed)
    terms = jnp.concatenate([first_terms, second_terms]) * factor
    terms = grid.total(terms, "shard")
    q1_over, terms = tie(q1_over, terms)
    q1_passed = grid.scatter_home(q1_over)
    q1_sent = grid.scatter_z(q1[0], q1_other, q1_over, q1_passed)
    norm_grad = grid.total(terms, "dp")
    q0_total, q1_total = grid.scatter_end(q0_sent), grid.scatter_end(q1_sent)
    grad_qkv = jnp.concatenate([q0_total, q1_total[:, : cuts[1]]], axis=1)
    grad_out = q1_total[:, cuts[1] :]
    totals = [grid.scatter_end(r0_sent), grid.scatter_end(r1_sent)]

    def pieces_of(first, lanes):
        return [
            t[:, i * both_lanes + first : i * both_lanes + first + lanes]
            for t in totals
            for i in range(chunks // 2)
        ]

    grad_up = jnp.stack(
        [piece.reshape(rows, per_shard, -1) for piece in pieces_of(0, up_lanes)], axis=2
    ).reshape(master_up.shape)
    grad_down = jnp.concatenate(pieces_of(up_lanes, down_lanes))
    new_qkv, new_moment_qkv, new_square_qkv = adam_update(
        master_qkv, moment_qkv, square_qkv, grad_qkv, RATE_MATRIX
    )
    new_out, new_moment_out, new_square_out = adam_update(
        master_out, moment_out, square_out, grad_out, RATE_OUTPUT
    )
    new_up, new_moment_up, new_square_up = adam_update(
        master_up, moment_up, square_up, grad_up, RATE_MATRIX
    )
    new_down, new_moment_down, new_square_down = adam_update(
        master_down, moment_down, square_down, grad_down, RATE_MATRIX
    )
    new_norm, new_norm_moment, new_norm_square = adam_update(
        norm_params, norm_moment, norm_square, norm_grad, RATE_NORMS
    )
    return (
        block_out,
        input_grad,
        grad_qkv,
        grad_out,
        grad_up,
        grad_down,
        new_qkv,
        new_out,
        new_up,
        new_down,
        new_moment_qkv,
        new_moment_out,
        new_moment_up,
        new_moment_down,
        new_square_qkv,
        new_square_out,
        new_square_up,
        new_square_down,
        thin(new_qkv),
        thin(new_out),
        thin(new_up),
        thin(new_down),
        norm_grad,
        new_norm,
        new_norm_moment,
        new_norm_square,
    )


def solution(mesh):
    rows = P(("dp", "shard"), None)
    owned = P("dp", "shard")
    in_specs = (rows, rows, P(("dp", "shard")), P()) + (owned,) * 12 + (P(),) * 3
    out_specs = (rows, rows) + (owned,) * 20 + (P(),) * 4
    step = functools.partial(local, Grid(mesh.shape["dp"], mesh.shape["shard"]))
    return jax.shard_map(step, mesh=mesh, in_specs=in_specs, out_specs=out_specs, check_vma=False)
```

profile of v0, /device:TPU:0, one launch (start us, length us, event | category | flops | bytes accessed | tf_op | source)
XLA Modules:
  0.0 424.8 jit_solution(13536501587093519099)
XLA Ops:
  1.8 4.1 collective-permute-start.1
  8.0 5.9 %collective-permute-done.1 = bf16[128,512]{1,0:T(8,128)(2,1)S(1)} collective-permute-done((bf16[128,512]{1,0:T(8,128)(2,1)S(1)}, bf16[128,512]{1,0:T(8,128)(2,1)S(1)}, u32[]{:S(2)}, u32[]{:S(2)}) %collective-permute-start.1) | collective-permute-done | bytes 131104 | tf_op jit(solution)/shard_map/ppermute | solution.py:98
  13.9 2.4 collective-permute-done.2
  16.8 1.6 collective-permute-done.3.refs_1_
  18.3 2.4 collective-permute-start.8
  20.7 1.9 collective-permute-start.7
  22.6 2.9 collective-permute-start.6
  25.5 1.7 slice_reduce_fusion.1
  27.2 1.6 collective-permute-start.4
  29.3 2.1 collective-permute-done.7
  31.6 4.8 %collective-permute-done.4.refs_2_ = bf16[4,128,512]{2,1,0:T(8,128)(2,1)S(1)} collective-permute-done((bf16[4,128,512]{2,1,0:T(8,128)(2,1)S(1)}, bf16[4,128,512]{2,1,0:T(8,128)(2,1)S(1)}, u32[]{:S(2)}, u32[]{:S(2)}) %collective-permute-start.4) | collective-permute-done | bytes 524320 | tf_op jit(solution)/shard_map/ppermute | solution.py:77
  36.5 5.6 %collective-permute-done.5.refs_3_ = bf16[4,128,512]{2,1,0:T(8,128)(2,1)S(1)} collective-permute-done((bf16[4,128,512]{2,1,0:T(8,128)(2,1)S(1)}, bf16[4,128,512]{2,1,0:T(8,128)(2,1)S(1)}, u32[]{:S(2)}, u32[]{:S(2)}) %collective-permute-start.5) | collective-permute-done | bytes 524320 | tf_op jit(solution)/shard_map/ppermute | solution.py:77
  42.1 1.6 collective-permute-start.10
  46.2 7.0 %collective-permute-done.15 = bf16[128,1024]{1,0:T(8,128)(2,1)S(1)} collective-permute-done((bf16[128,1024]{1,0:T(8,128)(2,1)S(1)}, bf16[128,1024]{1,0:T(8,128)(2,1)S(1)}, u32[]{:S(2)}, u32[]{:S(2)}) %collective-permute-start.15) | collective-permute-done | bytes 262176 | tf_op jit(solution)/shard_map/ppermute | solution.py:98
  53.3 8.7 %collective-permute-done.14 = bf16[128,1024]{1,0:T(8,128)(2,1)S(1)} collective-permute-done((bf16[128,1024]{1,0:T(8,128)(2,1)S(1)}, bf16[128,1024]{1,0:T(8,128)(2,1)S(1)}, u32[]{:S(2)}, u32[]{:S(2)}) %collective-permute-start.14) | collective-permute-done | bytes 262176 | tf_op jit(solution)/shard_map/ppermute | solution.py:98
  62.0 1.7 collective-permute-done.13
  63.9 1.6 collective-permute-start.19
  66.3 6.9 %collective-permute-done.19.refs_12_.refs_4_ = bf16[4,128,512]{2,1,0:T(8,128)(2,1)S(1)} collective-permute-done((bf16[4,128,512]{2,1,0:T(8,128)(2,1)S(1)}, bf16[4,128,512]{2,1,0:T(8,128)(2,1)S(1)}, u32[]{:S(2)}, u32[]{:S(2)}) %collective-permute-start.19) | collective-permute-done | bytes 524320 | tf_op jit(solution)/shard_map/ppermute | solution.py:77
  80.6 5.9 %all-to-all-start = ((bf16[4,128,1024]{2,1,0:T(8,128)(2,1)}), bf16[4,128,1024]{2,1,0:T(8,128)(2,1)S(1)}, u32[]{:S(2)}, u32[]{:S(2)}) async-start(bf16[4,128,1024]{2,1,0:T(8,128)(2,1)} %broadcast_in_dim.12), calls=%async_computation | async-start | bytes 2097152 | tf_op jit(solution)/shard_map/all_to_all | solution.py:81
  86.5 14.5 %shard_map.386 = (bf16[1024,1024]{1,0:T(8,128)(2,1)}, bf16[1024,3072]{1,0:T(8,128)(2,1)}, bf16[1024,3072]{1,0:T(8,128)(2,1)}) custom-call(bf16[1024,1024]{1,0:T(8,128)(2,1)} %refs_3_.1, f32[4,1024]{1,0:T(4,128)} %refs_4_.1, bf16[4,128,512]{2,1,0:T(8,128)(2,1)} %copy-done.27, bf16[4,128,512]{2,1,0:T(8,128)(2,1)} %copy-done.45, ...), custom_call_target="tpu_custom_call" | custom-call | flops 6442450944 | bytes 25165824 | tf_op jit(solution)/shard_map/pallas_call | solution.py:286
  103.9 1.6 collective-permute-start.25
  105.5 18.6 %shard_map.387 = (bf16[1024,1024]{1,0:T(8,128)(2,1)}, f32[4,16,256]{2,1,0:T(8,128)}, f32[1024,1024]{1,0:T(8,128)}, bf16[1024,1024]{1,0:T(8,128)(2,1)}, bf16[1024,1024]{1,0:T(8,128)(2,1)}) custom-call(bf16[1024,3072]{1,0:T(8,128)(2,1)} %get-tuple-element.229.j_ref, s32[1024,1]{1,0:T(8,128)} %copy.66.sc_ref, s32[4,1,256]{2,1,0:T(1,128)} %bitcast.43, ...), custom_call_target="tpu_custom_call" | custom-call | flops 8589934592 | bytes 20971520 | tf_op jit(solution)/shard_map/pallas_call | solution.py:359
  132.1 1.5 collective-permute-start.31
  133.6 20.1 %shard_map.388 = (f32[1024,1024]{1,0:T(8,128)}, f32[1024,1024]{1,0:T(8,128)}, bf16[16,128,1024]{2,1,0:T(8,128)(2,1)}, bf16[16,128,1024]{2,1,0:T(8,128)(2,1)}) custom-call(f32[1,1]{1,0:T(1,128)} %bitcast.f_ref, bf16[1024,1024]{1,0:T(8,128)(2,1)} %get-tuple-element.239.s_hbm, bf16[1024,1024]{1,0:T(8,128)(2,1)} %get-tuple-element.240.st_hbm, ...), custom_call_target="tpu_custom_call" | custom-call | flops 12884901888 | bytes 31457280 | tf_op jit(solution)/shard_map/pallas_call | solution.py:459
  153.8 2.1 collective-permute-done.33.refs_5_
  160.2 20.0 %shard_map.389 = (f32[1024,1024]{1,0:T(8,128)}, f32[1024,1024]{1,0:T(8,128)}, bf16[16,128,1024]{2,1,0:T(8,128)(2,1)}, bf16[16,128,1024]{2,1,0:T(8,128)(2,1)}) custom-call(f32[1,1]{1,0:T(1,128)} %bitcast.f_ref, bf16[1024,1024]{1,0:T(8,128)(2,1)} %get-tuple-element.239.s_hbm, ...), custom_call_target="tpu_custom_call", output_to_operand_aliasing={{0}: (10, {}), {1}: (11, {}), {2}: (12, {}), {3}: (13, {})} | custom-call | flops 12884901888 | bytes 31457280 | tf_op jit(solution)/shard_map/pallas_call | solution.py:459
  180.3 2.1 collective-permute-done.37.refs_5_
  183.6 20.0 %shard_map.390 = (f32[1024,1024]{1,0:T(8,128)}, f32[1024,1024]{1,0:T(8,128)}, bf16[16,128,1024]{2,1,0:T(8,128)(2,1)}, bf16[16,128,1024]{2,1,0:T(8,128)(2,1)}) custom-call(f32[1,1]{1,0:T(1,128)} %bitcast.f_ref, bf16[1024,1024]{1,0:T(8,128)(2,1)} %get-tuple-element.239.s_hbm, ...), custom_call_target="tpu_custom_call", output_to_operand_aliasing={{0}: (10, {}), {1}: (11, {})} | custom-call | flops 12884901888 | bytes 31457280 | tf_op jit(solution)/shard_map/pallas_call | solution.py:459
  206.2 2.0 add_convert_fusion.7
  209.3 20.2 %shard_map.391 = (f32[1024,1024]{1,0:T(8,128)}, f32[1024,1024]{1,0:T(8,128)}, bf16[16,128,1024]{2,1,0:T(8,128)(2,1)}, bf16[16,128,1024]{2,1,0:T(8,128)(2,1)}) custom-call(f32[1,1]{1,0:T(1,128)} %bitcast.f_ref, bf16[1024,1024]{1,0:T(8,128)(2,1)} %get-tuple-element.239.s_hbm, ...), custom_call_target="tpu_custom_call", output_to_operand_aliasing={{0}: (10, {}), {1}: (11, {}), {2}: (12, {}), {3}: (13, {})} | custom-call | flops 12884901888 | bytes 31457280 | tf_op jit(solution)/shard_map/pallas_call | solution.py:459
  229.6 3.4 add_convert_fusion.5
  233.0 1.6 collective-permute-start.44
  235.1 12.7 %shard_map.392 = (bf16[1024,1024]{1,0:T(8,128)(2,1)}, f32[1024,1024]{1,0:T(8,128)}, bf16[1024,1024]{1,0:T(8,128)(2,1)}, bf16[1024,1024]{1,0:T(8,128)(2,1)}, f32[2,1024]{1,0:T(2,128)}) custom-call(f32[1024,1024]{1,0:T(8,128)} %get-tuple-element.309.o_ref, f32[1024,1024]{1,0:T(8,128)} %get-tuple-element.310.b_ref, f32[1024,1024]{1,0:T(8,128)} %get-tuple-element.311.res_ref, ...), custom_call_target="tpu_custom_call" | custom-call | flops 2147483648 | bytes 25165824 | tf_op jit(solution)/shard_map/pallas_call | solution.py:515
  247.8 7.1 %shard_map.393 = (bf16[16,128,512]{2,1,0:T(8,128)(2,1)}, bf16[16,128,512]{2,1,0:T(8,128)(2,1)}) custom-call(f32[1,1]{1,0:T(1,128)} %bitcast.f_ref, bf16[1024,1024]{1,0:T(8,128)(2,1)} %get-tuple-element.316.t_ref, bf16[1024,1024]{1,0:T(8,128)(2,1)} %get-tuple-element.317.refs_0_), custom_call_target="tpu_custom_call" | custom-call | flops 2147483648 | bytes 6291456 | tf_op jit(solution)/shard_map/pallas_call | solution.py:645
  254.9 4.3 %collective-permute-done.43 = bf16[4,128,1024]{2,1,0:T(8,128)(2,1)S(1)} collective-permute-done((bf16[4,128,1024]{2,1,0:T(8,128)(2,1)S(1)}, bf16[4,128,1024]{2,1,0:T(8,128)(2,1)S(1)}, u32[]{:S(2)}, u32[]{:S(2)}) %collective-permute-start.43) | collective-permute-done | bytes 1048608 | tf_op jit(solution)/shard_map/ppermute | solution.py:77
  259.1 2.9 add_convert_fusion.4
  263.4 14.0 %shard_map.394.refs_0_ = bf16[512,3072]{1,0:T(8,128)(2,1)} custom-call(bf16[1024,3072]{1,0:T(8,128)(2,1)} %get-tuple-element.229.j_ref, bf16[1024,1024]{1,0:T(8,128)(2,1)} %get-tuple-element.326.gm_ref, f32[4,16,256]{2,1,0:T(8,128)} %get-tuple-element.321.log_ref, s32[1024,1]{1,0:T(8,128)} %copy.66.sc_ref, s32[4,1,256]{2,1,0:T(1,128)} %bitcast.44), custom_call_target="tpu_custom_call" | custom-call | flops 5368709120 | bytes 7340032 | tf_op jit(solution)/shard_map/pallas_call | solution.py:568
  277.4 3.5 add_convert_fusion.1
  280.9 5.1 %all-to-all-start.1 = ((bf16[4,128,1024]{2,1,0:T(8,128)(2,1)}), bf16[4,128,1024]{2,1,0:T(8,128)(2,1)S(1)}, u32[]{:S(2)}, u32[]{:S(2)}) async-start(bf16[4,128,1024]{2,1,0:T(8,128)(2,1)} %add_convert_fusion.1), calls=%async_computation.1 | async-start | bytes 2097152 | tf_op jit(solution)/shard_map/all_to_all | solution.py:81
  286.0 4.4 %add_convert_fusion.2 = (bf16[4,128,1024]{2,1,0:T(8,128)(2,1)}, bf16[4,128,1024]{2,1,0:T(8,128)(2,1)S(1)}) fusion(bf16[16,128,1024]{2,1,0:T(8,128)(2,1)} %collective-permute-done.45, bf16[16,128,1024]{2,1,0:T(8,128)(2,1)} %get-tuple-element.322, bf16[4,128,1024]{2,1,0:T(8,128)(2,1)S(1)} %collective-permute-done.46), kind=kLoop, calls=%fused_computation.4 | loop fusion | flops 5242880 | bytes 7340032 | tf_op jit(solution)/shard_map/convert_element_type | solution.py:44
  292.5 13.8 %shard_map.395.refs_1_ = bf16[512,3072]{1,0:T(8,128)(2,1)} custom-call(bf16[1024,3072]{1,0:T(8,128)(2,1)} %get-tuple-element.229.j_ref, bf16[1024,1024]{1,0:T(8,128)(2,1)} %get-tuple-element.326.gm_ref, f32[4,16,256]{2,1,0:T(8,128)} %get-tuple-element.321.log_ref, s32[1024,1]{1,0:T(8,128)} %copy.66.sc_ref, s32[4,1,256]{2,1,0:T(1,128)} %bitcast.45), custom_call_target="tpu_custom_call" | custom-call | flops 5368709120 | bytes 7340032 | tf_op jit(solution)/shard_map/pallas_call | solution.py:568
  306.2 10.6 %shard_map.396 = (bf16[16,128,512]{2,1,0:T(8,128)(2,1)}, bf16[16,128,512]{2,1,0:T(8,128)(2,1)}) custom-call(f32[1,1]{1,0:T(1,128)} %bitcast.f_ref, bf16[1024,1024]{1,0:T(8,128)(2,1)} %get-tuple-element.327.t_ref, bf16[512,3072]{1,0:T(8,128)(2,1)} %shard_map.394.refs_0_, bf16[512,3072]{1,0:T(8,128)(2,1)} %shard_map.395.refs_1_), custom_call_target="tpu_custom_call" | custom-call | flops 4294967296 | bytes 10485760 | tf_op jit(solution)/shard_map/pallas_call | solution.py:645
  318.4 7.2 %shard_map.397 = (bf16[16,128,512]{2,1,0:T(8,128)(2,1)}, bf16[16,128,512]{2,1,0:T(8,128)(2,1)}) custom-call(f32[1,1]{1,0:T(1,128)} %bitcast.f_ref, bf16[1024,1024]{1,0:T(8,128)(2,1)} %get-tuple-element.327.t_ref, bf16[512,3072]{1,0:T(8,128)(2,1)} %shard_map.394.refs_0_, ...), custom_call_target="tpu_custom_call", output_to_operand_aliasing={{0}: (4, {}), {1}: (5, {})} | custom-call | flops 2147483648 | bytes 6291456 | tf_op jit(solution)/shard_map/pallas_call | solution.py:645
  325.7 2.5 add_convert_fusion.13
  329.2 4.1 add_convert_fusion
  333.3 5.5 %all-to-all-start.4 = ((bf16[4,128,1024]{2,1,0:T(8,128)(2,1)}), bf16[4,128,1024]{2,1,0:T(8,128)(2,1)}, u32[]{:S(2)}, u32[]{:S(2)}) async-start(bf16[4,128,1024]{2,1,0:T(8,128)(2,1)} %add_convert_fusion), calls=%async_computation.4 | async-start | bytes 2097152 | tf_op jit(solution)/shard_map/all_to_all | solution.py:81
  340.1 2.4 add_convert_fusion.14
  342.4 2.0 add_convert_fusion.12
  346.3 14.7 %shard_map.398 = (f32[1024,1024]{1,0:T(8,128)}, f32[2,1024]{1,0:T(2,128)}) custom-call(bf16[512,3072]{1,0:T(8,128)(2,1)} %shard_map.394.refs_0_, bf16[512,3072]{1,0:T(8,128)(2,1)} %shard_map.395.refs_1_, f32[1024,1024]{1,0:T(8,128)} %get-tuple-element.343.refs_2_, bf16[1024,1024]{1,0:T(8,128)(2,1)} %refs_3_.1, f32[4,1024]{1,0:T(4,128)} %refs_4_.1, ...), custom_call_target="tpu_custom_call" | custom-call | flops 6442450944 | bytes 23068672 | tf_op jit(solution)/shard_map/pallas_call | solution.py:615
  361.1 2.9 add_convert_fusion.9
  369.1 2.8 collective-permute-done.61
  371.9 1.5 collective-permute-done.59
  373.4 5.6 %collective-permute-done.58 = bf16[4,128,512]{2,1,0:T(8,128)(2,1)} collective-permute-done((bf16[4,128,512]{2,1,0:T(8,128)(2,1)}, bf16[4,128,512]{2,1,0:T(8,128)(2,1)}, u32[]{:S(2)}, u32[]{:S(2)}) %collective-permute-start.58) | collective-permute-done | bytes 524320 | tf_op jit(solution)/shard_map/ppermute | solution.py:77
  379.1 2.6 add_convert_fusion.11
  381.6 5.1 %all-to-all-start.2 = ((bf16[4,128,512]{2,1,0:T(8,128)(2,1)}), bf16[4,128,512]{2,1,0:T(8,128)(2,1)}, u32[]{:S(2)}, u32[]{:S(2)}) async-start(bf16[4,128,512]{2,1,0:T(8,128)(2,1)} %add_convert_fusion.11), calls=%async_computation.2 | async-start | bytes 1048576 | tf_op jit(solution)/shard_map/all_to_all | solution.py:81
  391.1 1.9 collective-permute-done.63
  394.3 2.0 collective-permute-start.64
  396.3 2.4 add_convert_fusion.8
  398.7 3.3 all-to-all-done.2
  402.0 3.5 all-to-all-start.3
  405.5 2.8 fusion.9
  409.1 2.9 collective-permute-start.65
  412.0 1.5 fusion.7
  413.6 6.9 %collective-permute-done.65 = f32[4,1024]{1,0:T(4,128)S(1)} collective-permute-done((f32[4,1024]{1,0:T(4,128)S(1)}, f32[4,1024]{1,0:T(4,128)S(1)}, u32[]{:S(2)}, u32[]{:S(2)}) %collective-permute-start.65) | collective-permute-done | bytes 16416 | tf_op jit(solution)/shard_map/ppermute | solution.py:87
  (272 shorter events, 59.1 us)
Async XLA Ops:
  1.8 12.1 %collective-permute-start.1 = (bf16[128,512]{1,0:T(8,128)(2,1)S(1)}, bf16[128,512]{1,0:T(8,128)(2,1)S(1)}, u32[]{:S(2)}, u32[]{:S(2)}) collective-permute-start(bf16[128,512]{1,0:T(8,128)(2,1)S(1)} %get-tuple-element.423), channel_id=1, source_target_pairs={{16,0},{20,4},{24,8},{28,12},{0,16},{4,20},{8,24},{12,28},{17,1},{... | collective-permute-start | bytes 393224 | tf_op jit(solution)/shard_map/ppermute | solution.py:98
  5.9 8.0 %collective-permute-start = (bf16[128,512]{1,0:T(8,128)(2,1)S(1)}, bf16[128,512]{1,0:T(8,128)(2,1)S(1)}, u32[]{:S(2)}, u32[]{:S(2)}) collective-permute-start(bf16[128,512]{1,0:T(8,128)(2,1)S(1)} %get-tuple-element.423), channel_id=1, source_target_pairs={{8,0},{12,4},{16,8},{20,12},{24,16},{28,20},{0,24},{4,28},{9,1},{1... | collective-permute-start | bytes 393224 | tf_op jit(solution)/shard_map/ppermute | solution.py:98
  7.3 9.0 %collective-permute-start.2 = (bf16[128,512]{1,0:T(8,128)(2,1)S(1)}, bf16[128,512]{1,0:T(8,128)(2,1)S(1)}, u32[]{:S(2)}, u32[]{:S(2)}) collective-permute-start(bf16[128,512]{1,0:T(8,128)(2,1)S(1)} %get-tuple-element.423), channel_id=1, source_target_pairs={{24,0},{28,4},{0,8},{4,12},{8,16},{12,20},{16,24},{20,28},{25,1},{... | collective-permute-start | bytes 393224 | tf_op jit(solution)/shard_map/ppermute | solution.py:98
  18.3 11.0 %collective-permute-start.8 = (bf16[128,512]{1,0:T(8,128)(2,1)S(1)}, bf16[128,512]{1,0:T(8,128)(2,1)S(1)}, u32[]{:S(2)}, u32[]{:S(2)}) collective-permute-start(bf16[128,512]{1,0:T(8,128)(2,1)S(1)} %pad_maximum_fusion.12), channel_id=1, source_target_pairs={{24,0},{28,4},{0,8},{4,12},{8,16},{12,20},{16,24},{20,28},{25,1},{... | collective-permute-start | bytes 393224 | tf_op jit(solution)/shard_map/ppermute | solution.py:98
  20.7 10.7 %collective-permute-start.7 = (bf16[128,512]{1,0:T(8,128)(2,1)S(1)}, bf16[128,512]{1,0:T(8,128)(2,1)S(1)}, u32[]{:S(2)}, u32[]{:S(2)}) collective-permute-start(bf16[128,512]{1,0:T(8,128)(2,1)S(1)} %pad_maximum_fusion.12), channel_id=1, source_target_pairs={{16,0},{20,4},{24,8},{28,12},{0,16},{4,20},{8,24},{12,28},{17,1},{... | collective-permute-start | bytes 393224 | tf_op jit(solution)/shard_map/ppermute | solution.py:98
  22.6 8.8 %collective-permute-start.6 = (bf16[128,512]{1,0:T(8,128)(2,1)S(1)}, bf16[128,512]{1,0:T(8,128)(2,1)S(1)}, u32[]{:S(2)}, u32[]{:S(2)}) collective-permute-start(bf16[128,512]{1,0:T(8,128)(2,1)S(1)} %pad_maximum_fusion.12), channel_id=1, source_target_pairs={{8,0},{12,4},{16,8},{20,12},{24,16},{28,20},{0,24},{4,28},{9,1},{1... | collective-permute-start | bytes 393224 | tf_op jit(solution)/shard_map/ppermute | solution.py:98
  27.2 9.2 %collective-permute-start.4 = (bf16[4,128,512]{2,1,0:T(8,128)(2,1)S(1)}, bf16[4,128,512]{2,1,0:T(8,128)(2,1)S(1)}, u32[]{:S(2)}, u32[]{:S(2)}) collective-permute-start(bf16[4,128,512]{2,1,0:T(8,128)(2,1)S(1)} %pad_maximum_fusion.5.refs_0_), channel_id=1, source_target_pairs={{0,4},{1,3},{2,6},{3,1},{4,0},{5,7},{6,2},{7,5},{8,12},{9,11},{10,... | collective-permute-start | bytes 1572872 | tf_op jit(solution)/shard_map/ppermute | solution.py:77
  28.8 13.3 %collective-permute-start.5 = (bf16[4,128,512]{2,1,0:T(8,128)(2,1)S(1)}, bf16[4,128,512]{2,1,0:T(8,128)(2,1)S(1)}, u32[]{:S(2)}, u32[]{:S(2)}) collective-permute-start(bf16[4,128,512]{2,1,0:T(8,128)(2,1)S(1)} %collective-permute-done.3.refs_1_), channel_id=1, source_target_pairs={{0,4},{1,3},{2,6},{3,1},{4,0},{5,7},{6,2},{7,5},{8,12},{9,11},{10,... | collective-permute-start | bytes 1572872 | tf_op jit(solution)/shard_map/ppermute | solution.py:77
  31.5 10.6 %collective-permute-start.9 = (bf16[4,128,512]{2,1,0:T(8,128)(2,1)S(1)}, bf16[4,128,512]{2,1,0:T(8,128)(2,1)S(1)}, u32[]{:S(2)}, u32[]{:S(2)}) collective-permute-start(bf16[4,128,512]{2,1,0:T(8,128)(2,1)S(1)} %pad_maximum_fusion.6.refs_8_.refs_0_), channel_id=1, source_target_pairs={{0,1},{1,0},{2,3},{3,2},{4,5},{5,4},{6,7},{7,6},{8,9},{9,8},{10,11... | collective-permute-start | bytes 1572872 | tf_op jit(solution)/shard_map/ppermute | solution.py:68
  42.1 11.2 %collective-permute-start.15 = (bf16[128,1024]{1,0:T(8,128)(2,1)S(1)}, bf16[128,1024]{1,0:T(8,128)(2,1)S(1)}, u32[]{:S(2)}, u32[]{:S(2)}) collective-permute-start(bf16[128,1024]{1,0:T(8,128)(2,1)S(1)} %pad_maximum_fusion.10), channel_id=1, source_target_pairs={{24,0},{28,4},{0,8},{4,12},{8,16},{12,20},{16,24},{20,28},{25,1},{... | collective-permute-start | bytes 786440 | tf_op jit(solution)/shard_map/ppermute | solution.py:98
  42.1 21.6 %collective-permute-start.10 = (bf16[4,128,512]{2,1,0:T(8,128)(2,1)S(1)}, bf16[4,128,512]{2,1,0:T(8,128)(2,1)S(1)}, u32[]{:S(2)}, u32[]{:S(2)}) collective-permute-start(bf16[4,128,512]{2,1,0:T(8,128)(2,1)S(1)} %pad_maximum_fusion.6.refs_8_.refs_0_), channel_id=1, source_target_pairs={{0,4},{1,3},{2,6},{3,1},{4,0},{5,7},{6,2},{7,5},{8,12},{9,11},{10,... | collective-permute-start | bytes 1572872 | tf_op jit(solution)/shard_map/ppermute | solution.py:77
  43.7 20.1 %collective-permute-start.11 = (bf16[4,128,512]{2,1,0:T(8,128)(2,1)S(1)}, bf16[4,128,512]{2,1,0:T(8,128)(2,1)S(1)}, u32[]{:S(2)}, u32[]{:S(2)}) collective-permute-start(bf16[4,128,512]{2,1,0:T(8,128)(2,1)S(1)} %collective-permute-done.9.refs_9_.refs_1_), channel_id=1, source_target_pairs={{0,4},{1,3},{2,6},{3,1},{4,0},{5,7},{6,2},{7,5},{8,12},{9,11},{10,... | collective-permute-start | bytes 1572872 | tf_op jit(solution)/shard_map/ppermute | solution.py:77
  44.2 19.6 %collective-permute-start.12 = (bf16[4,128,512]{2,1,0:T(8,128)(2,1)S(1)}, bf16[4,128,512]{2,1,0:T(8,128)(2,1)S(1)}, u32[]{:S(2)}, u32[]{:S(2)}) collective-permute-start(bf16[4,128,512]{2,1,0:T(8,128)(2,1)S(1)} %collective-permute-done.4.refs_2_), channel_id=1, source_target_pairs={{0,2},{1,5},{2,0},{3,7},{4,6},{5,1},{6,4},{7,3},{8,10},{9,13},{10,... | collective-permute-start | bytes 1572872 | tf_op jit(solution)/shard_map/ppermute | solution.py:77
  45.8 16.2 %collective-permute-start.14 = (bf16[128,1024]{1,0:T(8,128)(2,1)S(1)}, bf16[128,1024]{1,0:T(8,128)(2,1)S(1)}, u32[]{:S(2)}, u32[]{:S(2)}) collective-permute-start(bf16[128,1024]{1,0:T(8,128)(2,1)S(1)} %pad_maximum_fusion.10), channel_id=1, source_target_pairs={{16,0},{20,4},{24,8},{28,12},{0,16},{4,20},{8,24},{12,28},{17,1},{... | collective-permute-start | bytes 786440 | tf_op jit(solution)/shard_map/ppermute | solution.py:98
  53.3 10.4 %collective-permute-start.13 = (bf16[128,1024]{1,0:T(8,128)(2,1)S(1)}, bf16[128,1024]{1,0:T(8,128)(2,1)S(1)}, u32[]{:S(2)}, u32[]{:S(2)}) collective-permute-start(bf16[128,1024]{1,0:T(8,128)(2,1)S(1)} %pad_maximum_fusion.10), channel_id=1, source_target_pairs={{8,0},{12,4},{16,8},{20,12},{24,16},{28,20},{0,24},{4,28},{9,1},{1... | collective-permute-start | bytes 786440 | tf_op jit(solution)/shard_map/ppermute | solution.py:98
  63.8 9.3 %collective-permute-start.20 = (bf16[4,128,1024]{2,1,0:T(8,128)(2,1)S(1)}, bf16[4,128,1024]{2,1,0:T(8,128)(2,1)S(1)}, u32[]{:S(2)}, u32[]{:S(2)}) collective-permute-start(bf16[4,128,1024]{2,1,0:T(8,128)(2,1)S(1)} %pad_maximum_fusion), channel_id=1, source_target_pairs={{0,1},{1,0},{2,3},{3,2},{4,5},{5,4},{6,7},{7,6},{8,9},{9,8},{10,11... | collective-permute-start | bytes 3145736 | tf_op jit(solution)/shard_map/ppermute | solution.py:68
  63.9 9.2 %collective-permute-start.19 = (bf16[4,128,512]{2,1,0:T(8,128)(2,1)S(1)}, bf16[4,128,512]{2,1,0:T(8,128)(2,1)S(1)}, u32[]{:S(2)}, u32[]{:S(2)}) collective-permute-start(bf16[4,128,512]{2,1,0:T(8,128)(2,1)S(1)} %collective-permute-done.10.refs_10_.refs_2_), channel_id=1, source_target_pairs={{0,2},{1,5},{2,0},{3,7},{4,6},{5,1},{6,4},{7,3},{8,10},{9,13},{10,... | collective-permute-start | bytes 1572872 | tf_op jit(solution)/shard_map/ppermute | solution.py:77
  65.5 8.2 %collective-permute-start.17 = (bf16[4,128,512]{2,1,0:T(8,128)(2,1)S(1)}, bf16[4,128,512]{2,1,0:T(8,128)(2,1)S(1)}, u32[]{:S(2)}, u32[]{:S(2)}) collective-permute-start(bf16[4,128,512]{2,1,0:T(8,128)(2,1)S(1)} %collective-permute-done.5.refs_3_), channel_id=1, source_target_pairs={{0,1},{1,0},{2,3},{3,2},{4,5},{5,4},{6,7},{7,6},{8,9},{9,8},{10,11... | collective-permute-start | bytes 1572872 | tf_op jit(solution)/shard_map/ppermute | solution.py:68
  65.7 9.2 %collective-permute-start.16 = (bf16[4,128,512]{2,1,0:T(8,128)(2,1)S(1)}, bf16[4,128,512]{2,1,0:T(8,128)(2,1)S(1)}, u32[]{:S(2)}, u32[]{:S(2)}) collective-permute-start(bf16[4,128,512]{2,1,0:T(8,128)(2,1)S(1)} %collective-permute-done.4.refs_2_), channel_id=1, source_target_pairs={{0,1},{1,0},{2,3},{3,2},{4,5},{5,4},{6,7},{7,6},{8,9},{9,8},{10,11... | collective-permute-start | bytes 1572872 | tf_op jit(solution)/shard_map/ppermute | solution.py:68
  66.1 9.7 %collective-permute-start.21 = (bf16[4,128,512]{2,1,0:T(8,128)(2,1)S(1)}, bf16[4,128,512]{2,1,0:T(8,128)(2,1)S(1)}, u32[]{:S(2)}, u32[]{:S(2)}) collective-permute-start(bf16[4,128,512]{2,1,0:T(8,128)(2,1)S(1)} %collective-permute-done.10.refs_10_.refs_2_), channel_id=1, source_target_pairs={{0,1},{1,0},{2,3},{3,2},{4,5},{5,4},{6,7},{7,6},{8,9},{9,8},{10,11... | collective-permute-start | bytes 1572872 | tf_op jit(solution)/shard_map/ppermute | solution.py:68
  73.2 2.7 collective-permute-start.22
  78.0 23.1 %collective-permute-start.24 = (bf16[8,128,512]{2,1,0:T(8,128)(2,1)}, bf16[8,128,512]{2,1,0:T(8,128)(2,1)}, u32[]{:S(2)}, u32[]{:S(2)}) collective-permute-start(bf16[8,128,512]{2,1,0:T(8,128)(2,1)} %pad_maximum_fusion.1), channel_id=1, source_target_pairs={{0,4},{1,3},{2,6},{3,1},{4,0},{5,7},{6,2},{7,5},{8,12},{9,11},{10,... | collective-permute-start | bytes 3145736 | tf_op jit(solution)/shard_map/ppermute | solution.py:77
  80.6 43.4 %all-to-all-start = ((bf16[4,128,1024]{2,1,0:T(8,128)(2,1)}), bf16[4,128,1024]{2,1,0:T(8,128)(2,1)S(1)}, u32[]{:S(2)}, u32[]{:S(2)}) async-start(bf16[4,128,1024]{2,1,0:T(8,128)(2,1)} %broadcast_in_dim.12), calls=%async_computation | async-start | bytes 2097152 | tf_op jit(solution)/shard_map/all_to_all | solution.py:81
  101.2 22.9 %collective-permute-start.26 = (bf16[8,128,512]{2,1,0:T(8,128)(2,1)S(1)}, bf16[8,128,512]{2,1,0:T(8,128)(2,1)}, u32[]{:S(2)}, u32[]{:S(2)}) collective-permute-start(bf16[8,128,512]{2,1,0:T(8,128)(2,1)S(1)} %pad_maximum_fusion.2), channel_id=1, source_target_pairs={{0,4},{1,3},{2,6},{3,1},{4,0},{5,7},{6,2},{7,5},{8,12},{9,11},{10,... | collective-permute-start | bytes 3145736 | tf_op jit(solution)/shard_map/ppermute | solution.py:77
  103.9 20.2 %collective-permute-start.25 = (bf16[4,128,512]{2,1,0:T(8,128)(2,1)S(1)}, bf16[4,128,512]{2,1,0:T(8,128)(2,1)S(1)}, u32[]{:S(2)}, u32[]{:S(2)}) collective-permute-start(bf16[4,128,512]{2,1,0:T(8,128)(2,1)S(1)} %slice.212), channel_id=1, source_target_pairs={{0,2},{1,5},{2,0},{3,7},{4,6},{5,1},{6,4},{7,3},{8,10},{9,13},{10,... | collective-permute-start | bytes 1572872 | tf_op jit(solution)/shard_map/ppermute | solution.py:77
  124.8 4.1 collective-permute-start.29
  124.9 4.5 %collective-permute-start.27 = (bf16[8,128,512]{2,1,0:T(8,128)(2,1)}, bf16[8,128,512]{2,1,0:T(8,128)(2,1)}, u32[]{:S(2)}, u32[]{:S(2)}) collective-permute-start(bf16[8,128,512]{2,1,0:T(8,128)(2,1)} %collective-permute-done.24.refs_2_), channel_id=1, source_target_pairs={{0,1},{1,0},{2,3},{3,2},{4,5},{5,4},{6,7},{7,6},{8,9},{9,8},{10,11... | collective-permute-start | bytes 3145736 | tf_op jit(solution)/shard_map/ppermute | solution.py:68
  127.3 2.7 collective-permute-start.28
  131.2 22.6 %collective-permute-start.32 = (bf16[8,128,512]{2,1,0:T(8,128)(2,1)}, bf16[8,128,512]{2,1,0:T(8,128)(2,1)}, u32[]{:S(2)}, u32[]{:S(2)}) collective-permute-start(bf16[8,128,512]{2,1,0:T(8,128)(2,1)} %collective-permute-done.26.refs_2_), channel_id=1, source_target_pairs={{0,1},{1,0},{2,3},{3,2},{4,5},{5,4},{6,7},{7,6},{8,9},{9,8},{10,11... | collective-permute-start | bytes 3145736 | tf_op jit(solution)/shard_map/ppermute | solution.py:68
  131.4 22.2 %collective-permute-start.30 = (bf16[4,128,512]{2,1,0:T(8,128)(2,1)S(1)}, bf16[4,128,512]{2,1,0:T(8,128)(2,1)}, u32[]{:S(2)}, u32[]{:S(2)}) collective-permute-start(bf16[4,128,512]{2,1,0:T(8,128)(2,1)S(1)} %slice.215), channel_id=1, source_target_pairs={{0,2},{1,5},{2,0},{3,7},{4,6},{5,1},{6,4},{7,3},{8,10},{9,13},{10,... | collective-permute-start | bytes 1572872 | tf_op jit(solution)/shard_map/ppermute | solution.py:77
  132.1 21.6 %collective-permute-start.31 = (bf16[8,128,512]{2,1,0:T(8,128)(2,1)S(1)}, bf16[8,128,512]{2,1,0:T(8,128)(2,1)}, u32[]{:S(2)}, u32[]{:S(2)}) collective-permute-start(bf16[8,128,512]{2,1,0:T(8,128)(2,1)S(1)} %pad_maximum_fusion.3), channel_id=1, source_target_pairs={{0,4},{1,3},{2,6},{3,1},{4,0},{5,7},{6,2},{7,5},{8,12},{9,11},{10,... | collective-permute-start | bytes 3145736 | tf_op jit(solution)/shard_map/ppermute | solution.py:77
  157.8 22.5 %collective-permute-start.36 = (bf16[8,128,512]{2,1,0:T(8,128)(2,1)}, bf16[8,128,512]{2,1,0:T(8,128)(2,1)}, u32[]{:S(2)}, u32[]{:S(2)}) collective-permute-start(bf16[8,128,512]{2,1,0:T(8,128)(2,1)} %collective-permute-done.31.refs_2_), channel_id=1, source_target_pairs={{0,1},{1,0},{2,3},{3,2},{4,5},{5,4},{6,7},{7,6},{8,9},{9,8},{10,11... | collective-permute-start | bytes 3145736 | tf_op jit(solution)/shard_map/ppermute | solution.py:68
  158.0 22.2 %collective-permute-start.34 = (bf16[4,128,512]{2,1,0:T(8,128)(2,1)S(1)}, bf16[4,128,512]{2,1,0:T(8,128)(2,1)}, u32[]{:S(2)}, u32[]{:S(2)}) collective-permute-start(bf16[4,128,512]{2,1,0:T(8,128)(2,1)S(1)} %slice.218), channel_id=1, source_target_pairs={{0,2},{1,5},{2,0},{3,7},{4,6},{5,1},{6,4},{7,3},{8,10},{9,13},{10,... | collective-permute-start | bytes 1572872 | tf_op jit(solution)/shard_map/ppermute | solution.py:77
  159.6 20.6 %collective-permute-start.35 = (bf16[8,128,512]{2,1,0:T(8,128)(2,1)S(1)}, bf16[8,128,512]{2,1,0:T(8,128)(2,1)S(1)}, u32[]{:S(2)}, u32[]{:S(2)}) collective-permute-start(bf16[8,128,512]{2,1,0:T(8,128)(2,1)S(1)} %pad_maximum_fusion.4), channel_id=1, source_target_pairs={{0,4},{1,3},{2,6},{3,1},{4,0},{5,7},{6,2},{7,5},{8,12},{9,11},{10,... | collective-permute-start | bytes 3145736 | tf_op jit(solution)/shard_map/ppermute | solution.py:77
  182.4 21.3 %collective-permute-start.39 = (bf16[16,128,1024]{2,1,0:T(8,128)(2,1)}, bf16[16,128,1024]{2,1,0:T(8,128)(2,1)}, u32[]{:S(2)}, u32[]{:S(2)}) collective-permute-start(bf16[16,128,1024]{2,1,0:T(8,128)(2,1)} %get-tuple-element.288), channel_id=1, source_target_pairs={{0,1},{1,0},{2,3},{3,2},{4,5},{5,4},{6,7},{7,6},{8,9},{9,8},{10,11... | collective-permute-start | bytes 12582920 | tf_op jit(solution)/shard_map/ppermute | solution.py:68
  182.6 22.0 %collective-permute-start.40 = (bf16[8,128,512]{2,1,0:T(8,128)(2,1)S(1)}, bf16[8,128,512]{2,1,0:T(8,128)(2,1)S(1)}, u32[]{:S(2)}, u32[]{:S(2)}) collective-permute-start(bf16[8,128,512]{2,1,0:T(8,128)(2,1)S(1)} %collective-permute-done.35.refs_2_), channel_id=1, source_target_pairs={{0,1},{1,0},{2,3},{3,2},{4,5},{5,4},{6,7},{7,6},{8,9},{9,8},{10,11... | collective-permute-start | bytes 3145736 | tf_op jit(solution)/shard_map/ppermute | solution.py:68
  183.0 20.6 %collective-permute-start.38 = (bf16[4,128,512]{2,1,0:T(8,128)(2,1)S(1)}, bf16[4,128,512]{2,1,0:T(8,128)(2,1)S(1)}, u32[]{:S(2)}, u32[]{:S(2)}) collective-permute-start(bf16[4,128,512]{2,1,0:T(8,128)(2,1)S(1)} %slice.219), channel_id=1, source_target_pairs={{0,2},{1,5},{2,0},{3,7},{4,6},{5,1},{6,4},{7,3},{8,10},{9,13},{10,... | collective-permute-start | bytes 1572872 | tf_op jit(solution)/shard_map/ppermute | solution.py:77
  208.2 21.4 %collective-permute-start.42 = (bf16[4,128,1024]{2,1,0:T(8,128)(2,1)S(1)}, bf16[4,128,1024]{2,1,0:T(8,128)(2,1)S(1)}, u32[]{:S(2)}, u32[]{:S(2)}) collective-permute-start(bf16[4,128,1024]{2,1,0:T(8,128)(2,1)S(1)} %add_convert_fusion.7), channel_id=1, source_target_pairs={{0,2},{1,5},{2,0},{3,7},{4,6},{5,1},{6,4},{7,3},{8,10},{9,13},{10,... | collective-permute-start | bytes 3145736 | tf_op jit(solution)/shard_map/ppermute | solution.py:77
  229.5 29.6 %collective-permute-start.45 = (bf16[16,128,1024]{2,1,0:T(8,128)(2,1)}, bf16[16,128,1024]{2,1,0:T(8,128)(2,1)}, u32[]{:S(2)}, u32[]{:S(2)}) collective-permute-start(bf16[16,128,1024]{2,1,0:T(8,128)(2,1)} %get-tuple-element.315), channel_id=1, source_target_pairs={{0,1},{1,0},{2,3},{3,2},{4,5},{5,4},{6,7},{7,6},{8,9},{9,8},{10,11... | collective-permute-start | bytes 12582920 | tf_op jit(solution)/shard_map/ppermute | solution.py:68
  233.0 21.8 %collective-permute-start.44 = (bf16[4,128,1024]{2,1,0:T(8,128)(2,1)S(1)}, bf16[4,128,1024]{2,1,0:T(8,128)(2,1)}, u32[]{:S(2)}, u32[]{:S(2)}) collective-permute-start(bf16[4,128,1024]{2,1,0:T(8,128)(2,1)S(1)} %get-tuple-element.395), channel_id=1, source_target_pairs={{0,4},{1,3},{2,6},{3,1},{4,0},{5,7},{6,2},{7,5},{8,12},{9,11},{10,... | collective-permute-start | bytes 3145736 | tf_op jit(solution)/shard_map/ppermute | solution.py:77
  234.6 24.5 %collective-permute-start.43 = (bf16[4,128,1024]{2,1,0:T(8,128)(2,1)S(1)}, bf16[4,128,1024]{2,1,0:T(8,128)(2,1)S(1)}, u32[]{:S(2)}, u32[]{:S(2)}) collective-permute-start(bf16[4,128,1024]{2,1,0:T(8,128)(2,1)S(1)} %get-tuple-element.396), channel_id=1, source_target_pairs={{0,4},{1,3},{2,6},{3,1},{4,0},{5,7},{6,2},{7,5},{8,12},{9,11},{10,... | collective-permute-start | bytes 3145736 | tf_op jit(solution)/shard_map/ppermute | solution.py:77
  262.1 15.3 %collective-permute-start.46 = (bf16[4,128,1024]{2,1,0:T(8,128)(2,1)}, bf16[4,128,1024]{2,1,0:T(8,128)(2,1)S(1)}, u32[]{:S(2)}, u32[]{:S(2)}) collective-permute-start(bf16[4,128,1024]{2,1,0:T(8,128)(2,1)} %add_convert_fusion.4), channel_id=1, source_target_pairs={{0,2},{1,5},{2,0},{3,7},{4,6},{5,1},{6,4},{7,3},{8,10},{9,13},{10,... | collective-permute-start | bytes 3145736 | tf_op jit(solution)/shard_map/ppermute | solution.py:77
  263.4 14.0 %collective-permute-start.47 = (bf16[4,128,1024]{2,1,0:T(8,128)(2,1)}, bf16[4,128,1024]{2,1,0:T(8,128)(2,1)S(1)}, u32[]{:S(2)}, u32[]{:S(2)}) collective-permute-start(bf16[4,128,1024]{2,1,0:T(8,128)(2,1)} %collective-permute-done.44), channel_id=1, source_target_pairs={{0,1},{1,0},{2,3},{3,2},{4,5},{5,4},{6,7},{7,6},{8,9},{9,8},{10,11... | collective-permute-start | bytes 3145736 | tf_op jit(solution)/shard_map/ppermute | solution.py:68
  280.9 36.0 %all-to-all-start.1 = ((bf16[4,128,1024]{2,1,0:T(8,128)(2,1)}), bf16[4,128,1024]{2,1,0:T(8,128)(2,1)S(1)}, u32[]{:S(2)}, u32[]{:S(2)}) async-start(bf16[4,128,1024]{2,1,0:T(8,128)(2,1)} %add_convert_fusion.1), calls=%async_computation.1 | async-start | bytes 2097152 | tf_op jit(solution)/shard_map/all_to_all | solution.py:81
  290.4 26.5 %collective-permute-start.49 = (bf16[4,128,1024]{2,1,0:T(8,128)(2,1)}, bf16[4,128,1024]{2,1,0:T(8,128)(2,1)S(1)}, u32[]{:S(2)}, u32[]{:S(2)}) collective-permute-start(bf16[4,128,1024]{2,1,0:T(8,128)(2,1)} %get-tuple-element.393), channel_id=1, source_target_pairs={{0,4},{1,3},{2,6},{3,1},{4,0},{5,7},{6,2},{7,5},{8,12},{9,11},{10,... | collective-permute-start | bytes 3145736 | tf_op jit(solution)/shard_map/ppermute | solution.py:77
  291.6 25.3 %collective-permute-start.48 = (bf16[4,128,1024]{2,1,0:T(8,128)(2,1)S(1)}, bf16[4,128,1024]{2,1,0:T(8,128)(2,1)}, u32[]{:S(2)}, u32[]{:S(2)}) collective-permute-start(bf16[4,128,1024]{2,1,0:T(8,128)(2,1)S(1)} %get-tuple-element.394), channel_id=1, source_target_pairs={{0,4},{1,3},{2,6},{3,1},{4,0},{5,7},{6,2},{7,5},{8,12},{9,11},{10,... | collective-permute-start | bytes 3145736 | tf_op jit(solution)/shard_map/ppermute | solution.py:77
  317.9 7.7 %collective-permute-start.50 = (bf16[16,128,512]{2,1,0:T(8,128)(2,1)}, bf16[16,128,512]{2,1,0:T(8,128)(2,1)}, u32[]{:S(2)}, u32[]{:S(2)}) collective-permute-start(bf16[16,128,512]{2,1,0:T(8,128)(2,1)} %get-tuple-element.335), channel_id=1, source_target_pairs={{0,1},{1,0},{2,3},{3,2},{4,5},{5,4},{6,7},{7,6},{8,9},{9,8},{10,11... | collective-permute-start | bytes 6291464 | tf_op jit(solution)/shard_map/ppermute | solution.py:68
  317.9 7.7 %collective-permute-start.51 = (bf16[4,128,1024]{2,1,0:T(8,128)(2,1)}, bf16[4,128,1024]{2,1,0:T(8,128)(2,1)}, u32[]{:S(2)}, u32[]{:S(2)}) collective-permute-start(bf16[4,128,1024]{2,1,0:T(8,128)(2,1)} %copy-done.44), channel_id=1, source_target_pairs={{0,1},{1,0},{2,3},{3,2},{4,5},{5,4},{6,7},{7,6},{8,9},{9,8},{10,11... | collective-permute-start | bytes 3145736 | tf_op jit(solution)/shard_map/ppermute | solution.py:68
  325.7 14.4 %collective-permute-start.53 = (bf16[16,128,512]{2,1,0:T(8,128)(2,1)}, bf16[16,128,512]{2,1,0:T(8,128)(2,1)}, u32[]{:S(2)}, u32[]{:S(2)}) collective-permute-start(bf16[16,128,512]{2,1,0:T(8,128)(2,1)} %get-tuple-element.349), channel_id=1, source_target_pairs={{0,1},{1,0},{2,3},{3,2},{4,5},{5,4},{6,7},{7,6},{8,9},{9,8},{10,11... | collective-permute-start | bytes 6291464 | tf_op jit(solution)/shard_map/ppermute | solution.py:68
  328.2 11.8 %collective-permute-start.52 = (bf16[4,128,512]{2,1,0:T(8,128)(2,1)}, bf16[4,128,512]{2,1,0:T(8,128)(2,1)}, u32[]{:S(2)}, u32[]{:S(2)}) collective-permute-start(bf16[4,128,512]{2,1,0:T(8,128)(2,1)} %get-tuple-element.400), channel_id=1, source_target_pairs={{0,2},{1,5},{2,0},{3,7},{4,6},{5,1},{6,4},{7,3},{8,10},{9,13},{10,... | collective-permute-start | bytes 1572872 | tf_op jit(solution)/shard_map/ppermute | solution.py:77
  333.3 48.3 %all-to-all-start.4 = ((bf16[4,128,1024]{2,1,0:T(8,128)(2,1)}), bf16[4,128,1024]{2,1,0:T(8,128)(2,1)}, u32[]{:S(2)}, u32[]{:S(2)}) async-start(bf16[4,128,1024]{2,1,0:T(8,128)(2,1)} %add_convert_fusion), calls=%async_computation.4 | async-start | bytes 2097152 | tf_op jit(solution)/shard_map/all_to_all | solution.py:81
  338.8 22.2 %collective-permute-start.55 = (bf16[4,128,512]{2,1,0:T(8,128)(2,1)}, bf16[4,128,512]{2,1,0:T(8,128)(2,1)}, u32[]{:S(2)}, u32[]{:S(2)}) collective-permute-start(bf16[4,128,512]{2,1,0:T(8,128)(2,1)} %get-tuple-element.399), channel_id=1, source_target_pairs={{0,4},{1,3},{2,6},{3,1},{4,0},{5,7},{6,2},{7,5},{8,12},{9,11},{10,... | collective-permute-start | bytes 1572872 | tf_op jit(solution)/shard_map/ppermute | solution.py:77
  344.4 16.6 %collective-permute-start.56 = (bf16[4,128,512]{2,1,0:T(8,128)(2,1)}, bf16[4,128,512]{2,1,0:T(8,128)(2,1)}, u32[]{:S(2)}, u32[]{:S(2)}) collective-permute-start(bf16[4,128,512]{2,1,0:T(8,128)(2,1)} %add_convert_fusion.12), channel_id=1, source_target_pairs={{0,2},{1,5},{2,0},{3,7},{4,6},{5,1},{6,4},{7,3},{8,10},{9,13},{10,... | collective-permute-start | bytes 1572872 | tf_op jit(solution)/shard_map/ppermute | solution.py:77
  345.4 15.7 %collective-permute-start.54 = (bf16[4,128,512]{2,1,0:T(8,128)(2,1)}, bf16[4,128,512]{2,1,0:T(8,128)(2,1)S(1)}, u32[]{:S(2)}, u32[]{:S(2)}) collective-permute-start(bf16[4,128,512]{2,1,0:T(8,128)(2,1)} %add_convert_fusion.14), channel_id=1, source_target_pairs={{0,4},{1,3},{2,6},{3,1},{4,0},{5,7},{6,2},{7,5},{8,12},{9,11},{10,... | collective-permute-start | bytes 1572872 | tf_op jit(solution)/shard_map/ppermute | solution.py:77
  363.9 9.5 %collective-permute-start.59 = (bf16[4,128,512]{2,1,0:T(8,128)(2,1)}, bf16[4,128,512]{2,1,0:T(8,128)(2,1)}, u32[]{:S(2)}, u32[]{:S(2)}) collective-permute-start(bf16[4,128,512]{2,1,0:T(8,128)(2,1)} %get-tuple-element.397), channel_id=1, source_target_pairs={{0,4},{1,3},{2,6},{3,1},{4,0},{5,7},{6,2},{7,5},{8,12},{9,11},{10,... | collective-permute-start | bytes 1572872 | tf_op jit(solution)/shard_map/ppermute | solution.py:77
  365.1 14.0 %collective-permute-start.58 = (bf16[4,128,512]{2,1,0:T(8,128)(2,1)}, bf16[4,128,512]{2,1,0:T(8,128)(2,1)}, u32[]{:S(2)}, u32[]{:S(2)}) collective-permute-start(bf16[4,128,512]{2,1,0:T(8,128)(2,1)} %get-tuple-element.398), channel_id=1, source_target_pairs={{0,4},{1,3},{2,6},{3,1},{4,0},{5,7},{6,2},{7,5},{8,12},{9,11},{10,... | collective-permute-start | bytes 1572872 | tf_op jit(solution)/shard_map/ppermute | solution.py:77
  366.0 13.1 %collective-permute-start.57 = (bf16[4,128,512]{2,1,0:T(8,128)(2,1)}, bf16[4,128,512]{2,1,0:T(8,128)(2,1)}, u32[]{:S(2)}, u32[]{:S(2)}) collective-permute-start(bf16[4,128,512]{2,1,0:T(8,128)(2,1)} %collective-permute-done.55), channel_id=1, source_target_pairs={{0,1},{1,0},{2,3},{3,2},{4,5},{5,4},{6,7},{7,6},{8,9},{9,8},{10,11... | collective-permute-start | bytes 1572872 | tf_op jit(solution)/shard_map/ppermute | solution.py:68
  367.9 4.0 collective-permute-start.61
  379.0 17.3 %collective-permute-start.62 = (bf16[4,128,512]{2,1,0:T(8,128)(2,1)}, bf16[4,128,512]{2,1,0:T(8,128)(2,1)}, u32[]{:S(2)}, u32[]{:S(2)}) collective-permute-start(bf16[4,128,512]{2,1,0:T(8,128)(2,1)} %collective-permute-done.59), channel_id=1, source_target_pairs={{0,1},{1,0},{2,3},{3,2},{4,5},{5,4},{6,7},{7,6},{8,9},{9,8},{10,11... | collective-permute-start | bytes 1572872 | tf_op jit(solution)/shard_map/ppermute | solution.py:68
  381.6 20.4 %all-to-all-start.2 = ((bf16[4,128,512]{2,1,0:T(8,128)(2,1)}), bf16[4,128,512]{2,1,0:T(8,128)(2,1)}, u32[]{:S(2)}, u32[]{:S(2)}) async-start(bf16[4,128,512]{2,1,0:T(8,128)(2,1)} %add_convert_fusion.11), calls=%async_computation.2 | async-start | bytes 1048576 | tf_op jit(solution)/shard_map/all_to_all | solution.py:81
  389.1 3.9 collective-permute-start.63
  394.3 14.1 %collective-permute-start.64 = (f32[4,1024]{1,0:T(4,128)}, f32[4,1024]{1,0:T(4,128)S(1)}, u32[]{:S(2)}, u32[]{:S(2)}) collective-permute-start(f32[4,1024]{1,0:T(4,128)} %add.224), channel_id=1, source_target_pairs={{0,8},{4,12},{8,0},{12,4},{16,24},{20,28},{24,16},{28,20},{1,9},{5... | collective-permute-start | bytes 49160 | tf_op jit(solution)/shard_map/ppermute | solution.py:87
  402.0 20.3 %all-to-all-start.3 = ((bf16[4,128,512]{2,1,0:T(8,128)(2,1)}), bf16[4,128,512]{2,1,0:T(8,128)(2,1)S(1)}, u32[]{:S(2)}, u32[]{:S(2)}) async-start(bf16[4,128,512]{2,1,0:T(8,128)(2,1)} %add_convert_fusion.8), calls=%async_computation.3 | async-start | bytes 1048576 | tf_op jit(solution)/shard_map/all_to_all | solution.py:81
  409.1 11.4 %collective-permute-start.65 = (f32[4,1024]{1,0:T(4,128)S(1)}, f32[4,1024]{1,0:T(4,128)S(1)}, u32[]{:S(2)}, u32[]{:S(2)}) collective-permute-start(f32[4,1024]{1,0:T(4,128)S(1)} %add.225), channel_id=1, source_target_pairs={{0,16},{4,20},{8,24},{12,28},{16,0},{20,4},{24,8},{28,12},{1,17},{... | collective-permute-start | bytes 49160 | tf_op jit(solution)/shard_map/ppermute | solution.py:87
  (64 other events, 685.4 us)
where the time goes:
time: 430 us; the launch traced here: 425 us
  Pallas kernels  193 us (45%)
  waiting for transfers between devices  83 us (19%)
  starting transfers between devices  79.6 us (19%)
  other arithmetic  50.8 us (12%)
  local copies, waits for them, and re-layouts  14.4 us (3%)
    pallas_call x4, Pallas kernels, feed_forward(): pl.pallas_call(kernel, out_shape=(shape_of((count, width), F32),) * 2 + (...  80.3 us
    convert_element_type x19, other arithmetic, thin(): return values.astype(BF16)  41.6 us
    ppermute x26, waiting for transfers between devices, cross(): return lax.ppermute(values, ('dp', 'shard'), pairs)  28.8 us
    ppermute x26, starting transfers between devices, cross(): return lax.ppermute(values, ('dp', 'shard'), pairs)  28.4 us
    pallas_call x2, Pallas kernels, attention_back(): pl.pallas_call(kernel, grid=(blocks,), out_shape=shape_of((count, 3 * wid...  27.8 us
    ppermute x9, waiting for transfers between devices, gather_z(): parts.append(lax.ppermute(piece, 'dp', shift))  27.8 us
    all_to_all x5, starting transfers between devices, z_exchange(): lax.all_to_all(values, 'dp', 0, 0, axis_index_groups=groups, tiled=True)  25 us
    pallas_call x3, Pallas kernels, weight_grad(): pl.pallas_call(kernel, out_shape=(region, region), in_specs=[SCALAR, HELD...  24.9 us
  transfers between devices with their start and end apart: 71, of which 27 were waited for; matrix products, arithmetic and copies ran while one was open for 11% of the time, Pallas kernels for 46%

commit v1 on v0

--- a/solution.py
+++ b/solution.py
@@ -630,28 +630,40 @@
     columns = lanes * grid.shard
     region = shape_of((4 * grid.depth, width // grid.dp, region_lanes), BF16)
 
-    def kernel(f_ref, t_ref, *refs):
-        near, far, grad, whole, sems, load_sems = refs[parts + len(regions) :]
-        pairs = []
-        for n in range(parts):
-            for s in range(grid.shard):
+    def kernel(f_ref, t_hbm, *refs):
+        near, far, turned_rows, grad, whole, sems, load_sems, row_sems = refs[parts + len(regions) :]
+        loads = []
+        for s in range(grid.shard):
+            if s == 1:
+                loads += start_copies([(t_hbm, turned_rows)], row_sems)
+            pairs = []
+            for n in range(parts):
                 source = refs[n].at[:, pl.ds(s * across + offset, lanes)]
-                rows = pl.ds(n * share, share)
-                pairs.append((source, grad.at[rows, pl.ds(s * lanes, lanes)]))
-        run_copies(pairs, load_sems)
-        whole[...] = thin(dot(t_ref[...], grad[...]) * f_ref[0, 0])
+                pairs.append((source, grad.at[pl.ds(n * share, share), pl.ds(s * lanes, lanes)]))
+            loads.append(start_copies(pairs, load_sems.at[pl.ds(s * parts, parts)]))
+        loads = [loads[0], [loads[1]], *loads[2:]]
+        for copy in loads[0] + loads[1] + loads[2]:
+            copy.wait()
+        half = columns // 2
+        whole[:, :half] = thin(dot(turned_rows[...], grad[:, :half]) * f_ref[0, 0])
+        for copies in loads[3:]:
+            for copy in copies:
+                copy.wait()
+        whole[:, half:] = thin(dot(turned_rows[...], grad[:, half:]) * f_ref[0, 0])
         run_copies(block_stores(grid, whole, lanes, near, far, region_lane), sems)
 
     return pl.pallas_call(
         kernel,
         out_shape=(region, region),
-        in_specs=[SCALAR, HELD] + [ANYWHERE] * (parts + len(regions)),
+        in_specs=[SCALAR] + [ANYWHERE] * (1 + parts + len(regions)),
         out_specs=(ANYWHERE,) * 2,
         scratch_shapes=[
+            pltpu.VMEM((width, count), BF16),
             pltpu.VMEM((count, columns), BF16),
             pltpu.VMEM((width, columns), BF16),
             pltpu.SemaphoreType.DMA((grid.dp * grid.shard,)),
             pltpu.SemaphoreType.DMA((parts * grid.shard,)),
+            pltpu.SemaphoreType.DMA((1,)),
         ],
         input_output_aliases={2 + parts + n: n for n in range(len(regions))},
         compiler_params=limits(60),
@@ -728,10 +740,11 @@
     q1_over = grid.gather_xy(q1)
     q0_far = grid.gather_far(q0_over)
     m01 = grid.gather_z(piece)
-    q1_over, q0_far, m01 = tie(q1_over, q0_far, m01)
+    q1_over, q0_far, m01, piece = tie(q1_over, q0_far, m01, large(2, 3))
     q0_pieces = grid.gather_end(q0, q0_over, q0_far)
     q1_far = grid.gather_far(q1_over)
     m01 = grid.both(m01)
+    m23 = grid.z_exchange(grid.copies(piece))
     q1_far, m01 = tie(q1_far, m01)
     q1_pieces = grid.gather_end(q1, q1_over, q1_far)
 
@@ -741,22 +754,21 @@
 
     m0, m1 = halves(m01)
 
-    q0_pieces, q1_pieces, m0, piece = tie(q0_pieces, q1_pieces, m0, large(2, 3))
+    q0_pieces, q1_pieces, m0 = tie(q0_pieces, q1_pieces, m0)
     first_turned, joined, qkv_weight = first_projection(
         grid, [q0_pieces, q1_pieces], cuts, tokens, norm_params
     )
     m0_over = grid.gather_xy_joined(m0)
-    m23 = grid.z_exchange(grid.copies(piece))
-
-    joined, m0_over, m1 = tie(joined, m0_over, m1)
+
+    joined, m0_over, m1, m23 = tie(joined, m0_over, m1, m23)
+    m2, m3 = halves(grid.both(m23))
     mixed_turned, logs, residual, second, second_turned = attention(
         grid, q1_pieces, cuts[1], joined, seg_column, seg_row, tokens, norm_params
     )
     m0_far = grid.gather_far_joined(m0_over)
     m1_over = grid.gather_xy_joined(m1)
-    second, m0_far, m1_over, m23 = tie(second, m0_far, m1_over, m23)
+    second, m0_far, m1_over, m2, m3 = tie(second, m0_far, m1_over, m2, m3)
     m0_pieces = grid.gather_end_joined(m0, m0_over, m0_far)
-    m2, m3 = halves(grid.both(m23))
 
     def chunk(weights, sums, regions, place, turned):
         out_sum, back_sum, near, far = feed_forward(
@@ -832,13 +844,13 @@
     input_grad, first_terms = first_norm_back(
         grad_joined, grad_residual, tokens, norm_params, qkv_weight
     )
-    first_terms, q0_over, q1_far = tie(first_terms, q0_over, q1_far)
+    first_terms, q0_over, q1_far, r1_sent = tie(first_terms, q0_over, q1_far, r1_sent)
     q0_passed = grid.scatter_home(q0_over)
     q1_over = grid.scatter_xy(q1[0], q1_other, q1_far)
     q0_sent = grid.scatter_z(q0[0], q0_other, q0_over, q0_passed)
     terms = jnp.concatenate([first_terms, second_terms]) * factor
     terms = grid.total(terms, "shard")
-    q1_over, terms = tie(q1_over, terms)
+    q1_over, q0_sent, terms = tie(q1_over, q0_sent, terms)
     q1_passed = grid.scatter_home(q1_over)
     q1_sent = grid.scatter_z(q1[0], q1_other, q1_over, q1_passed)
     norm_grad = grid.total(terms, "dp")

time: 430 us -> 419 us (0.974)
  waiting for transfers between devices: 83 us -> 73.5 us
    ppermute x26, waiting for transfers between devices: 28.8 us -> 19.8 us  [cross(): return lax.ppermute(values, ('dp', 'shard'), pairs)]
    all_to_all x5, waiting for transfers between devices: 3.28 us -> 9.83 us  [z_exchange(): lax.all_to_all(values, 'dp', 0, 0, axis_index_groups=groups, tiled=True)]
    ppermute x5, waiting for transfers between devices: 12.7 us -> 6.78 us  [total(): values = values + lax.ppermute(values, axis, pairs)]
  transfers between devices with their start and end apart: 71 -> 71, of which waited for: 27 -> 26; matrix products, arithmetic and copies ran while one was open for 11% -> 12% of each run, Pallas kernels for 46% -> 46%
where the time goes in v1:
time: 419 us; the launch traced here: 414 us
  Pallas kernels  191 us (46%)
  starting transfers between devices  78.7 us (19%)
  waiting for transfers between devices  73.5 us (18%)
  other arithmetic  50.9 us (12%)
  local copies, waits for them, and re-layouts  16.7 us (4%)
    pallas_call x4, Pallas kernels, feed_forward(): pl.pallas_call(kernel, out_shape=(shape_of((count, width), F32),) * 2 + (...  80.3 us
    convert_element_type x19, other arithmetic, thin(): return values.astype(BF16)  42.1 us
    ppermute x26, starting transfers between devices, cross(): return lax.ppermute(values, ('dp', 'shard'), pairs)  29.2 us
    pallas_call x2, Pallas kernels, attention_back(): pl.pallas_call(kernel, grid=(blocks,), out_shape=shape_of((count, 3 * wid...  27.8 us
    ppermute x9, waiting for transfers between devices, gather_z(): parts.append(lax.ppermute(piece, 'dp', shift))  27.7 us
    all_to_all x5, starting transfers between devices, z_exchange(): lax.all_to_all(values, 'dp', 0, 0, axis_index_groups=groups, tiled=True)  22.4 us
    pallas_call x3, Pallas kernels, weight_grad(): pl.pallas_call(kernel, out_shape=(region, region), in_specs=[SCALAR] + [A...  22.3 us
    ppermute x26, waiting for transfers between devices, cross(): return lax.ppermute(values, ('dp', 'shard'), pairs)  19.8 us
  transfers between devices with their start and end apart: 71, of which 26 were waited for; matrix products, arithmetic and copies ran while one was open for 12% of the time, Pallas kernels for 46%

profile of v1, /device:TPU:0, one launch (start us, length us, event | category | flops | bytes accessed | tf_op | source)
XLA Modules:
  0.0 414.0 jit_solution(5508337097312447615)
XLA Ops:
  1.8 4.1 collective-permute-start.1
  8.0 5.9 %collective-permute-done.1 = bf16[128,512]{1,0:T(8,128)(2,1)S(1)} collective-permute-done((bf16[128,512]{1,0:T(8,128)(2,1)S(1)}, bf16[128,512]{1,0:T(8,128)(2,1)S(1)}, u32[]{:S(2)}, u32[]{:S(2)}) %collective-permute-start.1) | collective-permute-done | bytes 131104 | tf_op jit(solution)/shard_map/ppermute | solution.py:98
  13.9 2.4 collective-permute-done.2
  16.8 1.6 collective-permute-done.3.refs_1_
  18.3 2.4 collective-permute-start.8
  20.7 1.9 collective-permute-start.7
  22.6 2.9 collective-permute-start.6
  25.5 1.7 slice_reduce_fusion.1
  27.2 1.6 collective-permute-start.4
  29.3 2.1 collective-permute-done.7
  31.6 4.9 %collective-permute-done.4.refs_2_ = bf16[4,128,512]{2,1,0:T(8,128)(2,1)} collective-permute-done((bf16[4,128,512]{2,1,0:T(8,128)(2,1)S(1)}, bf16[4,128,512]{2,1,0:T(8,128)(2,1)}, u32[]{:S(2)}, u32[]{:S(2)}) %collective-permute-start.4) | collective-permute-done | bytes 524320 | tf_op jit(solution)/shard_map/ppermute | solution.py:77
  36.6 5.6 %collective-permute-done.5.refs_3_ = bf16[4,128,512]{2,1,0:T(8,128)(2,1)} collective-permute-done((bf16[4,128,512]{2,1,0:T(8,128)(2,1)S(1)}, bf16[4,128,512]{2,1,0:T(8,128)(2,1)}, u32[]{:S(2)}, u32[]{:S(2)}) %collective-permute-start.5) | collective-permute-done | bytes 524320 | tf_op jit(solution)/shard_map/ppermute | solution.py:77
  42.2 1.6 collective-permute-start.10
  44.3 1.5 collective-permute-start.12
  46.3 7.0 %collective-permute-done.15 = bf16[128,1024]{1,0:T(8,128)(2,1)S(1)} collective-permute-done((bf16[128,1024]{1,0:T(8,128)(2,1)S(1)}, bf16[128,1024]{1,0:T(8,128)(2,1)S(1)}, u32[]{:S(2)}, u32[]{:S(2)}) %collective-permute-start.15) | collective-permute-done | bytes 262176 | tf_op jit(solution)/shard_map/ppermute | solution.py:98
  53.4 8.6 %collective-permute-done.14 = bf16[128,1024]{1,0:T(8,128)(2,1)S(1)} collective-permute-done((bf16[128,1024]{1,0:T(8,128)(2,1)S(1)}, bf16[128,1024]{1,0:T(8,128)(2,1)S(1)}, u32[]{:S(2)}, u32[]{:S(2)}) %collective-permute-start.14) | collective-permute-done | bytes 262176 | tf_op jit(solution)/shard_map/ppermute | solution.py:98
  62.0 1.7 collective-permute-done.13
  65.5 1.5 collective-permute-start.19
  68.6 5.9 %all-to-all-start = ((bf16[4,128,1024]{2,1,0:T(8,128)(2,1)}), bf16[4,128,1024]{2,1,0:T(8,128)(2,1)S(1)}, u32[]{:S(2)}, u32[]{:S(2)}) async-start(bf16[4,128,1024]{2,1,0:T(8,128)(2,1)} %broadcast_in_dim.11), calls=%async_computation | async-start | bytes 2097152 | tf_op jit(solution)/shard_map/all_to_all | solution.py:81
  82.3 14.4 %shard_map.386 = (bf16[1024,1024]{1,0:T(8,128)(2,1)}, bf16[1024,3072]{1,0:T(8,128)(2,1)}, bf16[1024,3072]{1,0:T(8,128)(2,1)}) custom-call(bf16[1024,1024]{1,0:T(8,128)(2,1)} %refs_3_.1, f32[4,1024]{1,0:T(4,128)} %refs_4_.1, bf16[4,128,512]{2,1,0:T(8,128)(2,1)} %copy-done.25, bf16[4,128,512]{2,1,0:T(8,128)(2,1)} %copy-done.42, ...), custom_call_target="tpu_custom_call" | custom-call | flops 6442450944 | bytes 25165824 | tf_op jit(solution)/shard_map/pallas_call | solution.py:286
  96.7 4.2 %all-to-all-done = bf16[4,128,1024]{2,1,0:T(8,128)(2,1)S(1)} async-done(((bf16[4,128,1024]{2,1,0:T(8,128)(2,1)}), bf16[4,128,1024]{2,1,0:T(8,128)(2,1)S(1)}, u32[]{:S(2)}, u32[]{:S(2)}) %all-to-all-start) | async-done | bytes 1048608 | tf_op jit(solution)/shard_map/all_to_all | solution.py:81
  105.1 18.6 %shard_map.387 = (bf16[1024,1024]{1,0:T(8,128)(2,1)}, f32[4,16,256]{2,1,0:T(8,128)}, f32[1024,1024]{1,0:T(8,128)}, bf16[1024,1024]{1,0:T(8,128)(2,1)}, bf16[1024,1024]{1,0:T(8,128)(2,1)}) custom-call(bf16[1024,3072]{1,0:T(8,128)(2,1)} %get-tuple-element.236.j_ref, s32[1024,1]{1,0:T(8,128)} %copy.66.sc_ref, s32[4,1,256]{2,1,0:T(1,128)} %bitcast.43, ...), custom_call_target="tpu_custom_call" | custom-call | flops 8589934592 | bytes 20971520 | tf_op jit(solution)/shard_map/pallas_call | solution.py:359
  128.2 1.5 collective-permute-start.30
  130.5 20.0 %shard_map.388 = (f32[1024,1024]{1,0:T(8,128)}, f32[1024,1024]{1,0:T(8,128)}, bf16[16,128,1024]{2,1,0:T(8,128)(2,1)}, bf16[16,128,1024]{2,1,0:T(8,128)(2,1)}) custom-call(f32[1,1]{1,0:T(1,128)} %bitcast.f_ref, bf16[1024,1024]{1,0:T(8,128)(2,1)} %get-tuple-element.247.s_hbm, bf16[1024,1024]{1,0:T(8,128)(2,1)} %get-tuple-element.248.st_hbm, ...), custom_call_target="tpu_custom_call" | custom-call | flops 12884901888 | bytes 31457280 | tf_op jit(solution)/shard_map/pallas_call | solution.py:459
  150.6 2.2 collective-permute-done.33.refs_5_
  156.3 19.9 %shard_map.389 = (f32[1024,1024]{1,0:T(8,128)}, f32[1024,1024]{1,0:T(8,128)}, bf16[16,128,1024]{2,1,0:T(8,128)(2,1)}, bf16[16,128,1024]{2,1,0:T(8,128)(2,1)}) custom-call(f32[1,1]{1,0:T(1,128)} %bitcast.f_ref, bf16[1024,1024]{1,0:T(8,128)(2,1)} %get-tuple-element.247.s_hbm, ...), custom_call_target="tpu_custom_call", output_to_operand_aliasing={{0}: (10, {}), {1}: (11, {}), {2}: (12, {}), {3}: (13, {})} | custom-call | flops 12884901888 | bytes 31457280 | tf_op jit(solution)/shard_map/pallas_call | solution.py:459
  176.4 1.9 collective-permute-done.37.refs_5_
  179.9 1.5 collective-permute-start.38
  181.5 20.0 %shard_map.390 = (f32[1024,1024]{1,0:T(8,128)}, f32[1024,1024]{1,0:T(8,128)}, bf16[16,128,1024]{2,1,0:T(8,128)(2,1)}, bf16[16,128,1024]{2,1,0:T(8,128)(2,1)}) custom-call(f32[1,1]{1,0:T(1,128)} %bitcast.f_ref, bf16[1024,1024]{1,0:T(8,128)(2,1)} %get-tuple-element.247.s_hbm, ...), custom_call_target="tpu_custom_call", output_to_operand_aliasing={{0}: (10, {}), {1}: (11, {})} | custom-call | flops 12884901888 | bytes 31457280 | tf_op jit(solution)/shard_map/pallas_call | solution.py:459
  201.6 1.9 collective-permute-done.41.refs_5_
  203.5 2.1 add_convert_fusion.7
  206.2 20.3 %shard_map.391 = (f32[1024,1024]{1,0:T(8,128)}, f32[1024,1024]{1,0:T(8,128)}, bf16[16,128,1024]{2,1,0:T(8,128)(2,1)}, bf16[16,128,1024]{2,1,0:T(8,128)(2,1)}) custom-call(f32[1,1]{1,0:T(1,128)} %bitcast.f_ref, bf16[1024,1024]{1,0:T(8,128)(2,1)} %get-tuple-element.247.s_hbm, ...), custom_call_target="tpu_custom_call", output_to_operand_aliasing={{0}: (10, {}), {1}: (11, {}), {2}: (12, {}), {3}: (13, {})} | custom-call | flops 12884901888 | bytes 31457280 | tf_op jit(solution)/shard_map/pallas_call | solution.py:459
  226.6 3.4 add_convert_fusion.5
  232.1 12.7 %shard_map.392 = (bf16[1024,1024]{1,0:T(8,128)(2,1)}, f32[1024,1024]{1,0:T(8,128)}, bf16[1024,1024]{1,0:T(8,128)(2,1)}, bf16[1024,1024]{1,0:T(8,128)(2,1)}, f32[2,1024]{1,0:T(2,128)}) custom-call(f32[1024,1024]{1,0:T(8,128)} %get-tuple-element.319.o_ref, f32[1024,1024]{1,0:T(8,128)} %get-tuple-element.320.b_ref, f32[1024,1024]{1,0:T(8,128)} %get-tuple-element.321.res_ref, ...), custom_call_target="tpu_custom_call" | custom-call | flops 2147483648 | bytes 25165824 | tf_op jit(solution)/shard_map/pallas_call | solution.py:515
  244.8 6.2 %shard_map.393 = (bf16[16,128,512]{2,1,0:T(8,128)(2,1)}, bf16[16,128,512]{2,1,0:T(8,128)(2,1)}) custom-call(f32[1,1]{1,0:T(1,128)} %bitcast.f_ref, bf16[1024,1024]{1,0:T(8,128)(2,1)} %get-tuple-element.326.t_hbm, bf16[1024,1024]{1,0:T(8,128)(2,1)} %get-tuple-element.327.refs_0_), custom_call_target="tpu_custom_call" | custom-call | flops 2147483648 | bytes 6291456 | tf_op jit(solution)/shard_map/pallas_call | solution.py:655
  251.0 5.1 %collective-permute-done.43 = bf16[4,128,1024]{2,1,0:T(8,128)(2,1)S(1)} collective-permute-done((bf16[4,128,1024]{2,1,0:T(8,128)(2,1)S(1)}, bf16[4,128,1024]{2,1,0:T(8,128)(2,1)S(1)}, u32[]{:S(2)}, u32[]{:S(2)}) %collective-permute-start.43) | collective-permute-done | bytes 1048608 | tf_op jit(solution)/shard_map/ppermute | solution.py:77
  256.1 2.9 add_convert_fusion.4
  260.6 14.0 %shard_map.394.refs_0_ = bf16[512,3072]{1,0:T(8,128)(2,1)} custom-call(bf16[1024,3072]{1,0:T(8,128)(2,1)} %get-tuple-element.236.j_ref, bf16[1024,1024]{1,0:T(8,128)(2,1)} %get-tuple-element.336.gm_ref, f32[4,16,256]{2,1,0:T(8,128)} %get-tuple-element.331.log_ref, s32[1024,1]{1,0:T(8,128)} %copy.66.sc_ref, s32[4,1,256]{2,1,0:T(1,128)} %bitcast.44), custom_call_target="tpu_custom_call" | custom-call | flops 5368709120 | bytes 7340032 | tf_op jit(solution)/shard_map/pallas_call | solution.py:568
  274.6 3.4 add_convert_fusion.1
  278.1 3.5 all-to-all-start.1
  281.6 4.4 %add_convert_fusion.2 = (bf16[4,128,1024]{2,1,0:T(8,128)(2,1)}, bf16[4,128,1024]{2,1,0:T(8,128)(2,1)S(1)}) fusion(bf16[16,128,1024]{2,1,0:T(8,128)(2,1)} %collective-permute-done.45, bf16[16,128,1024]{2,1,0:T(8,128)(2,1)} %get-tuple-element.332, bf16[4,128,1024]{2,1,0:T(8,128)(2,1)S(1)} %collective-permute-done.46), kind=kLoop, calls=%fused_computation.4 | loop fusion | flops 5242880 | bytes 7340032 | tf_op jit(solution)/shard_map/convert_element_type | solution.py:44
  288.0 13.8 %shard_map.395.refs_1_ = bf16[512,3072]{1,0:T(8,128)(2,1)} custom-call(bf16[1024,3072]{1,0:T(8,128)(2,1)} %get-tuple-element.236.j_ref, bf16[1024,1024]{1,0:T(8,128)(2,1)} %get-tuple-element.336.gm_ref, f32[4,16,256]{2,1,0:T(8,128)} %get-tuple-element.331.log_ref, s32[1024,1]{1,0:T(8,128)} %copy.66.sc_ref, s32[4,1,256]{2,1,0:T(1,128)} %bitcast.45), custom_call_target="tpu_custom_call" | custom-call | flops 5368709120 | bytes 7340032 | tf_op jit(solution)/shard_map/pallas_call | solution.py:568
  301.8 9.7 %shard_map.396 = (bf16[16,128,512]{2,1,0:T(8,128)(2,1)}, bf16[16,128,512]{2,1,0:T(8,128)(2,1)}) custom-call(f32[1,1]{1,0:T(1,128)} %bitcast.f_ref, bf16[1024,1024]{1,0:T(8,128)(2,1)} %get-tuple-element.337.t_hbm, bf16[512,3072]{1,0:T(8,128)(2,1)} %shard_map.394.refs_0_, bf16[512,3072]{1,0:T(8,128)(2,1)} %shard_map.395.refs_1_), custom_call_target="tpu_custom_call" | custom-call | flops 4294967296 | bytes 10485760 | tf_op jit(solution)/shard_map/pallas_call | solution.py:655
  313.7 6.3 %shard_map.397 = (bf16[16,128,512]{2,1,0:T(8,128)(2,1)}, bf16[16,128,512]{2,1,0:T(8,128)(2,1)}) custom-call(f32[1,1]{1,0:T(1,128)} %bitcast.f_ref, bf16[1024,1024]{1,0:T(8,128)(2,1)} %get-tuple-element.337.t_hbm, bf16[512,3072]{1,0:T(8,128)(2,1)} %shard_map.394.refs_0_, ...), custom_call_target="tpu_custom_call", output_to_operand_aliasing={{0}: (4, {}), {1}: (5, {})} | custom-call | flops 2147483648 | bytes 6291456 | tf_op jit(solution)/shard_map/pallas_call | solution.py:655
  320.2 2.8 add_convert_fusion.15
  323.9 3.8 add_convert_fusion
  327.7 5.3 %all-to-all-start.2 = ((bf16[4,128,1024]{2,1,0:T(8,128)(2,1)}), bf16[4,128,1024]{2,1,0:T(8,128)(2,1)}, u32[]{:S(2)}, u32[]{:S(2)}) async-start(bf16[4,128,1024]{2,1,0:T(8,128)(2,1)} %add_convert_fusion), calls=%async_computation.2 | async-start | bytes 2097152 | tf_op jit(solution)/shard_map/all_to_all | solution.py:81
  333.0 3.1 add_convert_fusion.13
  338.2 2.5 add_convert_fusion.10
  341.7 14.8 %shard_map.398 = (f32[1024,1024]{1,0:T(8,128)}, f32[2,1024]{1,0:T(2,128)}) custom-call(bf16[512,3072]{1,0:T(8,128)(2,1)} %shard_map.394.refs_0_, bf16[512,3072]{1,0:T(8,128)(2,1)} %shard_map.395.refs_1_, f32[1024,1024]{1,0:T(8,128)} %get-tuple-element.353.refs_2_, bf16[1024,1024]{1,0:T(8,128)(2,1)} %refs_3_.1, f32[4,1024]{1,0:T(4,128)} %refs_4_.1, ...), custom_call_target="tpu_custom_call" | custom-call | flops 6442450944 | bytes 23068672 | tf_op jit(solution)/shard_map/pallas_call | solution.py:615
  356.4 2.2 all-to-all-done.2
  360.9 2.4 add_convert_fusion.9
  363.3 4.3 %all-to-all-start.3 = ((bf16[4,128,512]{2,1,0:T(8,128)(2,1)}), bf16[4,128,512]{2,1,0:T(8,128)(2,1)}, u32[]{:S(2)}, u32[]{:S(2)}) async-start(bf16[4,128,512]{2,1,0:T(8,128)(2,1)} %add_convert_fusion.9), calls=%async_computation.3 | async-start | bytes 1048576 | tf_op jit(solution)/shard_map/all_to_all | solution.py:81
  367.6 2.2 add_convert_fusion.11
  373.4 2.8 collective-permute-done.61
  376.2 3.0 collective-permute-done.57
  379.3 3.4 all-to-all-done.3
  389.0 2.4 add_convert_fusion.8
  391.4 3.5 all-to-all-start.4
  395.0 2.8 fusion.9
  398.5 2.0 collective-permute-start.64
  400.6 1.6 fusion.7
  402.1 2.4 collective-permute-done.64
  404.6 4.6 %collective-permute-start.65 = (f32[4,1024]{1,0:T(4,128)S(1)}, f32[4,1024]{1,0:T(4,128)S(1)}, u32[]{:S(2)}, u32[]{:S(2)}) collective-permute-start(f32[4,1024]{1,0:T(4,128)S(1)} %add.225), channel_id=1, source_target_pairs={{0,16},{4,20},{8,24},{12,28},{16,0},{20,4},{24,8},{28,12},{1,17},{... | collective-permute-start | bytes 49160 | tf_op jit(solution)/shard_map/ppermute | solution.py:87
  (256 shorter events, 59.9 us)
Async XLA Ops:
  1.8 12.1 %collective-permute-start.1 = (bf16[128,512]{1,0:T(8,128)(2,1)S(1)}, bf16[128,512]{1,0:T(8,128)(2,1)S(1)}, u32[]{:S(2)}, u32[]{:S(2)}) collective-permute-start(bf16[128,512]{1,0:T(8,128)(2,1)S(1)} %get-tuple-element.435), channel_id=1, source_target_pairs={{16,0},{20,4},{24,8},{28,12},{0,16},{4,20},{8,24},{12,28},{17,1},{... | collective-permute-start | bytes 393224 | tf_op jit(solution)/shard_map/ppermute | solution.py:98
  5.9 8.0 %collective-permute-start = (bf16[128,512]{1,0:T(8,128)(2,1)S(1)}, bf16[128,512]{1,0:T(8,128)(2,1)S(1)}, u32[]{:S(2)}, u32[]{:S(2)}) collective-permute-start(bf16[128,512]{1,0:T(8,128)(2,1)S(1)} %get-tuple-element.435), channel_id=1, source_target_pairs={{8,0},{12,4},{16,8},{20,12},{24,16},{28,20},{0,24},{4,28},{9,1},{1... | collective-permute-start | bytes 393224 | tf_op jit(solution)/shard_map/ppermute | solution.py:98
  7.3 9.0 %collective-permute-start.2 = (bf16[128,512]{1,0:T(8,128)(2,1)S(1)}, bf16[128,512]{1,0:T(8,128)(2,1)S(1)}, u32[]{:S(2)}, u32[]{:S(2)}) collective-permute-start(bf16[128,512]{1,0:T(8,128)(2,1)S(1)} %get-tuple-element.435), channel_id=1, source_target_pairs={{24,0},{28,4},{0,8},{4,12},{8,16},{12,20},{16,24},{20,28},{25,1},{... | collective-permute-start | bytes 393224 | tf_op jit(solution)/shard_map/ppermute | solution.py:98
  18.3 11.0 %collective-permute-start.8 = (bf16[128,512]{1,0:T(8,128)(2,1)S(1)}, bf16[128,512]{1,0:T(8,128)(2,1)S(1)}, u32[]{:S(2)}, u32[]{:S(2)}) collective-permute-start(bf16[128,512]{1,0:T(8,128)(2,1)S(1)} %pad_maximum_fusion.12), channel_id=1, source_target_pairs={{24,0},{28,4},{0,8},{4,12},{8,16},{12,20},{16,24},{20,28},{25,1},{... | collective-permute-start | bytes 393224 | tf_op jit(solution)/shard_map/ppermute | solution.py:98
  20.7 10.7 %collective-permute-start.7 = (bf16[128,512]{1,0:T(8,128)(2,1)S(1)}, bf16[128,512]{1,0:T(8,128)(2,1)S(1)}, u32[]{:S(2)}, u32[]{:S(2)}) collective-permute-start(bf16[128,512]{1,0:T(8,128)(2,1)S(1)} %pad_maximum_fusion.12), channel_id=1, source_target_pairs={{16,0},{20,4},{24,8},{28,12},{0,16},{4,20},{8,24},{12,28},{17,1},{... | collective-permute-start | bytes 393224 | tf_op jit(solution)/shard_map/ppermute | solution.py:98
  22.6 8.8 %collective-permute-start.6 = (bf16[128,512]{1,0:T(8,128)(2,1)S(1)}, bf16[128,512]{1,0:T(8,128)(2,1)S(1)}, u32[]{:S(2)}, u32[]{:S(2)}) collective-permute-start(bf16[128,512]{1,0:T(8,128)(2,1)S(1)} %pad_maximum_fusion.12), channel_id=1, source_target_pairs={{8,0},{12,4},{16,8},{20,12},{24,16},{28,20},{0,24},{4,28},{9,1},{1... | collective-permute-start | bytes 393224 | tf_op jit(solution)/shard_map/ppermute | solution.py:98
  27.2 9.4 %collective-permute-start.4 = (bf16[4,128,512]{2,1,0:T(8,128)(2,1)S(1)}, bf16[4,128,512]{2,1,0:T(8,128)(2,1)}, u32[]{:S(2)}, u32[]{:S(2)}) collective-permute-start(bf16[4,128,512]{2,1,0:T(8,128)(2,1)S(1)} %pad_maximum_fusion.5.refs_0_), channel_id=1, source_target_pairs={{0,4},{1,3},{2,6},{3,1},{4,0},{5,7},{6,2},{7,5},{8,12},{9,11},{10,... | collective-permute-start | bytes 1572872 | tf_op jit(solution)/shard_map/ppermute | solution.py:77
  28.8 13.4 %collective-permute-start.5 = (bf16[4,128,512]{2,1,0:T(8,128)(2,1)S(1)}, bf16[4,128,512]{2,1,0:T(8,128)(2,1)}, u32[]{:S(2)}, u32[]{:S(2)}) collective-permute-start(bf16[4,128,512]{2,1,0:T(8,128)(2,1)S(1)} %collective-permute-done.3.refs_1_), channel_id=1, source_target_pairs={{0,4},{1,3},{2,6},{3,1},{4,0},{5,7},{6,2},{7,5},{8,12},{9,11},{10,... | collective-permute-start | bytes 1572872 | tf_op jit(solution)/shard_map/ppermute | solution.py:77
  31.5 10.7 %collective-permute-start.9 = (bf16[4,128,512]{2,1,0:T(8,128)(2,1)S(1)}, bf16[4,128,512]{2,1,0:T(8,128)(2,1)S(1)}, u32[]{:S(2)}, u32[]{:S(2)}) collective-permute-start(bf16[4,128,512]{2,1,0:T(8,128)(2,1)S(1)} %pad_maximum_fusion.6.refs_8_.refs_0_), channel_id=1, source_target_pairs={{0,1},{1,0},{2,3},{3,2},{4,5},{5,4},{6,7},{7,6},{8,9},{9,8},{10,11... | collective-permute-start | bytes 1572872 | tf_op jit(solution)/shard_map/ppermute | solution.py:68
  42.2 11.1 %collective-permute-start.15 = (bf16[128,1024]{1,0:T(8,128)(2,1)S(1)}, bf16[128,1024]{1,0:T(8,128)(2,1)S(1)}, u32[]{:S(2)}, u32[]{:S(2)}) collective-permute-start(bf16[128,1024]{1,0:T(8,128)(2,1)S(1)} %pad_maximum_fusion.10), channel_id=1, source_target_pairs={{24,0},{28,4},{0,8},{4,12},{8,16},{12,20},{16,24},{20,28},{25,1},{... | collective-permute-start | bytes 786440 | tf_op jit(solution)/shard_map/ppermute | solution.py:98
  42.2 21.7 %collective-permute-start.10 = (bf16[4,128,512]{2,1,0:T(8,128)(2,1)S(1)}, bf16[4,128,512]{2,1,0:T(8,128)(2,1)}, u32[]{:S(2)}, u32[]{:S(2)}) collective-permute-start(bf16[4,128,512]{2,1,0:T(8,128)(2,1)S(1)} %pad_maximum_fusion.6.refs_8_.refs_0_), channel_id=1, source_target_pairs={{0,4},{1,3},{2,6},{3,1},{4,0},{5,7},{6,2},{7,5},{8,12},{9,11},{10,... | collective-permute-start | bytes 1572872 | tf_op jit(solution)/shard_map/ppermute | solution.py:77
  43.7 20.1 %collective-permute-start.11 = (bf16[4,128,512]{2,1,0:T(8,128)(2,1)S(1)}, bf16[4,128,512]{2,1,0:T(8,128)(2,1)S(1)}, u32[]{:S(2)}, u32[]{:S(2)}) collective-permute-start(bf16[4,128,512]{2,1,0:T(8,128)(2,1)S(1)} %collective-permute-done.9.refs_9_.refs_1_), channel_id=1, source_target_pairs={{0,4},{1,3},{2,6},{3,1},{4,0},{5,7},{6,2},{7,5},{8,12},{9,11},{10,... | collective-permute-start | bytes 1572872 | tf_op jit(solution)/shard_map/ppermute | solution.py:77
  44.3 19.6 %collective-permute-start.12 = (bf16[4,128,512]{2,1,0:T(8,128)(2,1)}, bf16[4,128,512]{2,1,0:T(8,128)(2,1)S(1)}, u32[]{:S(2)}, u32[]{:S(2)}) collective-permute-start(bf16[4,128,512]{2,1,0:T(8,128)(2,1)} %collective-permute-done.4.refs_2_), channel_id=1, source_target_pairs={{0,2},{1,5},{2,0},{3,7},{4,6},{5,1},{6,4},{7,3},{8,10},{9,13},{10,... | collective-permute-start | bytes 1572872 | tf_op jit(solution)/shard_map/ppermute | solution.py:77
  45.8 16.2 %collective-permute-start.14 = (bf16[128,1024]{1,0:T(8,128)(2,1)S(1)}, bf16[128,1024]{1,0:T(8,128)(2,1)S(1)}, u32[]{:S(2)}, u32[]{:S(2)}) collective-permute-start(bf16[128,1024]{1,0:T(8,128)(2,1)S(1)} %pad_maximum_fusion.10), channel_id=1, source_target_pairs={{16,0},{20,4},{24,8},{28,12},{0,16},{4,20},{8,24},{12,28},{17,1},{... | collective-permute-start | bytes 786440 | tf_op jit(solution)/shard_map/ppermute | solution.py:98
  53.3 10.4 %collective-permute-start.13 = (bf16[128,1024]{1,0:T(8,128)(2,1)S(1)}, bf16[128,1024]{1,0:T(8,128)(2,1)S(1)}, u32[]{:S(2)}, u32[]{:S(2)}) collective-permute-start(bf16[128,1024]{1,0:T(8,128)(2,1)S(1)} %pad_maximum_fusion.10), channel_id=1, source_target_pairs={{8,0},{12,4},{16,8},{20,12},{24,16},{28,20},{0,24},{4,28},{9,1},{1... | collective-permute-start | bytes 786440 | tf_op jit(solution)/shard_map/ppermute | solution.py:98
  64.7 10.3 %collective-permute-start.20 = (bf16[4,128,1024]{2,1,0:T(8,128)(2,1)S(1)}, bf16[4,128,1024]{2,1,0:T(8,128)(2,1)S(1)}, u32[]{:S(2)}, u32[]{:S(2)}) collective-permute-start(bf16[4,128,1024]{2,1,0:T(8,128)(2,1)S(1)} %pad_maximum_fusion), channel_id=1, source_target_pairs={{0,1},{1,0},{2,3},{3,2},{4,5},{5,4},{6,7},{7,6},{8,9},{9,8},{10,11... | collective-permute-start | bytes 3145736 | tf_op jit(solution)/shard_map/ppermute | solution.py:68
  65.5 9.5 %collective-permute-start.19 = (bf16[4,128,512]{2,1,0:T(8,128)(2,1)}, bf16[4,128,512]{2,1,0:T(8,128)(2,1)}, u32[]{:S(2)}, u32[]{:S(2)}) collective-permute-start(bf16[4,128,512]{2,1,0:T(8,128)(2,1)} %collective-permute-done.10.refs_10_.refs_2_), channel_id=1, source_target_pairs={{0,2},{1,5},{2,0},{3,7},{4,6},{5,1},{6,4},{7,3},{8,10},{9,13},{10,... | collective-permute-start | bytes 1572872 | tf_op jit(solution)/shard_map/ppermute | solution.py:77
  67.0 8.5 %collective-permute-start.17 = (bf16[4,128,512]{2,1,0:T(8,128)(2,1)}, bf16[4,128,512]{2,1,0:T(8,128)(2,1)}, u32[]{:S(2)}, u32[]{:S(2)}) collective-permute-start(bf16[4,128,512]{2,1,0:T(8,128)(2,1)} %collective-permute-done.5.refs_3_), channel_id=1, source_target_pairs={{0,1},{1,0},{2,3},{3,2},{4,5},{5,4},{6,7},{7,6},{8,9},{9,8},{10,11... | collective-permute-start | bytes 1572872 | tf_op jit(solution)/shard_map/ppermute | solution.py:68
  67.0 10.8 %collective-permute-start.16 = (bf16[4,128,512]{2,1,0:T(8,128)(2,1)}, bf16[4,128,512]{2,1,0:T(8,128)(2,1)}, u32[]{:S(2)}, u32[]{:S(2)}) collective-permute-start(bf16[4,128,512]{2,1,0:T(8,128)(2,1)} %collective-permute-done.4.refs_2_), channel_id=1, source_target_pairs={{0,1},{1,0},{2,3},{3,2},{4,5},{5,4},{6,7},{7,6},{8,9},{9,8},{10,11... | collective-permute-start | bytes 1572872 | tf_op jit(solution)/shard_map/ppermute | solution.py:68
  67.5 10.5 %collective-permute-start.21 = (bf16[4,128,512]{2,1,0:T(8,128)(2,1)}, bf16[4,128,512]{2,1,0:T(8,128)(2,1)}, u32[]{:S(2)}, u32[]{:S(2)}) collective-permute-start(bf16[4,128,512]{2,1,0:T(8,128)(2,1)} %collective-permute-done.10.refs_10_.refs_2_), channel_id=1, source_target_pairs={{0,1},{1,0},{2,3},{3,2},{4,5},{5,4},{6,7},{7,6},{8,9},{9,8},{10,11... | collective-permute-start | bytes 1572872 | tf_op jit(solution)/shard_map/ppermute | solution.py:68
  68.6 32.2 %all-to-all-start = ((bf16[4,128,1024]{2,1,0:T(8,128)(2,1)}), bf16[4,128,1024]{2,1,0:T(8,128)(2,1)S(1)}, u32[]{:S(2)}, u32[]{:S(2)}) async-start(bf16[4,128,1024]{2,1,0:T(8,128)(2,1)} %broadcast_in_dim.11), calls=%async_computation | async-start | bytes 2097152 | tf_op jit(solution)/shard_map/all_to_all | solution.py:81
  75.0 2.8 collective-permute-start.18
  75.0 3.0 collective-permute-start.22
  75.9 2.8 collective-permute-start.23
  79.8 21.1 %collective-permute-start.24 = (bf16[8,128,512]{2,1,0:T(8,128)(2,1)}, bf16[8,128,512]{2,1,0:T(8,128)(2,1)}, u32[]{:S(2)}, u32[]{:S(2)}) collective-permute-start(bf16[8,128,512]{2,1,0:T(8,128)(2,1)} %pad_maximum_fusion.1), channel_id=1, source_target_pairs={{0,4},{1,3},{2,6},{3,1},{4,0},{5,7},{6,2},{7,5},{8,12},{9,11},{10,... | collective-permute-start | bytes 3145736 | tf_op jit(solution)/shard_map/ppermute | solution.py:77
  101.9 24.6 %collective-permute-start.28 = (bf16[8,128,512]{2,1,0:T(8,128)(2,1)}, bf16[8,128,512]{2,1,0:T(8,128)(2,1)}, u32[]{:S(2)}, u32[]{:S(2)}) collective-permute-start(bf16[8,128,512]{2,1,0:T(8,128)(2,1)} %collective-permute-done.24.refs_2_), channel_id=1, source_target_pairs={{0,1},{1,0},{2,3},{3,2},{4,5},{5,4},{6,7},{7,6},{8,9},{9,8},{10,11... | collective-permute-start | bytes 3145736 | tf_op jit(solution)/shard_map/ppermute | solution.py:68
  102.0 22.0 %collective-permute-start.25 = (bf16[4,128,512]{2,1,0:T(8,128)(2,1)S(1)}, bf16[4,128,512]{2,1,0:T(8,128)(2,1)}, u32[]{:S(2)}, u32[]{:S(2)}) collective-permute-start(bf16[4,128,512]{2,1,0:T(8,128)(2,1)S(1)} %slice.212), channel_id=1, source_target_pairs={{0,2},{1,5},{2,0},{3,7},{4,6},{5,1},{6,4},{7,3},{8,10},{9,13},{10,... | collective-permute-start | bytes 1572872 | tf_op jit(solution)/shard_map/ppermute | solution.py:77
  103.9 20.1 %collective-permute-start.26 = (bf16[8,128,512]{2,1,0:T(8,128)(2,1)}, bf16[8,128,512]{2,1,0:T(8,128)(2,1)}, u32[]{:S(2)}, u32[]{:S(2)}) collective-permute-start(bf16[8,128,512]{2,1,0:T(8,128)(2,1)} %pad_maximum_fusion.2), channel_id=1, source_target_pairs={{0,4},{1,3},{2,6},{3,1},{4,0},{5,7},{6,2},{7,5},{8,12},{9,11},{10,... | collective-permute-start | bytes 3145736 | tf_op jit(solution)/shard_map/ppermute | solution.py:77
  105.1 18.7 %collective-permute-start.27 = (bf16[4,128,1024]{2,1,0:T(8,128)(2,1)S(1)}, bf16[4,128,1024]{2,1,0:T(8,128)(2,1)S(1)}, u32[]{:S(2)}, u32[]{:S(2)}) collective-permute-start(bf16[4,128,1024]{2,1,0:T(8,128)(2,1)S(1)} %all-to-all-done), channel_id=1, source_target_pairs={{0,1},{1,0},{2,3},{3,2},{4,5},{5,4},{6,7},{7,6},{8,9},{9,8},{10,11... | collective-permute-start | bytes 3145736 | tf_op jit(solution)/shard_map/ppermute | solution.py:68
  127.8 22.8 %collective-permute-start.32 = (bf16[8,128,512]{2,1,0:T(8,128)(2,1)}, bf16[8,128,512]{2,1,0:T(8,128)(2,1)}, u32[]{:S(2)}, u32[]{:S(2)}) collective-permute-start(bf16[8,128,512]{2,1,0:T(8,128)(2,1)} %collective-permute-done.26.refs_2_), channel_id=1, source_target_pairs={{0,1},{1,0},{2,3},{3,2},{4,5},{5,4},{6,7},{7,6},{8,9},{9,8},{10,11... | collective-permute-start | bytes 3145736 | tf_op jit(solution)/shard_map/ppermute | solution.py:68
  128.2 22.3 %collective-permute-start.30 = (bf16[4,128,512]{2,1,0:T(8,128)(2,1)S(1)}, bf16[4,128,512]{2,1,0:T(8,128)(2,1)}, u32[]{:S(2)}, u32[]{:S(2)}) collective-permute-start(bf16[4,128,512]{2,1,0:T(8,128)(2,1)S(1)} %slice.217), channel_id=1, source_target_pairs={{0,2},{1,5},{2,0},{3,7},{4,6},{5,1},{6,4},{7,3},{8,10},{9,13},{10,... | collective-permute-start | bytes 1572872 | tf_op jit(solution)/shard_map/ppermute | solution.py:77
  129.9 20.7 %collective-permute-start.31 = (bf16[8,128,512]{2,1,0:T(8,128)(2,1)S(1)}, bf16[8,128,512]{2,1,0:T(8,128)(2,1)}, u32[]{:S(2)}, u32[]{:S(2)}) collective-permute-start(bf16[8,128,512]{2,1,0:T(8,128)(2,1)S(1)} %pad_maximum_fusion.3), channel_id=1, source_target_pairs={{0,4},{1,3},{2,6},{3,1},{4,0},{5,7},{6,2},{7,5},{8,12},{9,11},{10,... | collective-permute-start | bytes 3145736 | tf_op jit(solution)/shard_map/ppermute | solution.py:77
  153.9 22.4 %collective-permute-start.36 = (bf16[8,128,512]{2,1,0:T(8,128)(2,1)}, bf16[8,128,512]{2,1,0:T(8,128)(2,1)}, u32[]{:S(2)}, u32[]{:S(2)}) collective-permute-start(bf16[8,128,512]{2,1,0:T(8,128)(2,1)} %collective-permute-done.31.refs_2_), channel_id=1, source_target_pairs={{0,1},{1,0},{2,3},{3,2},{4,5},{5,4},{6,7},{7,6},{8,9},{9,8},{10,11... | collective-permute-start | bytes 3145736 | tf_op jit(solution)/shard_map/ppermute | solution.py:68
  154.1 22.1 %collective-permute-start.34 = (bf16[4,128,512]{2,1,0:T(8,128)(2,1)S(1)}, bf16[4,128,512]{2,1,0:T(8,128)(2,1)S(1)}, u32[]{:S(2)}, u32[]{:S(2)}) collective-permute-start(bf16[4,128,512]{2,1,0:T(8,128)(2,1)S(1)} %slice.218), channel_id=1, source_target_pairs={{0,2},{1,5},{2,0},{3,7},{4,6},{5,1},{6,4},{7,3},{8,10},{9,13},{10,... | collective-permute-start | bytes 1572872 | tf_op jit(solution)/shard_map/ppermute | solution.py:77
  155.0 21.3 %collective-permute-start.35 = (bf16[8,128,512]{2,1,0:T(8,128)(2,1)S(1)}, bf16[8,128,512]{2,1,0:T(8,128)(2,1)S(1)}, u32[]{:S(2)}, u32[]{:S(2)}) collective-permute-start(bf16[8,128,512]{2,1,0:T(8,128)(2,1)S(1)} %pad_maximum_fusion.4), channel_id=1, source_target_pairs={{0,4},{1,3},{2,6},{3,1},{4,0},{5,7},{6,2},{7,5},{8,12},{9,11},{10,... | collective-permute-start | bytes 3145736 | tf_op jit(solution)/shard_map/ppermute | solution.py:77
  178.3 23.2 %collective-permute-start.39 = (bf16[16,128,1024]{2,1,0:T(8,128)(2,1)}, bf16[16,128,1024]{2,1,0:T(8,128)(2,1)}, u32[]{:S(2)}, u32[]{:S(2)}) collective-permute-start(bf16[16,128,1024]{2,1,0:T(8,128)(2,1)} %get-tuple-element.298), channel_id=1, source_target_pairs={{0,1},{1,0},{2,3},{3,2},{4,5},{5,4},{6,7},{7,6},{8,9},{9,8},{10,11... | collective-permute-start | bytes 12582920 | tf_op jit(solution)/shard_map/ppermute | solution.py:68
  179.5 22.1 %collective-permute-start.40 = (bf16[8,128,512]{2,1,0:T(8,128)(2,1)}, bf16[8,128,512]{2,1,0:T(8,128)(2,1)S(1)}, u32[]{:S(2)}, u32[]{:S(2)}) collective-permute-start(bf16[8,128,512]{2,1,0:T(8,128)(2,1)} %copy-done.31), channel_id=1, source_target_pairs={{0,1},{1,0},{2,3},{3,2},{4,5},{5,4},{6,7},{7,6},{8,9},{9,8},{10,11... | collective-permute-start | bytes 3145736 | tf_op jit(solution)/shard_map/ppermute | solution.py:68
  179.9 21.6 %collective-permute-start.38 = (bf16[4,128,512]{2,1,0:T(8,128)(2,1)S(1)}, bf16[4,128,512]{2,1,0:T(8,128)(2,1)S(1)}, u32[]{:S(2)}, u32[]{:S(2)}) collective-permute-start(bf16[4,128,512]{2,1,0:T(8,128)(2,1)S(1)} %slice.219), channel_id=1, source_target_pairs={{0,2},{1,5},{2,0},{3,7},{4,6},{5,1},{6,4},{7,3},{8,10},{9,13},{10,... | collective-permute-start | bytes 1572872 | tf_op jit(solution)/shard_map/ppermute | solution.py:77
  205.6 20.9 %collective-permute-start.42 = (bf16[4,128,1024]{2,1,0:T(8,128)(2,1)S(1)}, bf16[4,128,1024]{2,1,0:T(8,128)(2,1)S(1)}, u32[]{:S(2)}, u32[]{:S(2)}) collective-permute-start(bf16[4,128,1024]{2,1,0:T(8,128)(2,1)S(1)} %add_convert_fusion.7), channel_id=1, source_target_pairs={{0,2},{1,5},{2,0},{3,7},{4,6},{5,1},{6,4},{7,3},{8,10},{9,13},{10,... | collective-permute-start | bytes 3145736 | tf_op jit(solution)/shard_map/ppermute | solution.py:77
  226.5 29.6 %collective-permute-start.45 = (bf16[16,128,1024]{2,1,0:T(8,128)(2,1)}, bf16[16,128,1024]{2,1,0:T(8,128)(2,1)}, u32[]{:S(2)}, u32[]{:S(2)}) collective-permute-start(bf16[16,128,1024]{2,1,0:T(8,128)(2,1)} %get-tuple-element.325), channel_id=1, source_target_pairs={{0,1},{1,0},{2,3},{3,2},{4,5},{5,4},{6,7},{7,6},{8,9},{9,8},{10,11... | collective-permute-start | bytes 12582920 | tf_op jit(solution)/shard_map/ppermute | solution.py:68
  230.0 21.0 %collective-permute-start.44 = (bf16[4,128,1024]{2,1,0:T(8,128)(2,1)S(1)}, bf16[4,128,1024]{2,1,0:T(8,128)(2,1)}, u32[]{:S(2)}, u32[]{:S(2)}) collective-permute-start(bf16[4,128,1024]{2,1,0:T(8,128)(2,1)S(1)} %get-tuple-element.407), channel_id=1, source_target_pairs={{0,4},{1,3},{2,6},{3,1},{4,0},{5,7},{6,2},{7,5},{8,12},{9,11},{10,... | collective-permute-start | bytes 3145736 | tf_op jit(solution)/shard_map/ppermute | solution.py:77
  231.5 24.7 %collective-permute-start.43 = (bf16[4,128,1024]{2,1,0:T(8,128)(2,1)S(1)}, bf16[4,128,1024]{2,1,0:T(8,128)(2,1)S(1)}, u32[]{:S(2)}, u32[]{:S(2)}) collective-permute-start(bf16[4,128,1024]{2,1,0:T(8,128)(2,1)S(1)} %get-tuple-element.408), channel_id=1, source_target_pairs={{0,4},{1,3},{2,6},{3,1},{4,0},{5,7},{6,2},{7,5},{8,12},{9,11},{10,... | collective-permute-start | bytes 3145736 | tf_op jit(solution)/shard_map/ppermute | solution.py:77
  259.1 15.5 %collective-permute-start.46 = (bf16[4,128,1024]{2,1,0:T(8,128)(2,1)}, bf16[4,128,1024]{2,1,0:T(8,128)(2,1)S(1)}, u32[]{:S(2)}, u32[]{:S(2)}) collective-permute-start(bf16[4,128,1024]{2,1,0:T(8,128)(2,1)} %add_convert_fusion.4), channel_id=1, source_target_pairs={{0,2},{1,5},{2,0},{3,7},{4,6},{5,1},{6,4},{7,3},{8,10},{9,13},{10,... | collective-permute-start | bytes 3145736 | tf_op jit(solution)/shard_map/ppermute | solution.py:77
  260.6 14.0 %collective-permute-start.47 = (bf16[4,128,1024]{2,1,0:T(8,128)(2,1)}, bf16[4,128,1024]{2,1,0:T(8,128)(2,1)S(1)}, u32[]{:S(2)}, u32[]{:S(2)}) collective-permute-start(bf16[4,128,1024]{2,1,0:T(8,128)(2,1)} %collective-permute-done.44), channel_id=1, source_target_pairs={{0,1},{1,0},{2,3},{3,2},{4,5},{5,4},{6,7},{7,6},{8,9},{9,8},{10,11... | collective-permute-start | bytes 3145736 | tf_op jit(solution)/shard_map/ppermute | solution.py:68
  278.1 34.2 %all-to-all-start.1 = ((bf16[4,128,1024]{2,1,0:T(8,128)(2,1)}), bf16[4,128,1024]{2,1,0:T(8,128)(2,1)S(1)}, u32[]{:S(2)}, u32[]{:S(2)}) async-start(bf16[4,128,1024]{2,1,0:T(8,128)(2,1)} %add_convert_fusion.1), calls=%async_computation.1 | async-start | bytes 2097152 | tf_op jit(solution)/shard_map/all_to_all | solution.py:81
  286.0 25.6 %collective-permute-start.49 = (bf16[4,128,1024]{2,1,0:T(8,128)(2,1)}, bf16[4,128,1024]{2,1,0:T(8,128)(2,1)}, u32[]{:S(2)}, u32[]{:S(2)}) collective-permute-start(bf16[4,128,1024]{2,1,0:T(8,128)(2,1)} %get-tuple-element.405), channel_id=1, source_target_pairs={{0,4},{1,3},{2,6},{3,1},{4,0},{5,7},{6,2},{7,5},{8,12},{9,11},{10,... | collective-permute-start | bytes 3145736 | tf_op jit(solution)/shard_map/ppermute | solution.py:77
  286.8 25.4 %collective-permute-start.48 = (bf16[4,128,1024]{2,1,0:T(8,128)(2,1)S(1)}, bf16[4,128,1024]{2,1,0:T(8,128)(2,1)S(1)}, u32[]{:S(2)}, u32[]{:S(2)}) collective-permute-start(bf16[4,128,1024]{2,1,0:T(8,128)(2,1)S(1)} %get-tuple-element.406), channel_id=1, source_target_pairs={{0,4},{1,3},{2,6},{3,1},{4,0},{5,7},{6,2},{7,5},{8,12},{9,11},{10,... | collective-permute-start | bytes 3145736 | tf_op jit(solution)/shard_map/ppermute | solution.py:77
  313.2 6.9 %collective-permute-start.50 = (bf16[16,128,512]{2,1,0:T(8,128)(2,1)}, bf16[16,128,512]{2,1,0:T(8,128)(2,1)S(1)}, u32[]{:S(2)}, u32[]{:S(2)}) collective-permute-start(bf16[16,128,512]{2,1,0:T(8,128)(2,1)} %get-tuple-element.345), channel_id=1, source_target_pairs={{0,1},{1,0},{2,3},{3,2},{4,5},{5,4},{6,7},{7,6},{8,9},{9,8},{10,11... | collective-permute-start | bytes 6291464 | tf_op jit(solution)/shard_map/ppermute | solution.py:68
  313.2 6.9 %collective-permute-start.51 = (bf16[4,128,1024]{2,1,0:T(8,128)(2,1)}, bf16[4,128,1024]{2,1,0:T(8,128)(2,1)}, u32[]{:S(2)}, u32[]{:S(2)}) collective-permute-start(bf16[4,128,1024]{2,1,0:T(8,128)(2,1)} %collective-permute-done.49), channel_id=1, source_target_pairs={{0,1},{1,0},{2,3},{3,2},{4,5},{5,4},{6,7},{7,6},{8,9},{9,8},{10,11... | collective-permute-start | bytes 3145736 | tf_op jit(solution)/shard_map/ppermute | solution.py:68
  320.1 12.9 %collective-permute-start.53 = (bf16[16,128,512]{2,1,0:T(8,128)(2,1)}, bf16[16,128,512]{2,1,0:T(8,128)(2,1)}, u32[]{:S(2)}, u32[]{:S(2)}) collective-permute-start(bf16[16,128,512]{2,1,0:T(8,128)(2,1)} %get-tuple-element.359), channel_id=1, source_target_pairs={{0,1},{1,0},{2,3},{3,2},{4,5},{5,4},{6,7},{7,6},{8,9},{9,8},{10,11... | collective-permute-start | bytes 6291464 | tf_op jit(solution)/shard_map/ppermute | solution.py:68
  322.9 10.0 %collective-permute-start.52 = (bf16[4,128,512]{2,1,0:T(8,128)(2,1)}, bf16[4,128,512]{2,1,0:T(8,128)(2,1)}, u32[]{:S(2)}, u32[]{:S(2)}) collective-permute-start(bf16[4,128,512]{2,1,0:T(8,128)(2,1)} %add_convert_fusion.15), channel_id=1, source_target_pairs={{0,2},{1,5},{2,0},{3,7},{4,6},{5,1},{6,4},{7,3},{8,10},{9,13},{10,... | collective-permute-start | bytes 1572872 | tf_op jit(solution)/shard_map/ppermute | solution.py:77
  327.7 31.0 %all-to-all-start.2 = ((bf16[4,128,1024]{2,1,0:T(8,128)(2,1)}), bf16[4,128,1024]{2,1,0:T(8,128)(2,1)}, u32[]{:S(2)}, u32[]{:S(2)}) async-start(bf16[4,128,1024]{2,1,0:T(8,128)(2,1)} %add_convert_fusion), calls=%async_computation.2 | async-start | bytes 2097152 | tf_op jit(solution)/shard_map/all_to_all | solution.py:81
  336.1 22.5 %collective-permute-start.55 = (bf16[4,128,512]{2,1,0:T(8,128)(2,1)}, bf16[4,128,512]{2,1,0:T(8,128)(2,1)}, u32[]{:S(2)}, u32[]{:S(2)}) collective-permute-start(bf16[4,128,512]{2,1,0:T(8,128)(2,1)} %get-tuple-element.411), channel_id=1, source_target_pairs={{0,4},{1,3},{2,6},{3,1},{4,0},{5,7},{6,2},{7,5},{8,12},{9,11},{10,... | collective-permute-start | bytes 1572872 | tf_op jit(solution)/shard_map/ppermute | solution.py:77
  337.0 21.6 %collective-permute-start.54 = (bf16[4,128,512]{2,1,0:T(8,128)(2,1)}, bf16[4,128,512]{2,1,0:T(8,128)(2,1)}, u32[]{:S(2)}, u32[]{:S(2)}) collective-permute-start(bf16[4,128,512]{2,1,0:T(8,128)(2,1)} %get-tuple-element.412), channel_id=1, source_target_pairs={{0,4},{1,3},{2,6},{3,1},{4,0},{5,7},{6,2},{7,5},{8,12},{9,11},{10,... | collective-permute-start | bytes 1572872 | tf_op jit(solution)/shard_map/ppermute | solution.py:77
  340.6 18.0 %collective-permute-start.56 = (bf16[4,128,512]{2,1,0:T(8,128)(2,1)}, bf16[4,128,512]{2,1,0:T(8,128)(2,1)}, u32[]{:S(2)}, u32[]{:S(2)}) collective-permute-start(bf16[4,128,512]{2,1,0:T(8,128)(2,1)} %get-tuple-element.410), channel_id=1, source_target_pairs={{0,2},{1,5},{2,0},{3,7},{4,6},{5,1},{6,4},{7,3},{8,10},{9,13},{10,... | collective-permute-start | bytes 1572872 | tf_op jit(solution)/shard_map/ppermute | solution.py:77
  358.7 17.5 %collective-permute-start.58 = (bf16[4,128,512]{2,1,0:T(8,128)(2,1)}, bf16[4,128,512]{2,1,0:T(8,128)(2,1)}, u32[]{:S(2)}, u32[]{:S(2)}) collective-permute-start(bf16[4,128,512]{2,1,0:T(8,128)(2,1)} %get-tuple-element.409), channel_id=1, source_target_pairs={{0,4},{1,3},{2,6},{3,1},{4,0},{5,7},{6,2},{7,5},{8,12},{9,11},{10,... | collective-permute-start | bytes 1572872 | tf_op jit(solution)/shard_map/ppermute | solution.py:77
  363.3 19.4 %all-to-all-start.3 = ((bf16[4,128,512]{2,1,0:T(8,128)(2,1)}), bf16[4,128,512]{2,1,0:T(8,128)(2,1)}, u32[]{:S(2)}, u32[]{:S(2)}) async-start(bf16[4,128,512]{2,1,0:T(8,128)(2,1)} %add_convert_fusion.9), calls=%async_computation.3 | async-start | bytes 1048576 | tf_op jit(solution)/shard_map/all_to_all | solution.py:81
  369.8 9.5 %collective-permute-start.57 = (bf16[4,128,512]{2,1,0:T(8,128)(2,1)}, bf16[4,128,512]{2,1,0:T(8,128)(2,1)}, u32[]{:S(2)}, u32[]{:S(2)}) collective-permute-start(bf16[4,128,512]{2,1,0:T(8,128)(2,1)} %add_convert_fusion.11), channel_id=1, source_target_pairs={{0,4},{1,3},{2,6},{3,1},{4,0},{5,7},{6,2},{7,5},{8,12},{9,11},{10,... | collective-permute-start | bytes 1572872 | tf_op jit(solution)/shard_map/ppermute | solution.py:77
  372.3 4.0 collective-permute-start.61
  382.7 6.3 %collective-permute-start.62 = (bf16[4,128,512]{2,1,0:T(8,128)(2,1)}, bf16[4,128,512]{2,1,0:T(8,128)(2,1)}, u32[]{:S(2)}, u32[]{:S(2)}) collective-permute-start(bf16[4,128,512]{2,1,0:T(8,128)(2,1)} %collective-permute-done.58), channel_id=1, source_target_pairs={{0,1},{1,0},{2,3},{3,2},{4,5},{5,4},{6,7},{7,6},{8,9},{9,8},{10,11... | collective-permute-start | bytes 1572872 | tf_op jit(solution)/shard_map/ppermute | solution.py:68
  387.7 10.1 %collective-permute-start.63 = (f32[4,1024]{1,0:T(4,128)S(1)}, f32[4,1024]{1,0:T(4,128)}, u32[]{:S(2)}, u32[]{:S(2)}) collective-permute-start(f32[4,1024]{1,0:T(4,128)S(1)} %add.200), channel_id=1, source_target_pairs={{0,4},{4,0},{8,12},{12,8},{16,20},{20,16},{24,28},{28,24},{1,5},{5... | collective-permute-start | bytes 49160 | tf_op jit(solution)/shard_map/ppermute | solution.py:87
  391.4 20.1 %all-to-all-start.4 = ((bf16[4,128,512]{2,1,0:T(8,128)(2,1)}), bf16[4,128,512]{2,1,0:T(8,128)(2,1)S(1)}, u32[]{:S(2)}, u32[]{:S(2)}) async-start(bf16[4,128,512]{2,1,0:T(8,128)(2,1)} %add_convert_fusion.8), calls=%async_computation.4 | async-start | bytes 1048576 | tf_op jit(solution)/shard_map/all_to_all | solution.py:81
  398.5 6.0 %collective-permute-start.64 = (f32[4,1024]{1,0:T(4,128)S(1)}, f32[4,1024]{1,0:T(4,128)S(1)}, u32[]{:S(2)}, u32[]{:S(2)}) collective-permute-start(f32[4,1024]{1,0:T(4,128)S(1)} %add.224), channel_id=1, source_target_pairs={{0,8},{4,12},{8,0},{12,4},{16,24},{20,28},{24,16},{28,20},{1,9},{5... | collective-permute-start | bytes 49160 | tf_op jit(solution)/shard_map/ppermute | solution.py:87
  404.6 6.3 %collective-permute-start.65 = (f32[4,1024]{1,0:T(4,128)S(1)}, f32[4,1024]{1,0:T(4,128)S(1)}, u32[]{:S(2)}, u32[]{:S(2)}) collective-permute-start(f32[4,1024]{1,0:T(4,128)S(1)} %add.225), channel_id=1, source_target_pairs={{0,16},{4,20},{8,24},{12,28},{16,0},{20,4},{24,8},{28,12},{1,17},{... | collective-permute-start | bytes 49160 | tf_op jit(solution)/shard_map/ppermute | solution.py:87
  (56 other events, 540.9 us)

commit v2 on v1

--- a/solution.py
+++ b/solution.py
@@ -852,12 +852,14 @@
     terms = grid.total(terms, "shard")
     q1_over, q0_sent, terms = tie(q1_over, q0_sent, terms)
     q1_passed = grid.scatter_home(q1_over)
+    q1_passed, q0_sent, r0_sent, r1_sent = tie(q1_passed, q0_sent, r0_sent, r1_sent)
     q1_sent = grid.scatter_z(q1[0], q1_other, q1_over, q1_passed)
-    norm_grad = grid.total(terms, "dp")
     q0_total, q1_total = grid.scatter_end(q0_sent), grid.scatter_end(q1_sent)
     grad_qkv = jnp.concatenate([q0_total, q1_total[:, : cuts[1]]], axis=1)
     grad_out = q1_total[:, cuts[1] :]
     totals = [grid.scatter_end(r0_sent), grid.scatter_end(r1_sent)]
+    terms, totals = tie(terms, totals)
+    norm_grad = grid.total(terms, "dp")
 
     def pieces_of(first, lanes):
         return [

time: 419 us -> 416 us (level)
  transfers between devices with their start and end apart: 71 -> 71, of which waited for: 26 -> 26; matrix products, arithmetic and copies ran while one was open for 12% -> 10% of each run, Pallas kernels for 46% -> 46%
where the time goes in v2:
time: 416 us; the launch traced here: 410 us
  Pallas kernels  191 us (46%)
  starting transfers between devices  77.4 us (19%)
  waiting for transfers between devices  73.6 us (18%)
  other arithmetic  49.4 us (12%)
  local copies, waits for them, and re-layouts  15.9 us (4%)
    pallas_call x4, Pallas kernels, feed_forward(): pl.pallas_call(kernel, out_shape=(shape_of((count, width), F32),) * 2 + (...  80.3 us
    convert_element_type x19, other arithmetic, thin(): return values.astype(BF16)  40.6 us
    ppermute x26, starting transfers between devices, cross(): return lax.ppermute(values, ('dp', 'shard'), pairs)  29.3 us
    pallas_call x2, Pallas kernels, attention_back(): pl.pallas_call(kernel, grid=(blocks,), out_shape=shape_of((count, 3 * wid...  27.8 us
    ppermute x9, waiting for transfers between devices, gather_z(): parts.append(lax.ppermute(piece, 'dp', shift))  27.7 us
    all_to_all x5, starting transfers between devices, z_exchange(): lax.all_to_all(values, 'dp', 0, 0, axis_index_groups=groups, tiled=True)  22.4 us
    pallas_call x3, Pallas kernels, weight_grad(): pl.pallas_call(kernel, out_shape=(region, region), in_specs=[SCALAR] + [A...  22.4 us
    ppermute x26, waiting for transfers between devices, cross(): return lax.ppermute(values, ('dp', 'shard'), pairs)  18.8 us
  transfers between devices with their start and end apart: 71, of which 26 were waited for; matrix products, arithmetic and copies ran while one was open for 10% of the time, Pallas kernels for 46%

profile of v2, /device:TPU:0, one launch (start us, length us, event | category | flops | bytes accessed | tf_op | source)
XLA Modules:
  0.0 410.5 jit_solution(14313647585868317255)
XLA Ops:
  1.8 4.1 collective-permute-start.1
  8.0 5.9 %collective-permute-done.1 = bf16[128,512]{1,0:T(8,128)(2,1)S(1)} collective-permute-done((bf16[128,512]{1,0:T(8,128)(2,1)S(1)}, bf16[128,512]{1,0:T(8,128)(2,1)S(1)}, u32[]{:S(2)}, u32[]{:S(2)}) %collective-permute-start.1) | collective-permute-done | bytes 131104 | tf_op jit(solution)/shard_map/ppermute | solution.py:98
  13.9 2.4 collective-permute-done.2
  16.8 1.6 collective-permute-done.3.refs_1_
  18.3 2.4 collective-permute-start.8
  20.7 1.9 collective-permute-start.7
  22.6 2.9 collective-permute-start.6
  25.5 1.7 slice_reduce_fusion.1
  27.2 1.6 collective-permute-start.4
  29.3 2.1 collective-permute-done.7
  31.6 4.9 %collective-permute-done.4.refs_2_ = bf16[4,128,512]{2,1,0:T(8,128)(2,1)} collective-permute-done((bf16[4,128,512]{2,1,0:T(8,128)(2,1)S(1)}, bf16[4,128,512]{2,1,0:T(8,128)(2,1)}, u32[]{:S(2)}, u32[]{:S(2)}) %collective-permute-start.4) | collective-permute-done | bytes 524320 | tf_op jit(solution)/shard_map/ppermute | solution.py:77
  36.6 5.6 %collective-permute-done.5.refs_3_ = bf16[4,128,512]{2,1,0:T(8,128)(2,1)} collective-permute-done((bf16[4,128,512]{2,1,0:T(8,128)(2,1)S(1)}, bf16[4,128,512]{2,1,0:T(8,128)(2,1)}, u32[]{:S(2)}, u32[]{:S(2)}) %collective-permute-start.5) | collective-permute-done | bytes 524320 | tf_op jit(solution)/shard_map/ppermute | solution.py:77
  42.2 1.6 collective-permute-start.10
  44.3 1.5 collective-permute-start.12
  46.3 7.0 %collective-permute-done.15 = bf16[128,1024]{1,0:T(8,128)(2,1)S(1)} collective-permute-done((bf16[128,1024]{1,0:T(8,128)(2,1)S(1)}, bf16[128,1024]{1,0:T(8,128)(2,1)S(1)}, u32[]{:S(2)}, u32[]{:S(2)}) %collective-permute-start.15) | collective-permute-done | bytes 262176 | tf_op jit(solution)/shard_map/ppermute | solution.py:98
  53.4 8.6 %collective-permute-done.14 = bf16[128,1024]{1,0:T(8,128)(2,1)S(1)} collective-permute-done((bf16[128,1024]{1,0:T(8,128)(2,1)S(1)}, bf16[128,1024]{1,0:T(8,128)(2,1)S(1)}, u32[]{:S(2)}, u32[]{:S(2)}) %collective-permute-start.14) | collective-permute-done | bytes 262176 | tf_op jit(solution)/shard_map/ppermute | solution.py:98
  62.0 1.7 collective-permute-done.13
  65.5 1.5 collective-permute-start.19
  68.8 5.9 %all-to-all-start = ((bf16[4,128,1024]{2,1,0:T(8,128)(2,1)}), bf16[4,128,1024]{2,1,0:T(8,128)(2,1)S(1)}, u32[]{:S(2)}, u32[]{:S(2)}) async-start(bf16[4,128,1024]{2,1,0:T(8,128)(2,1)} %broadcast_in_dim.11), calls=%async_computation | async-start | bytes 2097152 | tf_op jit(solution)/shard_map/all_to_all | solution.py:81
  82.3 14.4 %shard_map.386 = (bf16[1024,1024]{1,0:T(8,128)(2,1)}, bf16[1024,3072]{1,0:T(8,128)(2,1)}, bf16[1024,3072]{1,0:T(8,128)(2,1)}) custom-call(bf16[1024,1024]{1,0:T(8,128)(2,1)} %refs_3_.1, f32[4,1024]{1,0:T(4,128)} %refs_4_.1, bf16[4,128,512]{2,1,0:T(8,128)(2,1)} %copy-done.24, bf16[4,128,512]{2,1,0:T(8,128)(2,1)} %copy-done.42, ...), custom_call_target="tpu_custom_call" | custom-call | flops 6442450944 | bytes 25165824 | tf_op jit(solution)/shard_map/pallas_call | solution.py:286
  96.7 4.2 %all-to-all-done = bf16[4,128,1024]{2,1,0:T(8,128)(2,1)S(1)} async-done(((bf16[4,128,1024]{2,1,0:T(8,128)(2,1)}), bf16[4,128,1024]{2,1,0:T(8,128)(2,1)S(1)}, u32[]{:S(2)}, u32[]{:S(2)}) %all-to-all-start) | async-done | bytes 1048608 | tf_op jit(solution)/shard_map/all_to_all | solution.py:81
  105.2 18.6 %shard_map.387 = (bf16[1024,1024]{1,0:T(8,128)(2,1)}, f32[4,16,256]{2,1,0:T(8,128)}, f32[1024,1024]{1,0:T(8,128)}, bf16[1024,1024]{1,0:T(8,128)(2,1)}, bf16[1024,1024]{1,0:T(8,128)(2,1)}) custom-call(bf16[1024,3072]{1,0:T(8,128)(2,1)} %get-tuple-element.243.j_ref, s32[1024,1]{1,0:T(8,128)} %copy.66.sc_ref, s32[4,1,256]{2,1,0:T(1,128)} %bitcast.43, ...), custom_call_target="tpu_custom_call" | custom-call | flops 8589934592 | bytes 20971520 | tf_op jit(solution)/shard_map/pallas_call | solution.py:359
  128.2 1.5 collective-permute-start.30
  130.5 20.0 %shard_map.388 = (f32[1024,1024]{1,0:T(8,128)}, f32[1024,1024]{1,0:T(8,128)}, bf16[16,128,1024]{2,1,0:T(8,128)(2,1)}, bf16[16,128,1024]{2,1,0:T(8,128)(2,1)}) custom-call(f32[1,1]{1,0:T(1,128)} %bitcast.f_ref, bf16[1024,1024]{1,0:T(8,128)(2,1)} %get-tuple-element.254.s_hbm, bf16[1024,1024]{1,0:T(8,128)(2,1)} %get-tuple-element.255.st_hbm, ...), custom_call_target="tpu_custom_call" | custom-call | flops 12884901888 | bytes 31457280 | tf_op jit(solution)/shard_map/pallas_call | solution.py:459
  150.6 2.2 collective-permute-done.33.refs_5_
  156.3 19.9 %shard_map.389 = (f32[1024,1024]{1,0:T(8,128)}, f32[1024,1024]{1,0:T(8,128)}, bf16[16,128,1024]{2,1,0:T(8,128)(2,1)}, bf16[16,128,1024]{2,1,0:T(8,128)(2,1)}) custom-call(f32[1,1]{1,0:T(1,128)} %bitcast.f_ref, bf16[1024,1024]{1,0:T(8,128)(2,1)} %get-tuple-element.254.s_hbm, ...), custom_call_target="tpu_custom_call", output_to_operand_aliasing={{0}: (10, {}), {1}: (11, {}), {2}: (12, {}), {3}: (13, {})} | custom-call | flops 12884901888 | bytes 31457280 | tf_op jit(solution)/shard_map/pallas_call | solution.py:459
  176.4 1.9 collective-permute-done.37.refs_5_
  179.7 1.5 collective-permute-start.38
  181.2 20.0 %shard_map.390 = (f32[1024,1024]{1,0:T(8,128)}, f32[1024,1024]{1,0:T(8,128)}, bf16[16,128,1024]{2,1,0:T(8,128)(2,1)}, bf16[16,128,1024]{2,1,0:T(8,128)(2,1)}) custom-call(f32[1,1]{1,0:T(1,128)} %bitcast.f_ref, bf16[1024,1024]{1,0:T(8,128)(2,1)} %get-tuple-element.254.s_hbm, ...), custom_call_target="tpu_custom_call", output_to_operand_aliasing={{0}: (10, {}), {1}: (11, {})} | custom-call | flops 12884901888 | bytes 31457280 | tf_op jit(solution)/shard_map/pallas_call | solution.py:459
  201.4 1.9 collective-permute-done.41.refs_5_
  203.3 2.1 add_convert_fusion.7
  206.0 20.3 %shard_map.391 = (f32[1024,1024]{1,0:T(8,128)}, f32[1024,1024]{1,0:T(8,128)}, bf16[16,128,1024]{2,1,0:T(8,128)(2,1)}, bf16[16,128,1024]{2,1,0:T(8,128)(2,1)}) custom-call(f32[1,1]{1,0:T(1,128)} %bitcast.f_ref, bf16[1024,1024]{1,0:T(8,128)(2,1)} %get-tuple-element.254.s_hbm, ...), custom_call_target="tpu_custom_call", output_to_operand_aliasing={{0}: (10, {}), {1}: (11, {}), {2}: (12, {}), {3}: (13, {})} | custom-call | flops 12884901888 | bytes 31457280 | tf_op jit(solution)/shard_map/pallas_call | solution.py:459
  226.4 3.4 add_convert_fusion.5
  231.9 12.7 %shard_map.392 = (bf16[1024,1024]{1,0:T(8,128)(2,1)}, f32[1024,1024]{1,0:T(8,128)}, bf16[1024,1024]{1,0:T(8,128)(2,1)}, bf16[1024,1024]{1,0:T(8,128)(2,1)}, f32[2,1024]{1,0:T(2,128)}) custom-call(f32[1024,1024]{1,0:T(8,128)} %get-tuple-element.326.o_ref, f32[1024,1024]{1,0:T(8,128)} %get-tuple-element.327.b_ref, f32[1024,1024]{1,0:T(8,128)} %get-tuple-element.328.res_ref, ...), custom_call_target="tpu_custom_call" | custom-call | flops 2147483648 | bytes 25165824 | tf_op jit(solution)/shard_map/pallas_call | solution.py:515
  244.6 6.2 %shard_map.393 = (bf16[16,128,512]{2,1,0:T(8,128)(2,1)}, bf16[16,128,512]{2,1,0:T(8,128)(2,1)}) custom-call(f32[1,1]{1,0:T(1,128)} %bitcast.f_ref, bf16[1024,1024]{1,0:T(8,128)(2,1)} %get-tuple-element.333.t_hbm, bf16[1024,1024]{1,0:T(8,128)(2,1)} %get-tuple-element.334.refs_0_), custom_call_target="tpu_custom_call" | custom-call | flops 2147483648 | bytes 6291456 | tf_op jit(solution)/shard_map/pallas_call | solution.py:655
  250.8 5.1 %collective-permute-done.43 = bf16[4,128,1024]{2,1,0:T(8,128)(2,1)S(1)} collective-permute-done((bf16[4,128,1024]{2,1,0:T(8,128)(2,1)S(1)}, bf16[4,128,1024]{2,1,0:T(8,128)(2,1)S(1)}, u32[]{:S(2)}, u32[]{:S(2)}) %collective-permute-start.43) | collective-permute-done | bytes 1048608 | tf_op jit(solution)/shard_map/ppermute | solution.py:77
  255.9 2.9 add_convert_fusion.4
  258.9 1.5 collective-permute-start.46
  260.4 14.0 %shard_map.394.refs_0_ = bf16[512,3072]{1,0:T(8,128)(2,1)} custom-call(bf16[1024,3072]{1,0:T(8,128)(2,1)} %get-tuple-element.243.j_ref, bf16[1024,1024]{1,0:T(8,128)(2,1)} %get-tuple-element.343.gm_ref, f32[4,16,256]{2,1,0:T(8,128)} %get-tuple-element.338.log_ref, s32[1024,1]{1,0:T(8,128)} %copy.66.sc_ref, s32[4,1,256]{2,1,0:T(1,128)} %bitcast.44), custom_call_target="tpu_custom_call" | custom-call | flops 5368709120 | bytes 7340032 | tf_op jit(solution)/shard_map/pallas_call | solution.py:568
  274.4 3.4 add_convert_fusion.1
  277.9 3.5 all-to-all-start.1
  281.4 4.4 %add_convert_fusion.2 = (bf16[4,128,1024]{2,1,0:T(8,128)(2,1)}, bf16[4,128,1024]{2,1,0:T(8,128)(2,1)S(1)}) fusion(bf16[16,128,1024]{2,1,0:T(8,128)(2,1)} %collective-permute-done.45, bf16[16,128,1024]{2,1,0:T(8,128)(2,1)} %get-tuple-element.339, bf16[4,128,1024]{2,1,0:T(8,128)(2,1)S(1)} %collective-permute-done.46), kind=kLoop, calls=%fused_computation.4 | loop fusion | flops 5242880 | bytes 7340032 | tf_op jit(solution)/shard_map/convert_element_type | solution.py:44
  287.8 13.8 %shard_map.395.refs_1_ = bf16[512,3072]{1,0:T(8,128)(2,1)} custom-call(bf16[1024,3072]{1,0:T(8,128)(2,1)} %get-tuple-element.243.j_ref, bf16[1024,1024]{1,0:T(8,128)(2,1)} %get-tuple-element.343.gm_ref, f32[4,16,256]{2,1,0:T(8,128)} %get-tuple-element.338.log_ref, s32[1024,1]{1,0:T(8,128)} %copy.66.sc_ref, s32[4,1,256]{2,1,0:T(1,128)} %bitcast.45), custom_call_target="tpu_custom_call" | custom-call | flops 5368709120 | bytes 7340032 | tf_op jit(solution)/shard_map/pallas_call | solution.py:568
  301.6 9.8 %shard_map.396 = (bf16[16,128,512]{2,1,0:T(8,128)(2,1)}, bf16[16,128,512]{2,1,0:T(8,128)(2,1)}) custom-call(f32[1,1]{1,0:T(1,128)} %bitcast.f_ref, bf16[1024,1024]{1,0:T(8,128)(2,1)} %get-tuple-element.344.t_hbm, bf16[512,3072]{1,0:T(8,128)(2,1)} %shard_map.394.refs_0_, bf16[512,3072]{1,0:T(8,128)(2,1)} %shard_map.395.refs_1_), custom_call_target="tpu_custom_call" | custom-call | flops 4294967296 | bytes 10485760 | tf_op jit(solution)/shard_map/pallas_call | solution.py:655
  312.9 6.3 %shard_map.397 = (bf16[16,128,512]{2,1,0:T(8,128)(2,1)}, bf16[16,128,512]{2,1,0:T(8,128)(2,1)}) custom-call(f32[1,1]{1,0:T(1,128)} %bitcast.f_ref, bf16[1024,1024]{1,0:T(8,128)(2,1)} %get-tuple-element.344.t_hbm, bf16[512,3072]{1,0:T(8,128)(2,1)} %shard_map.394.refs_0_, ...), custom_call_target="tpu_custom_call", output_to_operand_aliasing={{0}: (4, {}), {1}: (5, {})} | custom-call | flops 2147483648 | bytes 6291456 | tf_op jit(solution)/shard_map/pallas_call | solution.py:655
  320.6 2.0 add_convert_fusion.15
  323.5 4.1 add_convert_fusion
  327.6 5.3 %all-to-all-start.2 = ((bf16[4,128,1024]{2,1,0:T(8,128)(2,1)}), bf16[4,128,1024]{2,1,0:T(8,128)(2,1)}, u32[]{:S(2)}, u32[]{:S(2)}) async-start(bf16[4,128,1024]{2,1,0:T(8,128)(2,1)} %add_convert_fusion), calls=%async_computation.2 | async-start | bytes 2097152 | tf_op jit(solution)/shard_map/all_to_all | solution.py:81
  332.9 3.1 add_convert_fusion.13
  338.1 2.5 add_convert_fusion.10
  341.6 14.7 %shard_map.398 = (f32[1024,1024]{1,0:T(8,128)}, f32[2,1024]{1,0:T(2,128)}) custom-call(bf16[512,3072]{1,0:T(8,128)(2,1)} %shard_map.394.refs_0_, bf16[512,3072]{1,0:T(8,128)(2,1)} %shard_map.395.refs_1_, f32[1024,1024]{1,0:T(8,128)} %get-tuple-element.360.refs_2_, bf16[1024,1024]{1,0:T(8,128)(2,1)} %refs_3_.1, f32[4,1024]{1,0:T(4,128)} %refs_4_.1, ...), custom_call_target="tpu_custom_call" | custom-call | flops 6442450944 | bytes 23068672 | tf_op jit(solution)/shard_map/pallas_call | solution.py:615
  356.4 2.1 all-to-all-done.2
  360.7 2.4 add_convert_fusion.9
  363.1 4.3 %all-to-all-start.3 = ((bf16[4,128,512]{2,1,0:T(8,128)(2,1)}), bf16[4,128,512]{2,1,0:T(8,128)(2,1)}, u32[]{:S(2)}, u32[]{:S(2)}) async-start(bf16[4,128,512]{2,1,0:T(8,128)(2,1)} %add_convert_fusion.9), calls=%async_computation.3 | async-start | bytes 1048576 | tf_op jit(solution)/shard_map/all_to_all | solution.py:81
  372.3 3.0 collective-permute-done.61
  375.4 2.8 collective-permute-done.57
  378.2 4.4 %all-to-all-done.3 = bf16[4,128,512]{2,1,0:T(8,128)(2,1)} async-done(((bf16[4,128,512]{2,1,0:T(8,128)(2,1)}), bf16[4,128,512]{2,1,0:T(8,128)(2,1)}, u32[]{:S(2)}, u32[]{:S(2)}) %all-to-all-start.3) | async-done | bytes 524320 | tf_op jit(solution)/shard_map/all_to_all | solution.py:81
  382.5 2.1 collective-permute-done.62
  384.6 2.3 add_convert_fusion.8
  386.9 3.5 all-to-all-start.4
  395.5 2.8 fusion.9
  399.0 2.0 collective-permute-start.64
  401.0 1.5 fusion.7
  402.7 2.9 collective-permute-start.65
  (256 shorter events, 59.0 us)
Async XLA Ops:
  1.8 12.1 %collective-permute-start.1 = (bf16[128,512]{1,0:T(8,128)(2,1)S(1)}, bf16[128,512]{1,0:T(8,128)(2,1)S(1)}, u32[]{:S(2)}, u32[]{:S(2)}) collective-permute-start(bf16[128,512]{1,0:T(8,128)(2,1)S(1)} %get-tuple-element.449), channel_id=1, source_target_pairs={{16,0},{20,4},{24,8},{28,12},{0,16},{4,20},{8,24},{12,28},{17,1},{... | collective-permute-start | bytes 393224 | tf_op jit(solution)/shard_map/ppermute | solution.py:98
  5.9 8.0 %collective-permute-start = (bf16[128,512]{1,0:T(8,128)(2,1)S(1)}, bf16[128,512]{1,0:T(8,128)(2,1)S(1)}, u32[]{:S(2)}, u32[]{:S(2)}) collective-permute-start(bf16[128,512]{1,0:T(8,128)(2,1)S(1)} %get-tuple-element.449), channel_id=1, source_target_pairs={{8,0},{12,4},{16,8},{20,12},{24,16},{28,20},{0,24},{4,28},{9,1},{1... | collective-permute-start | bytes 393224 | tf_op jit(solution)/shard_map/ppermute | solution.py:98
  7.3 9.0 %collective-permute-start.2 = (bf16[128,512]{1,0:T(8,128)(2,1)S(1)}, bf16[128,512]{1,0:T(8,128)(2,1)S(1)}, u32[]{:S(2)}, u32[]{:S(2)}) collective-permute-start(bf16[128,512]{1,0:T(8,128)(2,1)S(1)} %get-tuple-element.449), channel_id=1, source_target_pairs={{24,0},{28,4},{0,8},{4,12},{8,16},{12,20},{16,24},{20,28},{25,1},{... | collective-permute-start | bytes 393224 | tf_op jit(solution)/shard_map/ppermute | solution.py:98
  18.3 11.0 %collective-permute-start.8 = (bf16[128,512]{1,0:T(8,128)(2,1)S(1)}, bf16[128,512]{1,0:T(8,128)(2,1)S(1)}, u32[]{:S(2)}, u32[]{:S(2)}) collective-permute-start(bf16[128,512]{1,0:T(8,128)(2,1)S(1)} %pad_maximum_fusion.12), channel_id=1, source_target_pairs={{24,0},{28,4},{0,8},{4,12},{8,16},{12,20},{16,24},{20,28},{25,1},{... | collective-permute-start | bytes 393224 | tf_op jit(solution)/shard_map/ppermute | solution.py:98
  20.7 10.7 %collective-permute-start.7 = (bf16[128,512]{1,0:T(8,128)(2,1)S(1)}, bf16[128,512]{1,0:T(8,128)(2,1)S(1)}, u32[]{:S(2)}, u32[]{:S(2)}) collective-permute-start(bf16[128,512]{1,0:T(8,128)(2,1)S(1)} %pad_maximum_fusion.12), channel_id=1, source_target_pairs={{16,0},{20,4},{24,8},{28,12},{0,16},{4,20},{8,24},{12,28},{17,1},{... | collective-permute-start | bytes 393224 | tf_op jit(solution)/shard_map/ppermute | solution.py:98
  22.6 8.8 %collective-permute-start.6 = (bf16[128,512]{1,0:T(8,128)(2,1)S(1)}, bf16[128,512]{1,0:T(8,128)(2,1)S(1)}, u32[]{:S(2)}, u32[]{:S(2)}) collective-permute-start(bf16[128,512]{1,0:T(8,128)(2,1)S(1)} %pad_maximum_fusion.12), channel_id=1, source_target_pairs={{8,0},{12,4},{16,8},{20,12},{24,16},{28,20},{0,24},{4,28},{9,1},{1... | collective-permute-start | bytes 393224 | tf_op jit(solution)/shard_map/ppermute | solution.py:98
  27.2 9.4 %collective-permute-start.4 = (bf16[4,128,512]{2,1,0:T(8,128)(2,1)S(1)}, bf16[4,128,512]{2,1,0:T(8,128)(2,1)}, u32[]{:S(2)}, u32[]{:S(2)}) collective-permute-start(bf16[4,128,512]{2,1,0:T(8,128)(2,1)S(1)} %pad_maximum_fusion.5.refs_0_), channel_id=1, source_target_pairs={{0,4},{1,3},{2,6},{3,1},{4,0},{5,7},{6,2},{7,5},{8,12},{9,11},{10,... | collective-permute-start | bytes 1572872 | tf_op jit(solution)/shard_map/ppermute | solution.py:77
  28.8 13.4 %collective-permute-start.5 = (bf16[4,128,512]{2,1,0:T(8,128)(2,1)S(1)}, bf16[4,128,512]{2,1,0:T(8,128)(2,1)}, u32[]{:S(2)}, u32[]{:S(2)}) collective-permute-start(bf16[4,128,512]{2,1,0:T(8,128)(2,1)S(1)} %collective-permute-done.3.refs_1_), channel_id=1, source_target_pairs={{0,4},{1,3},{2,6},{3,1},{4,0},{5,7},{6,2},{7,5},{8,12},{9,11},{10,... | collective-permute-start | bytes 1572872 | tf_op jit(solution)/shard_map/ppermute | solution.py:77
  31.5 10.7 %collective-permute-start.9 = (bf16[4,128,512]{2,1,0:T(8,128)(2,1)S(1)}, bf16[4,128,512]{2,1,0:T(8,128)(2,1)S(1)}, u32[]{:S(2)}, u32[]{:S(2)}) collective-permute-start(bf16[4,128,512]{2,1,0:T(8,128)(2,1)S(1)} %pad_maximum_fusion.6.refs_8_.refs_0_), channel_id=1, source_target_pairs={{0,1},{1,0},{2,3},{3,2},{4,5},{5,4},{6,7},{7,6},{8,9},{9,8},{10,11... | collective-permute-start | bytes 1572872 | tf_op jit(solution)/shard_map/ppermute | solution.py:68
  42.2 11.1 %collective-permute-start.15 = (bf16[128,1024]{1,0:T(8,128)(2,1)S(1)}, bf16[128,1024]{1,0:T(8,128)(2,1)S(1)}, u32[]{:S(2)}, u32[]{:S(2)}) collective-permute-start(bf16[128,1024]{1,0:T(8,128)(2,1)S(1)} %pad_maximum_fusion.10), channel_id=1, source_target_pairs={{24,0},{28,4},{0,8},{4,12},{8,16},{12,20},{16,24},{20,28},{25,1},{... | collective-permute-start | bytes 786440 | tf_op jit(solution)/shard_map/ppermute | solution.py:98
  42.2 21.7 %collective-permute-start.10 = (bf16[4,128,512]{2,1,0:T(8,128)(2,1)S(1)}, bf16[4,128,512]{2,1,0:T(8,128)(2,1)}, u32[]{:S(2)}, u32[]{:S(2)}) collective-permute-start(bf16[4,128,512]{2,1,0:T(8,128)(2,1)S(1)} %pad_maximum_fusion.6.refs_8_.refs_0_), channel_id=1, source_target_pairs={{0,4},{1,3},{2,6},{3,1},{4,0},{5,7},{6,2},{7,5},{8,12},{9,11},{10,... | collective-permute-start | bytes 1572872 | tf_op jit(solution)/shard_map/ppermute | solution.py:77
  43.7 20.1 %collective-permute-start.11 = (bf16[4,128,512]{2,1,0:T(8,128)(2,1)S(1)}, bf16[4,128,512]{2,1,0:T(8,128)(2,1)S(1)}, u32[]{:S(2)}, u32[]{:S(2)}) collective-permute-start(bf16[4,128,512]{2,1,0:T(8,128)(2,1)S(1)} %collective-permute-done.9.refs_9_.refs_1_), channel_id=1, source_target_pairs={{0,4},{1,3},{2,6},{3,1},{4,0},{5,7},{6,2},{7,5},{8,12},{9,11},{10,... | collective-permute-start | bytes 1572872 | tf_op jit(solution)/shard_map/ppermute | solution.py:77
  44.3 20.4 %collective-permute-start.12 = (bf16[4,128,512]{2,1,0:T(8,128)(2,1)}, bf16[4,128,512]{2,1,0:T(8,128)(2,1)S(1)}, u32[]{:S(2)}, u32[]{:S(2)}) collective-permute-start(bf16[4,128,512]{2,1,0:T(8,128)(2,1)} %collective-permute-done.4.refs_2_), channel_id=1, source_target_pairs={{0,2},{1,5},{2,0},{3,7},{4,6},{5,1},{6,4},{7,3},{8,10},{9,13},{10,... | collective-permute-start | bytes 1572872 | tf_op jit(solution)/shard_map/ppermute | solution.py:77
  45.8 16.2 %collective-permute-start.14 = (bf16[128,1024]{1,0:T(8,128)(2,1)S(1)}, bf16[128,1024]{1,0:T(8,128)(2,1)S(1)}, u32[]{:S(2)}, u32[]{:S(2)}) collective-permute-start(bf16[128,1024]{1,0:T(8,128)(2,1)S(1)} %pad_maximum_fusion.10), channel_id=1, source_target_pairs={{16,0},{20,4},{24,8},{28,12},{0,16},{4,20},{8,24},{12,28},{17,1},{... | collective-permute-start | bytes 786440 | tf_op jit(solution)/shard_map/ppermute | solution.py:98
  53.3 10.4 %collective-permute-start.13 = (bf16[128,1024]{1,0:T(8,128)(2,1)S(1)}, bf16[128,1024]{1,0:T(8,128)(2,1)S(1)}, u32[]{:S(2)}, u32[]{:S(2)}) collective-permute-start(bf16[128,1024]{1,0:T(8,128)(2,1)S(1)} %pad_maximum_fusion.10), channel_id=1, source_target_pairs={{8,0},{12,4},{16,8},{20,12},{24,16},{28,20},{0,24},{4,28},{9,1},{1... | collective-permute-start | bytes 786440 | tf_op jit(solution)/shard_map/ppermute | solution.py:98
  65.4 9.5 %collective-permute-start.20 = (bf16[4,128,1024]{2,1,0:T(8,128)(2,1)S(1)}, bf16[4,128,1024]{2,1,0:T(8,128)(2,1)S(1)}, u32[]{:S(2)}, u32[]{:S(2)}) collective-permute-start(bf16[4,128,1024]{2,1,0:T(8,128)(2,1)S(1)} %pad_maximum_fusion), channel_id=1, source_target_pairs={{0,1},{1,0},{2,3},{3,2},{4,5},{5,4},{6,7},{7,6},{8,9},{9,8},{10,11... | collective-permute-start | bytes 3145736 | tf_op jit(solution)/shard_map/ppermute | solution.py:68
  65.5 9.5 %collective-permute-start.19 = (bf16[4,128,512]{2,1,0:T(8,128)(2,1)}, bf16[4,128,512]{2,1,0:T(8,128)(2,1)}, u32[]{:S(2)}, u32[]{:S(2)}) collective-permute-start(bf16[4,128,512]{2,1,0:T(8,128)(2,1)} %collective-permute-done.10.refs_10_.refs_2_), channel_id=1, source_target_pairs={{0,2},{1,5},{2,0},{3,7},{4,6},{5,1},{6,4},{7,3},{8,10},{9,13},{10,... | collective-permute-start | bytes 1572872 | tf_op jit(solution)/shard_map/ppermute | solution.py:77
  67.0 8.5 %collective-permute-start.17 = (bf16[4,128,512]{2,1,0:T(8,128)(2,1)}, bf16[4,128,512]{2,1,0:T(8,128)(2,1)}, u32[]{:S(2)}, u32[]{:S(2)}) collective-permute-start(bf16[4,128,512]{2,1,0:T(8,128)(2,1)} %collective-permute-done.5.refs_3_), channel_id=1, source_target_pairs={{0,1},{1,0},{2,3},{3,2},{4,5},{5,4},{6,7},{7,6},{8,9},{9,8},{10,11... | collective-permute-start | bytes 1572872 | tf_op jit(solution)/shard_map/ppermute | solution.py:68
  67.2 10.6 %collective-permute-start.16 = (bf16[4,128,512]{2,1,0:T(8,128)(2,1)}, bf16[4,128,512]{2,1,0:T(8,128)(2,1)}, u32[]{:S(2)}, u32[]{:S(2)}) collective-permute-start(bf16[4,128,512]{2,1,0:T(8,128)(2,1)} %collective-permute-done.4.refs_2_), channel_id=1, source_target_pairs={{0,1},{1,0},{2,3},{3,2},{4,5},{5,4},{6,7},{7,6},{8,9},{9,8},{10,11... | collective-permute-start | bytes 1572872 | tf_op jit(solution)/shard_map/ppermute | solution.py:68
  67.5 10.5 %collective-permute-start.21 = (bf16[4,128,512]{2,1,0:T(8,128)(2,1)}, bf16[4,128,512]{2,1,0:T(8,128)(2,1)}, u32[]{:S(2)}, u32[]{:S(2)}) collective-permute-start(bf16[4,128,512]{2,1,0:T(8,128)(2,1)} %collective-permute-done.10.refs_10_.refs_2_), channel_id=1, source_target_pairs={{0,1},{1,0},{2,3},{3,2},{4,5},{5,4},{6,7},{7,6},{8,9},{9,8},{10,11... | collective-permute-start | bytes 1572872 | tf_op jit(solution)/shard_map/ppermute | solution.py:68
  68.8 32.1 %all-to-all-start = ((bf16[4,128,1024]{2,1,0:T(8,128)(2,1)}), bf16[4,128,1024]{2,1,0:T(8,128)(2,1)S(1)}, u32[]{:S(2)}, u32[]{:S(2)}) async-start(bf16[4,128,1024]{2,1,0:T(8,128)(2,1)} %broadcast_in_dim.11), calls=%async_computation | async-start | bytes 2097152 | tf_op jit(solution)/shard_map/all_to_all | solution.py:81
  75.0 2.8 collective-permute-start.18
  75.0 3.0 collective-permute-start.22
  75.9 2.8 collective-permute-start.23
  79.8 21.1 %collective-permute-start.24 = (bf16[8,128,512]{2,1,0:T(8,128)(2,1)}, bf16[8,128,512]{2,1,0:T(8,128)(2,1)}, u32[]{:S(2)}, u32[]{:S(2)}) collective-permute-start(bf16[8,128,512]{2,1,0:T(8,128)(2,1)} %pad_maximum_fusion.1), channel_id=1, source_target_pairs={{0,4},{1,3},{2,6},{3,1},{4,0},{5,7},{6,2},{7,5},{8,12},{9,11},{10,... | collective-permute-start | bytes 3145736 | tf_op jit(solution)/shard_map/ppermute | solution.py:77
  101.9 24.6 %collective-permute-start.28 = (bf16[8,128,512]{2,1,0:T(8,128)(2,1)}, bf16[8,128,512]{2,1,0:T(8,128)(2,1)}, u32[]{:S(2)}, u32[]{:S(2)}) collective-permute-start(bf16[8,128,512]{2,1,0:T(8,128)(2,1)} %collective-permute-done.24.refs_2_), channel_id=1, source_target_pairs={{0,1},{1,0},{2,3},{3,2},{4,5},{5,4},{6,7},{7,6},{8,9},{9,8},{10,11... | collective-permute-start | bytes 3145736 | tf_op jit(solution)/shard_map/ppermute | solution.py:68
  102.0 22.0 %collective-permute-start.25 = (bf16[4,128,512]{2,1,0:T(8,128)(2,1)S(1)}, bf16[4,128,512]{2,1,0:T(8,128)(2,1)}, u32[]{:S(2)}, u32[]{:S(2)}) collective-permute-start(bf16[4,128,512]{2,1,0:T(8,128)(2,1)S(1)} %slice.212), channel_id=1, source_target_pairs={{0,2},{1,5},{2,0},{3,7},{4,6},{5,1},{6,4},{7,3},{8,10},{9,13},{10,... | collective-permute-start | bytes 1572872 | tf_op jit(solution)/shard_map/ppermute | solution.py:77
  104.4 19.6 %collective-permute-start.26 = (bf16[8,128,512]{2,1,0:T(8,128)(2,1)}, bf16[8,128,512]{2,1,0:T(8,128)(2,1)}, u32[]{:S(2)}, u32[]{:S(2)}) collective-permute-start(bf16[8,128,512]{2,1,0:T(8,128)(2,1)} %pad_maximum_fusion.2), channel_id=1, source_target_pairs={{0,4},{1,3},{2,6},{3,1},{4,0},{5,7},{6,2},{7,5},{8,12},{9,11},{10,... | collective-permute-start | bytes 3145736 | tf_op jit(solution)/shard_map/ppermute | solution.py:77
  105.2 18.7 %collective-permute-start.27 = (bf16[4,128,1024]{2,1,0:T(8,128)(2,1)S(1)}, bf16[4,128,1024]{2,1,0:T(8,128)(2,1)S(1)}, u32[]{:S(2)}, u32[]{:S(2)}) collective-permute-start(bf16[4,128,1024]{2,1,0:T(8,128)(2,1)S(1)} %all-to-all-done), channel_id=1, source_target_pairs={{0,1},{1,0},{2,3},{3,2},{4,5},{5,4},{6,7},{7,6},{8,9},{9,8},{10,11... | collective-permute-start | bytes 3145736 | tf_op jit(solution)/shard_map/ppermute | solution.py:68
  124.0 2.5 collective-permute-start.29
  127.8 22.8 %collective-permute-start.32 = (bf16[8,128,512]{2,1,0:T(8,128)(2,1)}, bf16[8,128,512]{2,1,0:T(8,128)(2,1)}, u32[]{:S(2)}, u32[]{:S(2)}) collective-permute-start(bf16[8,128,512]{2,1,0:T(8,128)(2,1)} %collective-permute-done.26.refs_2_), channel_id=1, source_target_pairs={{0,1},{1,0},{2,3},{3,2},{4,5},{5,4},{6,7},{7,6},{8,9},{9,8},{10,11... | collective-permute-start | bytes 3145736 | tf_op jit(solution)/shard_map/ppermute | solution.py:68
  128.2 22.3 %collective-permute-start.30 = (bf16[4,128,512]{2,1,0:T(8,128)(2,1)S(1)}, bf16[4,128,512]{2,1,0:T(8,128)(2,1)}, u32[]{:S(2)}, u32[]{:S(2)}) collective-permute-start(bf16[4,128,512]{2,1,0:T(8,128)(2,1)S(1)} %slice.217), channel_id=1, source_target_pairs={{0,2},{1,5},{2,0},{3,7},{4,6},{5,1},{6,4},{7,3},{8,10},{9,13},{10,... | collective-permute-start | bytes 1572872 | tf_op jit(solution)/shard_map/ppermute | solution.py:77
  129.9 20.7 %collective-permute-start.31 = (bf16[8,128,512]{2,1,0:T(8,128)(2,1)S(1)}, bf16[8,128,512]{2,1,0:T(8,128)(2,1)}, u32[]{:S(2)}, u32[]{:S(2)}) collective-permute-start(bf16[8,128,512]{2,1,0:T(8,128)(2,1)S(1)} %pad_maximum_fusion.3), channel_id=1, source_target_pairs={{0,4},{1,3},{2,6},{3,1},{4,0},{5,7},{6,2},{7,5},{8,12},{9,11},{10,... | collective-permute-start | bytes 3145736 | tf_op jit(solution)/shard_map/ppermute | solution.py:77
  154.0 22.4 %collective-permute-start.36 = (bf16[8,128,512]{2,1,0:T(8,128)(2,1)}, bf16[8,128,512]{2,1,0:T(8,128)(2,1)}, u32[]{:S(2)}, u32[]{:S(2)}) collective-permute-start(bf16[8,128,512]{2,1,0:T(8,128)(2,1)} %collective-permute-done.31.refs_2_), channel_id=1, source_target_pairs={{0,1},{1,0},{2,3},{3,2},{4,5},{5,4},{6,7},{7,6},{8,9},{9,8},{10,11... | collective-permute-start | bytes 3145736 | tf_op jit(solution)/shard_map/ppermute | solution.py:68
  154.2 22.1 %collective-permute-start.34 = (bf16[4,128,512]{2,1,0:T(8,128)(2,1)S(1)}, bf16[4,128,512]{2,1,0:T(8,128)(2,1)S(1)}, u32[]{:S(2)}, u32[]{:S(2)}) collective-permute-start(bf16[4,128,512]{2,1,0:T(8,128)(2,1)S(1)} %slice.218), channel_id=1, source_target_pairs={{0,2},{1,5},{2,0},{3,7},{4,6},{5,1},{6,4},{7,3},{8,10},{9,13},{10,... | collective-permute-start | bytes 1572872 | tf_op jit(solution)/shard_map/ppermute | solution.py:77
  155.5 20.8 %collective-permute-start.35 = (bf16[8,128,512]{2,1,0:T(8,128)(2,1)S(1)}, bf16[8,128,512]{2,1,0:T(8,128)(2,1)S(1)}, u32[]{:S(2)}, u32[]{:S(2)}) collective-permute-start(bf16[8,128,512]{2,1,0:T(8,128)(2,1)S(1)} %pad_maximum_fusion.4), channel_id=1, source_target_pairs={{0,4},{1,3},{2,6},{3,1},{4,0},{5,7},{6,2},{7,5},{8,12},{9,11},{10,... | collective-permute-start | bytes 3145736 | tf_op jit(solution)/shard_map/ppermute | solution.py:77
  179.1 22.2 %collective-permute-start.39 = (bf16[16,128,1024]{2,1,0:T(8,128)(2,1)}, bf16[16,128,1024]{2,1,0:T(8,128)(2,1)}, u32[]{:S(2)}, u32[]{:S(2)}) collective-permute-start(bf16[16,128,1024]{2,1,0:T(8,128)(2,1)} %get-tuple-element.305), channel_id=1, source_target_pairs={{0,1},{1,0},{2,3},{3,2},{4,5},{5,4},{6,7},{7,6},{8,9},{9,8},{10,11... | collective-permute-start | bytes 12582920 | tf_op jit(solution)/shard_map/ppermute | solution.py:68
  179.3 22.1 %collective-permute-start.40 = (bf16[8,128,512]{2,1,0:T(8,128)(2,1)S(1)}, bf16[8,128,512]{2,1,0:T(8,128)(2,1)S(1)}, u32[]{:S(2)}, u32[]{:S(2)}) collective-permute-start(bf16[8,128,512]{2,1,0:T(8,128)(2,1)S(1)} %collective-permute-done.35.refs_2_), channel_id=1, source_target_pairs={{0,1},{1,0},{2,3},{3,2},{4,5},{5,4},{6,7},{7,6},{8,9},{9,8},{10,11... | collective-permute-start | bytes 3145736 | tf_op jit(solution)/shard_map/ppermute | solution.py:68
  179.7 21.6 %collective-permute-start.38 = (bf16[4,128,512]{2,1,0:T(8,128)(2,1)S(1)}, bf16[4,128,512]{2,1,0:T(8,128)(2,1)S(1)}, u32[]{:S(2)}, u32[]{:S(2)}) collective-permute-start(bf16[4,128,512]{2,1,0:T(8,128)(2,1)S(1)} %slice.219), channel_id=1, source_target_pairs={{0,2},{1,5},{2,0},{3,7},{4,6},{5,1},{6,4},{7,3},{8,10},{9,13},{10,... | collective-permute-start | bytes 1572872 | tf_op jit(solution)/shard_map/ppermute | solution.py:77
  205.4 20.9 %collective-permute-start.42 = (bf16[4,128,1024]{2,1,0:T(8,128)(2,1)S(1)}, bf16[4,128,1024]{2,1,0:T(8,128)(2,1)S(1)}, u32[]{:S(2)}, u32[]{:S(2)}) collective-permute-start(bf16[4,128,1024]{2,1,0:T(8,128)(2,1)S(1)} %add_convert_fusion.7), channel_id=1, source_target_pairs={{0,2},{1,5},{2,0},{3,7},{4,6},{5,1},{6,4},{7,3},{8,10},{9,13},{10,... | collective-permute-start | bytes 3145736 | tf_op jit(solution)/shard_map/ppermute | solution.py:77
  226.3 29.6 %collective-permute-start.45 = (bf16[16,128,1024]{2,1,0:T(8,128)(2,1)}, bf16[16,128,1024]{2,1,0:T(8,128)(2,1)}, u32[]{:S(2)}, u32[]{:S(2)}) collective-permute-start(bf16[16,128,1024]{2,1,0:T(8,128)(2,1)} %get-tuple-element.332), channel_id=1, source_target_pairs={{0,1},{1,0},{2,3},{3,2},{4,5},{5,4},{6,7},{7,6},{8,9},{9,8},{10,11... | collective-permute-start | bytes 12582920 | tf_op jit(solution)/shard_map/ppermute | solution.py:68
  229.8 21.0 %collective-permute-start.44 = (bf16[4,128,1024]{2,1,0:T(8,128)(2,1)S(1)}, bf16[4,128,1024]{2,1,0:T(8,128)(2,1)}, u32[]{:S(2)}, u32[]{:S(2)}) collective-permute-start(bf16[4,128,1024]{2,1,0:T(8,128)(2,1)S(1)} %get-tuple-element.421), channel_id=1, source_target_pairs={{0,4},{1,3},{2,6},{3,1},{4,0},{5,7},{6,2},{7,5},{8,12},{9,11},{10,... | collective-permute-start | bytes 3145736 | tf_op jit(solution)/shard_map/ppermute | solution.py:77
  231.2 24.7 %collective-permute-start.43 = (bf16[4,128,1024]{2,1,0:T(8,128)(2,1)S(1)}, bf16[4,128,1024]{2,1,0:T(8,128)(2,1)S(1)}, u32[]{:S(2)}, u32[]{:S(2)}) collective-permute-start(bf16[4,128,1024]{2,1,0:T(8,128)(2,1)S(1)} %get-tuple-element.422), channel_id=1, source_target_pairs={{0,4},{1,3},{2,6},{3,1},{4,0},{5,7},{6,2},{7,5},{8,12},{9,11},{10,... | collective-permute-start | bytes 3145736 | tf_op jit(solution)/shard_map/ppermute | solution.py:77
  258.9 15.6 %collective-permute-start.46 = (bf16[4,128,1024]{2,1,0:T(8,128)(2,1)}, bf16[4,128,1024]{2,1,0:T(8,128)(2,1)S(1)}, u32[]{:S(2)}, u32[]{:S(2)}) collective-permute-start(bf16[4,128,1024]{2,1,0:T(8,128)(2,1)} %add_convert_fusion.4), channel_id=1, source_target_pairs={{0,2},{1,5},{2,0},{3,7},{4,6},{5,1},{6,4},{7,3},{8,10},{9,13},{10,... | collective-permute-start | bytes 3145736 | tf_op jit(solution)/shard_map/ppermute | solution.py:77
  260.4 14.0 %collective-permute-start.47 = (bf16[4,128,1024]{2,1,0:T(8,128)(2,1)}, bf16[4,128,1024]{2,1,0:T(8,128)(2,1)S(1)}, u32[]{:S(2)}, u32[]{:S(2)}) collective-permute-start(bf16[4,128,1024]{2,1,0:T(8,128)(2,1)} %collective-permute-done.44), channel_id=1, source_target_pairs={{0,1},{1,0},{2,3},{3,2},{4,5},{5,4},{6,7},{7,6},{8,9},{9,8},{10,11... | collective-permute-start | bytes 3145736 | tf_op jit(solution)/shard_map/ppermute | solution.py:68
  277.9 34.5 %all-to-all-start.1 = ((bf16[4,128,1024]{2,1,0:T(8,128)(2,1)}), bf16[4,128,1024]{2,1,0:T(8,128)(2,1)S(1)}, u32[]{:S(2)}, u32[]{:S(2)}) async-start(bf16[4,128,1024]{2,1,0:T(8,128)(2,1)} %add_convert_fusion.1), calls=%async_computation.1 | async-start | bytes 2097152 | tf_op jit(solution)/shard_map/all_to_all | solution.py:81
  285.8 25.7 %collective-permute-start.49 = (bf16[4,128,1024]{2,1,0:T(8,128)(2,1)}, bf16[4,128,1024]{2,1,0:T(8,128)(2,1)S(1)}, u32[]{:S(2)}, u32[]{:S(2)}) collective-permute-start(bf16[4,128,1024]{2,1,0:T(8,128)(2,1)} %get-tuple-element.419), channel_id=1, source_target_pairs={{0,4},{1,3},{2,6},{3,1},{4,0},{5,7},{6,2},{7,5},{8,12},{9,11},{10,... | collective-permute-start | bytes 3145736 | tf_op jit(solution)/shard_map/ppermute | solution.py:77
  286.6 25.8 %collective-permute-start.48 = (bf16[4,128,1024]{2,1,0:T(8,128)(2,1)S(1)}, bf16[4,128,1024]{2,1,0:T(8,128)(2,1)}, u32[]{:S(2)}, u32[]{:S(2)}) collective-permute-start(bf16[4,128,1024]{2,1,0:T(8,128)(2,1)S(1)} %get-tuple-element.420), channel_id=1, source_target_pairs={{0,4},{1,3},{2,6},{3,1},{4,0},{5,7},{6,2},{7,5},{8,12},{9,11},{10,... | collective-permute-start | bytes 3145736 | tf_op jit(solution)/shard_map/ppermute | solution.py:77
  312.4 6.9 %collective-permute-start.50 = (bf16[16,128,512]{2,1,0:T(8,128)(2,1)}, bf16[16,128,512]{2,1,0:T(8,128)(2,1)S(1)}, u32[]{:S(2)}, u32[]{:S(2)}) collective-permute-start(bf16[16,128,512]{2,1,0:T(8,128)(2,1)} %get-tuple-element.352), channel_id=1, source_target_pairs={{0,1},{1,0},{2,3},{3,2},{4,5},{5,4},{6,7},{7,6},{8,9},{9,8},{10,11... | collective-permute-start | bytes 6291464 | tf_op jit(solution)/shard_map/ppermute | solution.py:68
  312.4 6.9 %collective-permute-start.51 = (bf16[4,128,1024]{2,1,0:T(8,128)(2,1)}, bf16[4,128,1024]{2,1,0:T(8,128)(2,1)}, u32[]{:S(2)}, u32[]{:S(2)}) collective-permute-start(bf16[4,128,1024]{2,1,0:T(8,128)(2,1)} %copy-done.41), channel_id=1, source_target_pairs={{0,1},{1,0},{2,3},{3,2},{4,5},{5,4},{6,7},{7,6},{8,9},{9,8},{10,11... | collective-permute-start | bytes 3145736 | tf_op jit(solution)/shard_map/ppermute | solution.py:68
  319.3 13.6 %collective-permute-start.53 = (bf16[16,128,512]{2,1,0:T(8,128)(2,1)}, bf16[16,128,512]{2,1,0:T(8,128)(2,1)}, u32[]{:S(2)}, u32[]{:S(2)}) collective-permute-start(bf16[16,128,512]{2,1,0:T(8,128)(2,1)} %get-tuple-element.366), channel_id=1, source_target_pairs={{0,1},{1,0},{2,3},{3,2},{4,5},{5,4},{6,7},{7,6},{8,9},{9,8},{10,11... | collective-permute-start | bytes 6291464 | tf_op jit(solution)/shard_map/ppermute | solution.py:68
  322.6 10.3 %collective-permute-start.52 = (bf16[4,128,512]{2,1,0:T(8,128)(2,1)}, bf16[4,128,512]{2,1,0:T(8,128)(2,1)}, u32[]{:S(2)}, u32[]{:S(2)}) collective-permute-start(bf16[4,128,512]{2,1,0:T(8,128)(2,1)} %add_convert_fusion.15), channel_id=1, source_target_pairs={{0,2},{1,5},{2,0},{3,7},{4,6},{5,1},{6,4},{7,3},{8,10},{9,13},{10,... | collective-permute-start | bytes 1572872 | tf_op jit(solution)/shard_map/ppermute | solution.py:77
  327.6 30.9 %all-to-all-start.2 = ((bf16[4,128,1024]{2,1,0:T(8,128)(2,1)}), bf16[4,128,1024]{2,1,0:T(8,128)(2,1)}, u32[]{:S(2)}, u32[]{:S(2)}) async-start(bf16[4,128,1024]{2,1,0:T(8,128)(2,1)} %add_convert_fusion), calls=%async_computation.2 | async-start | bytes 2097152 | tf_op jit(solution)/shard_map/all_to_all | solution.py:81
  336.1 22.4 %collective-permute-start.55 = (bf16[4,128,512]{2,1,0:T(8,128)(2,1)}, bf16[4,128,512]{2,1,0:T(8,128)(2,1)}, u32[]{:S(2)}, u32[]{:S(2)}) collective-permute-start(bf16[4,128,512]{2,1,0:T(8,128)(2,1)} %get-tuple-element.425), channel_id=1, source_target_pairs={{0,4},{1,3},{2,6},{3,1},{4,0},{5,7},{6,2},{7,5},{8,12},{9,11},{10,... | collective-permute-start | bytes 1572872 | tf_op jit(solution)/shard_map/ppermute | solution.py:77
  337.0 21.5 %collective-permute-start.54 = (bf16[4,128,512]{2,1,0:T(8,128)(2,1)}, bf16[4,128,512]{2,1,0:T(8,128)(2,1)}, u32[]{:S(2)}, u32[]{:S(2)}) collective-permute-start(bf16[4,128,512]{2,1,0:T(8,128)(2,1)} %get-tuple-element.426), channel_id=1, source_target_pairs={{0,4},{1,3},{2,6},{3,1},{4,0},{5,7},{6,2},{7,5},{8,12},{9,11},{10,... | collective-permute-start | bytes 1572872 | tf_op jit(solution)/shard_map/ppermute | solution.py:77
  340.5 18.0 %collective-permute-start.56 = (bf16[4,128,512]{2,1,0:T(8,128)(2,1)}, bf16[4,128,512]{2,1,0:T(8,128)(2,1)}, u32[]{:S(2)}, u32[]{:S(2)}) collective-permute-start(bf16[4,128,512]{2,1,0:T(8,128)(2,1)} %get-tuple-element.424), channel_id=1, source_target_pairs={{0,2},{1,5},{2,0},{3,7},{4,6},{5,1},{6,4},{7,3},{8,10},{9,13},{10,... | collective-permute-start | bytes 1572872 | tf_op jit(solution)/shard_map/ppermute | solution.py:77
  358.6 16.8 %collective-permute-start.58 = (bf16[4,128,512]{2,1,0:T(8,128)(2,1)}, bf16[4,128,512]{2,1,0:T(8,128)(2,1)}, u32[]{:S(2)}, u32[]{:S(2)}) collective-permute-start(bf16[4,128,512]{2,1,0:T(8,128)(2,1)} %get-tuple-element.423), channel_id=1, source_target_pairs={{0,4},{1,3},{2,6},{3,1},{4,0},{5,7},{6,2},{7,5},{8,12},{9,11},{10,... | collective-permute-start | bytes 1572872 | tf_op jit(solution)/shard_map/ppermute | solution.py:77
  363.1 19.4 %all-to-all-start.3 = ((bf16[4,128,512]{2,1,0:T(8,128)(2,1)}), bf16[4,128,512]{2,1,0:T(8,128)(2,1)}, u32[]{:S(2)}, u32[]{:S(2)}) async-start(bf16[4,128,512]{2,1,0:T(8,128)(2,1)} %add_convert_fusion.9), calls=%async_computation.3 | async-start | bytes 1048576 | tf_op jit(solution)/shard_map/all_to_all | solution.py:81
  368.8 9.4 %collective-permute-start.57 = (bf16[4,128,512]{2,1,0:T(8,128)(2,1)S(1)}, bf16[4,128,512]{2,1,0:T(8,128)(2,1)}, u32[]{:S(2)}, u32[]{:S(2)}) collective-permute-start(bf16[4,128,512]{2,1,0:T(8,128)(2,1)S(1)} %add_convert_fusion.11), channel_id=1, source_target_pairs={{0,4},{1,3},{2,6},{3,1},{4,0},{5,7},{6,2},{7,5},{8,12},{9,11},{10,... | collective-permute-start | bytes 1572872 | tf_op jit(solution)/shard_map/ppermute | solution.py:77
  371.4 4.0 collective-permute-start.61
  386.9 21.1 %all-to-all-start.4 = ((bf16[4,128,512]{2,1,0:T(8,128)(2,1)}), bf16[4,128,512]{2,1,0:T(8,128)(2,1)S(1)}, u32[]{:S(2)}, u32[]{:S(2)}) async-start(bf16[4,128,512]{2,1,0:T(8,128)(2,1)} %add_convert_fusion.8), calls=%async_computation.4 | async-start | bytes 1048576 | tf_op jit(solution)/shard_map/all_to_all | solution.py:81
  392.1 6.1 %collective-permute-start.63 = (f32[4,1024]{1,0:T(4,128)S(1)}, f32[4,1024]{1,0:T(4,128)}, u32[]{:S(2)}, u32[]{:S(2)}) collective-permute-start(f32[4,1024]{1,0:T(4,128)S(1)} %add.200), channel_id=1, source_target_pairs={{0,4},{4,0},{8,12},{12,8},{16,20},{20,16},{24,28},{28,24},{1,5},{5... | collective-permute-start | bytes 49160 | tf_op jit(solution)/shard_map/ppermute | solution.py:87
  399.0 3.7 collective-permute-start.64
  402.7 4.7 %collective-permute-start.65 = (f32[4,1024]{1,0:T(4,128)S(1)}, f32[4,1024]{1,0:T(4,128)S(1)}, u32[]{:S(2)}, u32[]{:S(2)}) collective-permute-start(f32[4,1024]{1,0:T(4,128)S(1)} %add.225), channel_id=1, source_target_pairs={{0,16},{4,20},{8,24},{12,28},{16,0},{20,4},{24,8},{28,12},{1,17},{... | collective-permute-start | bytes 49160 | tf_op jit(solution)/shard_map/ppermute | solution.py:87
  (56 other events, 495.7 us)

commit v3 on v2

--- a/solution.py
+++ b/solution.py
@@ -208,7 +208,9 @@
     pairs = []
     for i, place, (row, column) in grid.gathered_places(turned, len(refs) == 6):
         source = refs[i].at[place, :, pl.ds(lane, lanes)]
-        pairs.append((source, block(target, row * rows, rows, column * across + offset, lanes)))
+        start = pl.multiple_of(column * across + offset, math.gcd(across, offset, lanes))
+        held = pl.ds(pl.multiple_of(row * rows, rows), rows)
+        pairs.append((source, target.at[held, pl.ds(start, lanes)]))
     return pairs
 
 
@@ -740,11 +742,13 @@
     q1_over = grid.gather_xy(q1)
     q0_far = grid.gather_far(q0_over)
     m01 = grid.gather_z(piece)
-    q1_over, q0_far, m01, piece = tie(q1_over, q0_far, m01, large(2, 3))
+    q1_over, q0_far, m01, piece, seg_column = tie(
+        q1_over, q0_far, m01, grid.copies(large(2, 3)), seg_column
+    )
     q0_pieces = grid.gather_end(q0, q0_over, q0_far)
     q1_far = grid.gather_far(q1_over)
     m01 = grid.both(m01)
-    m23 = grid.z_exchange(grid.copies(piece))
+    m23 = grid.z_exchange(piece)
     q1_far, m01 = tie(q1_far, m01)
     q1_pieces = grid.gather_end(q1, q1_over, q1_far)
 

time: 416 us -> 414 us (level)
  transfers between devices with their start and end apart: 71 -> 71, of which waited for: 26 -> 26; matrix products, arithmetic and copies ran while one was open for 10% -> 10% of each run, Pallas kernels for 46% -> 47%
where the time goes in v3:
time: 414 us; the launch traced here: 409 us
  Pallas kernels  191 us (46%)
  starting transfers between devices  77.5 us (19%)
  waiting for transfers between devices  73.6 us (18%)
  other arithmetic  49.4 us (12%)
  local copies, waits for them, and re-layouts  14.5 us (4%)
    pallas_call x4, Pallas kernels, feed_forward(): pl.pallas_call(kernel, out_shape=(shape_of((count, width), F32),) * 2 + (...  80.3 us
    convert_element_type x19, other arithmetic, thin(): return values.astype(BF16)  40.6 us
    ppermute x26, starting transfers between devices, cross(): return lax.ppermute(values, ('dp', 'shard'), pairs)  29.4 us
    pallas_call x2, Pallas kernels, attention_back(): pl.pallas_call(kernel, grid=(blocks,), out_shape=shape_of((count, 3 * wid...  27.8 us
    ppermute x9, waiting for transfers between devices, gather_z(): parts.append(lax.ppermute(piece, 'dp', shift))  27.7 us
    all_to_all x5, starting transfers between devices, z_exchange(): lax.all_to_all(values, 'dp', 0, 0, axis_index_groups=groups, tiled=True)  22.4 us
    pallas_call x3, Pallas kernels, weight_grad(): pl.pallas_call(kernel, out_shape=(region, region), in_specs=[SCALAR] + [A...  22.4 us
    ppermute x26, waiting for transfers between devices, cross(): return lax.ppermute(values, ('dp', 'shard'), pairs)  19.9 us
  transfers between devices with their start and end apart: 71, of which 26 were waited for; matrix products, arithmetic and copies ran while one was open for 10% of the time, Pallas kernels for 47%

profile of v3, /device:TPU:0, one launch (start us, length us, event | category | flops | bytes accessed | tf_op | source)
XLA Modules:
  0.0 409.1 jit_solution(6772055983521761480)
XLA Ops:
  1.8 4.1 %collective-permute-start.1 = (bf16[128,512]{1,0:T(8,128)(2,1)S(1)}, bf16[128,512]{1,0:T(8,128)(2,1)S(1)}, u32[]{:S(2)}, u32[]{:S(2)}) collective-permute-start(bf16[128,512]{1,0:T(8,128)(2,1)S(1)} %get-tuple-element.451), channel_id=1, source_target_pairs={{16,0},{20,4},{24,8},{28,12},{0,16},{4,20},{8,24},{12,28},{17,1},{... | collective-permute-start | bytes 393224 | tf_op jit(solution)/shard_map/ppermute | solution.py:98
  8.0 5.9 %collective-permute-done.1 = bf16[128,512]{1,0:T(8,128)(2,1)S(1)} collective-permute-done((bf16[128,512]{1,0:T(8,128)(2,1)S(1)}, bf16[128,512]{1,0:T(8,128)(2,1)S(1)}, u32[]{:S(2)}, u32[]{:S(2)}) %collective-permute-start.1) | collective-permute-done | bytes 131104 | tf_op jit(solution)/shard_map/ppermute | solution.py:98
  13.9 2.4 collective-permute-done.2
  16.8 1.6 collective-permute-done.3.refs_1_
  18.3 2.4 collective-permute-start.8
  20.7 1.9 collective-permute-start.7
  22.6 2.9 collective-permute-start.6
  25.5 1.7 slice_reduce_fusion.1
  27.2 1.6 collective-permute-start.4
  29.3 2.1 collective-permute-done.7
  31.6 4.9 %collective-permute-done.4.refs_2_ = bf16[4,128,512]{2,1,0:T(8,128)(2,1)} collective-permute-done((bf16[4,128,512]{2,1,0:T(8,128)(2,1)S(1)}, bf16[4,128,512]{2,1,0:T(8,128)(2,1)}, u32[]{:S(2)}, u32[]{:S(2)}) %collective-permute-start.4) | collective-permute-done | bytes 524320 | tf_op jit(solution)/shard_map/ppermute | solution.py:77
  36.6 5.6 %collective-permute-done.5.refs_3_ = bf16[4,128,512]{2,1,0:T(8,128)(2,1)} collective-permute-done((bf16[4,128,512]{2,1,0:T(8,128)(2,1)S(1)}, bf16[4,128,512]{2,1,0:T(8,128)(2,1)}, u32[]{:S(2)}, u32[]{:S(2)}) %collective-permute-start.5) | collective-permute-done | bytes 524320 | tf_op jit(solution)/shard_map/ppermute | solution.py:77
  42.2 1.6 collective-permute-start.10
  44.3 1.5 collective-permute-start.12
  46.3 7.0 %collective-permute-done.15 = bf16[128,1024]{1,0:T(8,128)(2,1)S(1)} collective-permute-done((bf16[128,1024]{1,0:T(8,128)(2,1)S(1)}, bf16[128,1024]{1,0:T(8,128)(2,1)S(1)}, u32[]{:S(2)}, u32[]{:S(2)}) %collective-permute-start.15) | collective-permute-done | bytes 262176 | tf_op jit(solution)/shard_map/ppermute | solution.py:98
  53.4 8.6 %collective-permute-done.14 = bf16[128,1024]{1,0:T(8,128)(2,1)S(1)} collective-permute-done((bf16[128,1024]{1,0:T(8,128)(2,1)S(1)}, bf16[128,1024]{1,0:T(8,128)(2,1)S(1)}, u32[]{:S(2)}, u32[]{:S(2)}) %collective-permute-start.14) | collective-permute-done | bytes 262176 | tf_op jit(solution)/shard_map/ppermute | solution.py:98
  62.0 1.7 collective-permute-done.13
  65.1 1.6 collective-permute-start.19
  67.4 5.9 %all-to-all-start = ((bf16[4,128,1024]{2,1,0:T(8,128)(2,1)}), bf16[4,128,1024]{2,1,0:T(8,128)(2,1)S(1)}, u32[]{:S(2)}, u32[]{:S(2)}) async-start(bf16[4,128,1024]{2,1,0:T(8,128)(2,1)} %broadcast_in_dim.11), calls=%async_computation | async-start | bytes 2097152 | tf_op jit(solution)/shard_map/all_to_all | solution.py:81
  82.0 14.4 %shard_map.386 = (bf16[1024,1024]{1,0:T(8,128)(2,1)}, bf16[1024,3072]{1,0:T(8,128)(2,1)}, bf16[1024,3072]{1,0:T(8,128)(2,1)}) custom-call(bf16[1024,1024]{1,0:T(8,128)(2,1)} %refs_3_.1, f32[4,1024]{1,0:T(4,128)} %refs_4_.1, bf16[4,128,512]{2,1,0:T(8,128)(2,1)} %copy-done.24, bf16[4,128,512]{2,1,0:T(8,128)(2,1)} %copy-done.42, ...), custom_call_target="tpu_custom_call" | custom-call | flops 6442450944 | bytes 25165824 | tf_op jit(solution)/shard_map/pallas_call | solution.py:288
  96.4 3.1 all-to-all-done
  103.8 18.6 %shard_map.387 = (bf16[1024,1024]{1,0:T(8,128)(2,1)}, f32[4,16,256]{2,1,0:T(8,128)}, f32[1024,1024]{1,0:T(8,128)}, bf16[1024,1024]{1,0:T(8,128)(2,1)}, bf16[1024,1024]{1,0:T(8,128)(2,1)}) custom-call(bf16[1024,3072]{1,0:T(8,128)(2,1)} %get-tuple-element.244.j_ref, s32[1024,1]{1,0:T(8,128)} %copy.66.sc_ref, s32[4,1,256]{2,1,0:T(1,128)} %bitcast.43, ...), custom_call_target="tpu_custom_call" | custom-call | flops 8589934592 | bytes 20971520 | tf_op jit(solution)/shard_map/pallas_call | solution.py:361
  126.9 1.5 collective-permute-start.30
  129.1 20.0 %shard_map.388 = (f32[1024,1024]{1,0:T(8,128)}, f32[1024,1024]{1,0:T(8,128)}, bf16[16,128,1024]{2,1,0:T(8,128)(2,1)}, bf16[16,128,1024]{2,1,0:T(8,128)(2,1)}) custom-call(f32[1,1]{1,0:T(1,128)} %bitcast.f_ref, bf16[1024,1024]{1,0:T(8,128)(2,1)} %get-tuple-element.256.s_hbm, bf16[1024,1024]{1,0:T(8,128)(2,1)} %get-tuple-element.257.st_hbm, ...), custom_call_target="tpu_custom_call" | custom-call | flops 12884901888 | bytes 31457280 | tf_op jit(solution)/shard_map/pallas_call | solution.py:461
  149.3 2.2 collective-permute-done.33.refs_5_
  155.0 19.9 %shard_map.389 = (f32[1024,1024]{1,0:T(8,128)}, f32[1024,1024]{1,0:T(8,128)}, bf16[16,128,1024]{2,1,0:T(8,128)(2,1)}, bf16[16,128,1024]{2,1,0:T(8,128)(2,1)}) custom-call(f32[1,1]{1,0:T(1,128)} %bitcast.f_ref, bf16[1024,1024]{1,0:T(8,128)(2,1)} %get-tuple-element.256.s_hbm, ...), custom_call_target="tpu_custom_call", output_to_operand_aliasing={{0}: (10, {}), {1}: (11, {}), {2}: (12, {}), {3}: (13, {})} | custom-call | flops 12884901888 | bytes 31457280 | tf_op jit(solution)/shard_map/pallas_call | solution.py:461
  175.0 1.9 collective-permute-done.37.refs_5_
  178.3 1.5 collective-permute-start.38
  179.9 20.0 %shard_map.390 = (f32[1024,1024]{1,0:T(8,128)}, f32[1024,1024]{1,0:T(8,128)}, bf16[16,128,1024]{2,1,0:T(8,128)(2,1)}, bf16[16,128,1024]{2,1,0:T(8,128)(2,1)}) custom-call(f32[1,1]{1,0:T(1,128)} %bitcast.f_ref, bf16[1024,1024]{1,0:T(8,128)(2,1)} %get-tuple-element.256.s_hbm, ...), custom_call_target="tpu_custom_call", output_to_operand_aliasing={{0}: (10, {}), {1}: (11, {})} | custom-call | flops 12884901888 | bytes 31457280 | tf_op jit(solution)/shard_map/pallas_call | solution.py:461
  200.0 1.9 collective-permute-done.41.refs_5_
  201.9 2.1 add_convert_fusion.7
  204.7 20.3 %shard_map.391 = (f32[1024,1024]{1,0:T(8,128)}, f32[1024,1024]{1,0:T(8,128)}, bf16[16,128,1024]{2,1,0:T(8,128)(2,1)}, bf16[16,128,1024]{2,1,0:T(8,128)(2,1)}) custom-call(f32[1,1]{1,0:T(1,128)} %bitcast.f_ref, bf16[1024,1024]{1,0:T(8,128)(2,1)} %get-tuple-element.256.s_hbm, ...), custom_call_target="tpu_custom_call", output_to_operand_aliasing={{0}: (10, {}), {1}: (11, {}), {2}: (12, {}), {3}: (13, {})} | custom-call | flops 12884901888 | bytes 31457280 | tf_op jit(solution)/shard_map/pallas_call | solution.py:461
  225.0 3.4 add_convert_fusion.5
  230.6 12.7 %shard_map.392 = (bf16[1024,1024]{1,0:T(8,128)(2,1)}, f32[1024,1024]{1,0:T(8,128)}, bf16[1024,1024]{1,0:T(8,128)(2,1)}, bf16[1024,1024]{1,0:T(8,128)(2,1)}, f32[2,1024]{1,0:T(2,128)}) custom-call(f32[1024,1024]{1,0:T(8,128)} %get-tuple-element.328.o_ref, f32[1024,1024]{1,0:T(8,128)} %get-tuple-element.329.b_ref, f32[1024,1024]{1,0:T(8,128)} %get-tuple-element.330.res_ref, ...), custom_call_target="tpu_custom_call" | custom-call | flops 2147483648 | bytes 25165824 | tf_op jit(solution)/shard_map/pallas_call | solution.py:517
  243.2 6.2 %shard_map.393 = (bf16[16,128,512]{2,1,0:T(8,128)(2,1)}, bf16[16,128,512]{2,1,0:T(8,128)(2,1)}) custom-call(f32[1,1]{1,0:T(1,128)} %bitcast.f_ref, bf16[1024,1024]{1,0:T(8,128)(2,1)} %get-tuple-element.335.t_hbm, bf16[1024,1024]{1,0:T(8,128)(2,1)} %get-tuple-element.336.refs_0_), custom_call_target="tpu_custom_call" | custom-call | flops 2147483648 | bytes 6291456 | tf_op jit(solution)/shard_map/pallas_call | solution.py:657
  249.5 5.1 %collective-permute-done.43 = bf16[4,128,1024]{2,1,0:T(8,128)(2,1)S(1)} collective-permute-done((bf16[4,128,1024]{2,1,0:T(8,128)(2,1)S(1)}, bf16[4,128,1024]{2,1,0:T(8,128)(2,1)S(1)}, u32[]{:S(2)}, u32[]{:S(2)}) %collective-permute-start.43) | collective-permute-done | bytes 1048608 | tf_op jit(solution)/shard_map/ppermute | solution.py:77
  254.6 2.9 add_convert_fusion.4
  257.5 1.5 collective-permute-start.46
  259.0 14.0 %shard_map.394.refs_0_ = bf16[512,3072]{1,0:T(8,128)(2,1)} custom-call(bf16[1024,3072]{1,0:T(8,128)(2,1)} %get-tuple-element.244.j_ref, bf16[1024,1024]{1,0:T(8,128)(2,1)} %get-tuple-element.345.gm_ref, f32[4,16,256]{2,1,0:T(8,128)} %get-tuple-element.340.log_ref, s32[1024,1]{1,0:T(8,128)} %copy.66.sc_ref, s32[4,1,256]{2,1,0:T(1,128)} %bitcast.44), custom_call_target="tpu_custom_call" | custom-call | flops 5368709120 | bytes 7340032 | tf_op jit(solution)/shard_map/pallas_call | solution.py:570
  273.1 3.4 add_convert_fusion.1
  276.5 3.5 all-to-all-start.1
  280.0 4.4 %add_convert_fusion.2 = (bf16[4,128,1024]{2,1,0:T(8,128)(2,1)}, bf16[4,128,1024]{2,1,0:T(8,128)(2,1)S(1)}) fusion(bf16[16,128,1024]{2,1,0:T(8,128)(2,1)} %collective-permute-done.45, bf16[16,128,1024]{2,1,0:T(8,128)(2,1)} %get-tuple-element.341, bf16[4,128,1024]{2,1,0:T(8,128)(2,1)S(1)} %collective-permute-done.46), kind=kLoop, calls=%fused_computation.4 | loop fusion | flops 5242880 | bytes 7340032 | tf_op jit(solution)/shard_map/convert_element_type | solution.py:44
  286.4 13.8 %shard_map.395.refs_1_ = bf16[512,3072]{1,0:T(8,128)(2,1)} custom-call(bf16[1024,3072]{1,0:T(8,128)(2,1)} %get-tuple-element.244.j_ref, bf16[1024,1024]{1,0:T(8,128)(2,1)} %get-tuple-element.345.gm_ref, f32[4,16,256]{2,1,0:T(8,128)} %get-tuple-element.340.log_ref, s32[1024,1]{1,0:T(8,128)} %copy.66.sc_ref, s32[4,1,256]{2,1,0:T(1,128)} %bitcast.45), custom_call_target="tpu_custom_call" | custom-call | flops 5368709120 | bytes 7340032 | tf_op jit(solution)/shard_map/pallas_call | solution.py:570
  300.2 9.8 %shard_map.396 = (bf16[16,128,512]{2,1,0:T(8,128)(2,1)}, bf16[16,128,512]{2,1,0:T(8,128)(2,1)}) custom-call(f32[1,1]{1,0:T(1,128)} %bitcast.f_ref, bf16[1024,1024]{1,0:T(8,128)(2,1)} %get-tuple-element.346.t_hbm, bf16[512,3072]{1,0:T(8,128)(2,1)} %shard_map.394.refs_0_, bf16[512,3072]{1,0:T(8,128)(2,1)} %shard_map.395.refs_1_), custom_call_target="tpu_custom_call" | custom-call | flops 4294967296 | bytes 10485760 | tf_op jit(solution)/shard_map/pallas_call | solution.py:657
  311.6 6.3 %shard_map.397 = (bf16[16,128,512]{2,1,0:T(8,128)(2,1)}, bf16[16,128,512]{2,1,0:T(8,128)(2,1)}) custom-call(f32[1,1]{1,0:T(1,128)} %bitcast.f_ref, bf16[1024,1024]{1,0:T(8,128)(2,1)} %get-tuple-element.346.t_hbm, bf16[512,3072]{1,0:T(8,128)(2,1)} %shard_map.394.refs_0_, ...), custom_call_target="tpu_custom_call", output_to_operand_aliasing={{0}: (4, {}), {1}: (5, {})} | custom-call | flops 2147483648 | bytes 6291456 | tf_op jit(solution)/shard_map/pallas_call | solution.py:657
  319.2 2.0 add_convert_fusion.15
  322.2 4.1 add_convert_fusion
  326.2 5.3 %all-to-all-start.2 = ((bf16[4,128,1024]{2,1,0:T(8,128)(2,1)}), bf16[4,128,1024]{2,1,0:T(8,128)(2,1)}, u32[]{:S(2)}, u32[]{:S(2)}) async-start(bf16[4,128,1024]{2,1,0:T(8,128)(2,1)} %add_convert_fusion), calls=%async_computation.2 | async-start | bytes 2097152 | tf_op jit(solution)/shard_map/all_to_all | solution.py:81
  331.6 3.1 add_convert_fusion.13
  336.7 2.5 add_convert_fusion.10
  340.3 14.7 %shard_map.398 = (f32[1024,1024]{1,0:T(8,128)}, f32[2,1024]{1,0:T(2,128)}) custom-call(bf16[512,3072]{1,0:T(8,128)(2,1)} %shard_map.394.refs_0_, bf16[512,3072]{1,0:T(8,128)(2,1)} %shard_map.395.refs_1_, f32[1024,1024]{1,0:T(8,128)} %get-tuple-element.362.refs_2_, bf16[1024,1024]{1,0:T(8,128)(2,1)} %refs_3_.1, f32[4,1024]{1,0:T(4,128)} %refs_4_.1, ...), custom_call_target="tpu_custom_call" | custom-call | flops 6442450944 | bytes 23068672 | tf_op jit(solution)/shard_map/pallas_call | solution.py:617
  355.0 2.1 all-to-all-done.2
  359.3 2.4 add_convert_fusion.9
  361.8 4.3 %all-to-all-start.3 = ((bf16[4,128,512]{2,1,0:T(8,128)(2,1)}), bf16[4,128,512]{2,1,0:T(8,128)(2,1)}, u32[]{:S(2)}, u32[]{:S(2)}) async-start(bf16[4,128,512]{2,1,0:T(8,128)(2,1)} %add_convert_fusion.9), calls=%async_computation.3 | async-start | bytes 1048576 | tf_op jit(solution)/shard_map/all_to_all | solution.py:81
  371.0 3.0 collective-permute-done.61
  374.0 2.8 collective-permute-done.57
  376.8 4.4 %all-to-all-done.3 = bf16[4,128,512]{2,1,0:T(8,128)(2,1)} async-done(((bf16[4,128,512]{2,1,0:T(8,128)(2,1)}), bf16[4,128,512]{2,1,0:T(8,128)(2,1)}, u32[]{:S(2)}, u32[]{:S(2)}) %all-to-all-start.3) | async-done | bytes 524320 | tf_op jit(solution)/shard_map/all_to_all | solution.py:81
  381.2 2.1 collective-permute-done.62
  383.3 2.3 add_convert_fusion.8
  385.6 3.5 all-to-all-start.4
  394.1 2.8 fusion.9
  397.6 2.0 collective-permute-start.64
  399.7 1.5 fusion.7
  401.4 2.9 collective-permute-start.65
  (256 shorter events, 58.6 us)
Async XLA Ops:
  1.8 12.1 %collective-permute-start.1 = (bf16[128,512]{1,0:T(8,128)(2,1)S(1)}, bf16[128,512]{1,0:T(8,128)(2,1)S(1)}, u32[]{:S(2)}, u32[]{:S(2)}) collective-permute-start(bf16[128,512]{1,0:T(8,128)(2,1)S(1)} %get-tuple-element.451), channel_id=1, source_target_pairs={{16,0},{20,4},{24,8},{28,12},{0,16},{4,20},{8,24},{12,28},{17,1},{... | collective-permute-start | bytes 393224 | tf_op jit(solution)/shard_map/ppermute | solution.py:98
  5.9 8.0 %collective-permute-start = (bf16[128,512]{1,0:T(8,128)(2,1)S(1)}, bf16[128,512]{1,0:T(8,128)(2,1)S(1)}, u32[]{:S(2)}, u32[]{:S(2)}) collective-permute-start(bf16[128,512]{1,0:T(8,128)(2,1)S(1)} %get-tuple-element.451), channel_id=1, source_target_pairs={{8,0},{12,4},{16,8},{20,12},{24,16},{28,20},{0,24},{4,28},{9,1},{1... | collective-permute-start | bytes 393224 | tf_op jit(solution)/shard_map/ppermute | solution.py:98
  7.3 9.0 %collective-permute-start.2 = (bf16[128,512]{1,0:T(8,128)(2,1)S(1)}, bf16[128,512]{1,0:T(8,128)(2,1)S(1)}, u32[]{:S(2)}, u32[]{:S(2)}) collective-permute-start(bf16[128,512]{1,0:T(8,128)(2,1)S(1)} %get-tuple-element.451), channel_id=1, source_target_pairs={{24,0},{28,4},{0,8},{4,12},{8,16},{12,20},{16,24},{20,28},{25,1},{... | collective-permute-start | bytes 393224 | tf_op jit(solution)/shard_map/ppermute | solution.py:98
  18.3 11.0 %collective-permute-start.8 = (bf16[128,512]{1,0:T(8,128)(2,1)S(1)}, bf16[128,512]{1,0:T(8,128)(2,1)S(1)}, u32[]{:S(2)}, u32[]{:S(2)}) collective-permute-start(bf16[128,512]{1,0:T(8,128)(2,1)S(1)} %pad_maximum_fusion.12), channel_id=1, source_target_pairs={{24,0},{28,4},{0,8},{4,12},{8,16},{12,20},{16,24},{20,28},{25,1},{... | collective-permute-start | bytes 393224 | tf_op jit(solution)/shard_map/ppermute | solution.py:98
  20.7 10.7 %collective-permute-start.7 = (bf16[128,512]{1,0:T(8,128)(2,1)S(1)}, bf16[128,512]{1,0:T(8,128)(2,1)S(1)}, u32[]{:S(2)}, u32[]{:S(2)}) collective-permute-start(bf16[128,512]{1,0:T(8,128)(2,1)S(1)} %pad_maximum_fusion.12), channel_id=1, source_target_pairs={{16,0},{20,4},{24,8},{28,12},{0,16},{4,20},{8,24},{12,28},{17,1},{... | collective-permute-start | bytes 393224 | tf_op jit(solution)/shard_map/ppermute | solution.py:98
  22.6 8.8 %collective-permute-start.6 = (bf16[128,512]{1,0:T(8,128)(2,1)S(1)}, bf16[128,512]{1,0:T(8,128)(2,1)S(1)}, u32[]{:S(2)}, u32[]{:S(2)}) collective-permute-start(bf16[128,512]{1,0:T(8,128)(2,1)S(1)} %pad_maximum_fusion.12), channel_id=1, source_target_pairs={{8,0},{12,4},{16,8},{20,12},{24,16},{28,20},{0,24},{4,28},{9,1},{1... | collective-permute-start | bytes 393224 | tf_op jit(solution)/shard_map/ppermute | solution.py:98
  27.2 9.4 %collective-permute-start.4 = (bf16[4,128,512]{2,1,0:T(8,128)(2,1)S(1)}, bf16[4,128,512]{2,1,0:T(8,128)(2,1)}, u32[]{:S(2)}, u32[]{:S(2)}) collective-permute-start(bf16[4,128,512]{2,1,0:T(8,128)(2,1)S(1)} %pad_maximum_fusion.5.refs_0_), channel_id=1, source_target_pairs={{0,4},{1,3},{2,6},{3,1},{4,0},{5,7},{6,2},{7,5},{8,12},{9,11},{10,... | collective-permute-start | bytes 1572872 | tf_op jit(solution)/shard_map/ppermute | solution.py:77
  28.8 13.4 %collective-permute-start.5 = (bf16[4,128,512]{2,1,0:T(8,128)(2,1)S(1)}, bf16[4,128,512]{2,1,0:T(8,128)(2,1)}, u32[]{:S(2)}, u32[]{:S(2)}) collective-permute-start(bf16[4,128,512]{2,1,0:T(8,128)(2,1)S(1)} %collective-permute-done.3.refs_1_), channel_id=1, source_target_pairs={{0,4},{1,3},{2,6},{3,1},{4,0},{5,7},{6,2},{7,5},{8,12},{9,11},{10,... | collective-permute-start | bytes 1572872 | tf_op jit(solution)/shard_map/ppermute | solution.py:77
  31.5 10.7 %collective-permute-start.9 = (bf16[4,128,512]{2,1,0:T(8,128)(2,1)S(1)}, bf16[4,128,512]{2,1,0:T(8,128)(2,1)S(1)}, u32[]{:S(2)}, u32[]{:S(2)}) collective-permute-start(bf16[4,128,512]{2,1,0:T(8,128)(2,1)S(1)} %pad_maximum_fusion.6.refs_8_.refs_0_), channel_id=1, source_target_pairs={{0,1},{1,0},{2,3},{3,2},{4,5},{5,4},{6,7},{7,6},{8,9},{9,8},{10,11... | collective-permute-start | bytes 1572872 | tf_op jit(solution)/shard_map/ppermute | solution.py:68
  42.2 11.1 %collective-permute-start.15 = (bf16[128,1024]{1,0:T(8,128)(2,1)S(1)}, bf16[128,1024]{1,0:T(8,128)(2,1)S(1)}, u32[]{:S(2)}, u32[]{:S(2)}) collective-permute-start(bf16[128,1024]{1,0:T(8,128)(2,1)S(1)} %pad_maximum_fusion.10), channel_id=1, source_target_pairs={{24,0},{28,4},{0,8},{4,12},{8,16},{12,20},{16,24},{20,28},{25,1},{... | collective-permute-start | bytes 786440 | tf_op jit(solution)/shard_map/ppermute | solution.py:98
  42.2 21.7 %collective-permute-start.10 = (bf16[4,128,512]{2,1,0:T(8,128)(2,1)S(1)}, bf16[4,128,512]{2,1,0:T(8,128)(2,1)}, u32[]{:S(2)}, u32[]{:S(2)}) collective-permute-start(bf16[4,128,512]{2,1,0:T(8,128)(2,1)S(1)} %pad_maximum_fusion.6.refs_8_.refs_0_), channel_id=1, source_target_pairs={{0,4},{1,3},{2,6},{3,1},{4,0},{5,7},{6,2},{7,5},{8,12},{9,11},{10,... | collective-permute-start | bytes 1572872 | tf_op jit(solution)/shard_map/ppermute | solution.py:77
  43.7 20.1 %collective-permute-start.11 = (bf16[4,128,512]{2,1,0:T(8,128)(2,1)S(1)}, bf16[4,128,512]{2,1,0:T(8,128)(2,1)S(1)}, u32[]{:S(2)}, u32[]{:S(2)}) collective-permute-start(bf16[4,128,512]{2,1,0:T(8,128)(2,1)S(1)} %collective-permute-done.9.refs_9_.refs_1_), channel_id=1, source_target_pairs={{0,4},{1,3},{2,6},{3,1},{4,0},{5,7},{6,2},{7,5},{8,12},{9,11},{10,... | collective-permute-start | bytes 1572872 | tf_op jit(solution)/shard_map/ppermute | solution.py:77
  44.3 19.6 %collective-permute-start.12 = (bf16[4,128,512]{2,1,0:T(8,128)(2,1)}, bf16[4,128,512]{2,1,0:T(8,128)(2,1)S(1)}, u32[]{:S(2)}, u32[]{:S(2)}) collective-permute-start(bf16[4,128,512]{2,1,0:T(8,128)(2,1)} %collective-permute-done.4.refs_2_), channel_id=1, source_target_pairs={{0,2},{1,5},{2,0},{3,7},{4,6},{5,1},{6,4},{7,3},{8,10},{9,13},{10,... | collective-permute-start | bytes 1572872 | tf_op jit(solution)/shard_map/ppermute | solution.py:77
  45.8 16.2 %collective-permute-start.14 = (bf16[128,1024]{1,0:T(8,128)(2,1)S(1)}, bf16[128,1024]{1,0:T(8,128)(2,1)S(1)}, u32[]{:S(2)}, u32[]{:S(2)}) collective-permute-start(bf16[128,1024]{1,0:T(8,128)(2,1)S(1)} %pad_maximum_fusion.10), channel_id=1, source_target_pairs={{16,0},{20,4},{24,8},{28,12},{0,16},{4,20},{8,24},{12,28},{17,1},{... | collective-permute-start | bytes 786440 | tf_op jit(solution)/shard_map/ppermute | solution.py:98
  53.3 10.4 %collective-permute-start.13 = (bf16[128,1024]{1,0:T(8,128)(2,1)S(1)}, bf16[128,1024]{1,0:T(8,128)(2,1)S(1)}, u32[]{:S(2)}, u32[]{:S(2)}) collective-permute-start(bf16[128,1024]{1,0:T(8,128)(2,1)S(1)} %pad_maximum_fusion.10), channel_id=1, source_target_pairs={{8,0},{12,4},{16,8},{20,12},{24,16},{28,20},{0,24},{4,28},{9,1},{1... | collective-permute-start | bytes 786440 | tf_op jit(solution)/shard_map/ppermute | solution.py:98
  65.1 9.6 %collective-permute-start.20 = (bf16[4,128,1024]{2,1,0:T(8,128)(2,1)S(1)}, bf16[4,128,1024]{2,1,0:T(8,128)(2,1)S(1)}, u32[]{:S(2)}, u32[]{:S(2)}) collective-permute-start(bf16[4,128,1024]{2,1,0:T(8,128)(2,1)S(1)} %pad_maximum_fusion), channel_id=1, source_target_pairs={{0,1},{1,0},{2,3},{3,2},{4,5},{5,4},{6,7},{7,6},{8,9},{9,8},{10,11... | collective-permute-start | bytes 3145736 | tf_op jit(solution)/shard_map/ppermute | solution.py:68
  65.1 9.6 %collective-permute-start.19 = (bf16[4,128,512]{2,1,0:T(8,128)(2,1)}, bf16[4,128,512]{2,1,0:T(8,128)(2,1)}, u32[]{:S(2)}, u32[]{:S(2)}) collective-permute-start(bf16[4,128,512]{2,1,0:T(8,128)(2,1)} %collective-permute-done.10.refs_10_.refs_2_), channel_id=1, source_target_pairs={{0,2},{1,5},{2,0},{3,7},{4,6},{5,1},{6,4},{7,3},{8,10},{9,13},{10,... | collective-permute-start | bytes 1572872 | tf_op jit(solution)/shard_map/ppermute | solution.py:77
  66.7 8.5 %collective-permute-start.17 = (bf16[4,128,512]{2,1,0:T(8,128)(2,1)}, bf16[4,128,512]{2,1,0:T(8,128)(2,1)}, u32[]{:S(2)}, u32[]{:S(2)}) collective-permute-start(bf16[4,128,512]{2,1,0:T(8,128)(2,1)} %collective-permute-done.5.refs_3_), channel_id=1, source_target_pairs={{0,1},{1,0},{2,3},{3,2},{4,5},{5,4},{6,7},{7,6},{8,9},{9,8},{10,11... | collective-permute-start | bytes 1572872 | tf_op jit(solution)/shard_map/ppermute | solution.py:68
  66.9 10.7 %collective-permute-start.16 = (bf16[4,128,512]{2,1,0:T(8,128)(2,1)}, bf16[4,128,512]{2,1,0:T(8,128)(2,1)}, u32[]{:S(2)}, u32[]{:S(2)}) collective-permute-start(bf16[4,128,512]{2,1,0:T(8,128)(2,1)} %collective-permute-done.4.refs_2_), channel_id=1, source_target_pairs={{0,1},{1,0},{2,3},{3,2},{4,5},{5,4},{6,7},{7,6},{8,9},{9,8},{10,11... | collective-permute-start | bytes 1572872 | tf_op jit(solution)/shard_map/ppermute | solution.py:68
  67.2 10.5 %collective-permute-start.21 = (bf16[4,128,512]{2,1,0:T(8,128)(2,1)}, bf16[4,128,512]{2,1,0:T(8,128)(2,1)}, u32[]{:S(2)}, u32[]{:S(2)}) collective-permute-start(bf16[4,128,512]{2,1,0:T(8,128)(2,1)} %collective-permute-done.10.refs_10_.refs_2_), channel_id=1, source_target_pairs={{0,1},{1,0},{2,3},{3,2},{4,5},{5,4},{6,7},{7,6},{8,9},{9,8},{10,11... | collective-permute-start | bytes 1572872 | tf_op jit(solution)/shard_map/ppermute | solution.py:68
  67.4 32.1 %all-to-all-start = ((bf16[4,128,1024]{2,1,0:T(8,128)(2,1)}), bf16[4,128,1024]{2,1,0:T(8,128)(2,1)S(1)}, u32[]{:S(2)}, u32[]{:S(2)}) async-start(bf16[4,128,1024]{2,1,0:T(8,128)(2,1)} %broadcast_in_dim.11), calls=%async_computation | async-start | bytes 2097152 | tf_op jit(solution)/shard_map/all_to_all | solution.py:81
  74.7 2.8 collective-permute-start.18
  74.7 3.0 collective-permute-start.22
  75.7 2.8 collective-permute-start.23
  79.5 20.0 %collective-permute-start.24 = (bf16[8,128,512]{2,1,0:T(8,128)(2,1)}, bf16[8,128,512]{2,1,0:T(8,128)(2,1)}, u32[]{:S(2)}, u32[]{:S(2)}) collective-permute-start(bf16[8,128,512]{2,1,0:T(8,128)(2,1)} %pad_maximum_fusion.1), channel_id=1, source_target_pairs={{0,4},{1,3},{2,6},{3,1},{4,0},{5,7},{6,2},{7,5},{8,12},{9,11},{10,... | collective-permute-start | bytes 3145736 | tf_op jit(solution)/shard_map/ppermute | solution.py:77
  100.6 24.6 %collective-permute-start.28 = (bf16[8,128,512]{2,1,0:T(8,128)(2,1)}, bf16[8,128,512]{2,1,0:T(8,128)(2,1)}, u32[]{:S(2)}, u32[]{:S(2)}) collective-permute-start(bf16[8,128,512]{2,1,0:T(8,128)(2,1)} %collective-permute-done.24.refs_2_), channel_id=1, source_target_pairs={{0,1},{1,0},{2,3},{3,2},{4,5},{5,4},{6,7},{7,6},{8,9},{9,8},{10,11... | collective-permute-start | bytes 3145736 | tf_op jit(solution)/shard_map/ppermute | solution.py:68
  100.7 22.0 %collective-permute-start.25 = (bf16[4,128,512]{2,1,0:T(8,128)(2,1)S(1)}, bf16[4,128,512]{2,1,0:T(8,128)(2,1)}, u32[]{:S(2)}, u32[]{:S(2)}) collective-permute-start(bf16[4,128,512]{2,1,0:T(8,128)(2,1)S(1)} %slice.212), channel_id=1, source_target_pairs={{0,2},{1,5},{2,0},{3,7},{4,6},{5,1},{6,4},{7,3},{8,10},{9,13},{10,... | collective-permute-start | bytes 1572872 | tf_op jit(solution)/shard_map/ppermute | solution.py:77
  102.9 19.7 %collective-permute-start.26 = (bf16[8,128,512]{2,1,0:T(8,128)(2,1)}, bf16[8,128,512]{2,1,0:T(8,128)(2,1)}, u32[]{:S(2)}, u32[]{:S(2)}) collective-permute-start(bf16[8,128,512]{2,1,0:T(8,128)(2,1)} %pad_maximum_fusion.2), channel_id=1, source_target_pairs={{0,4},{1,3},{2,6},{3,1},{4,0},{5,7},{6,2},{7,5},{8,12},{9,11},{10,... | collective-permute-start | bytes 3145736 | tf_op jit(solution)/shard_map/ppermute | solution.py:77
  103.8 18.7 %collective-permute-start.27 = (bf16[4,128,1024]{2,1,0:T(8,128)(2,1)S(1)}, bf16[4,128,1024]{2,1,0:T(8,128)(2,1)S(1)}, u32[]{:S(2)}, u32[]{:S(2)}) collective-permute-start(bf16[4,128,1024]{2,1,0:T(8,128)(2,1)S(1)} %all-to-all-done), channel_id=1, source_target_pairs={{0,1},{1,0},{2,3},{3,2},{4,5},{5,4},{6,7},{7,6},{8,9},{9,8},{10,11... | collective-permute-start | bytes 3145736 | tf_op jit(solution)/shard_map/ppermute | solution.py:68
  122.7 2.5 collective-permute-start.29
  126.5 22.8 %collective-permute-start.32 = (bf16[8,128,512]{2,1,0:T(8,128)(2,1)}, bf16[8,128,512]{2,1,0:T(8,128)(2,1)}, u32[]{:S(2)}, u32[]{:S(2)}) collective-permute-start(bf16[8,128,512]{2,1,0:T(8,128)(2,1)} %collective-permute-done.26.refs_2_), channel_id=1, source_target_pairs={{0,1},{1,0},{2,3},{3,2},{4,5},{5,4},{6,7},{7,6},{8,9},{9,8},{10,11... | collective-permute-start | bytes 3145736 | tf_op jit(solution)/shard_map/ppermute | solution.py:68
  126.9 22.3 %collective-permute-start.30 = (bf16[4,128,512]{2,1,0:T(8,128)(2,1)S(1)}, bf16[4,128,512]{2,1,0:T(8,128)(2,1)}, u32[]{:S(2)}, u32[]{:S(2)}) collective-permute-start(bf16[4,128,512]{2,1,0:T(8,128)(2,1)S(1)} %slice.217), channel_id=1, source_target_pairs={{0,2},{1,5},{2,0},{3,7},{4,6},{5,1},{6,4},{7,3},{8,10},{9,13},{10,... | collective-permute-start | bytes 1572872 | tf_op jit(solution)/shard_map/ppermute | solution.py:77
  128.5 20.7 %collective-permute-start.31 = (bf16[8,128,512]{2,1,0:T(8,128)(2,1)S(1)}, bf16[8,128,512]{2,1,0:T(8,128)(2,1)}, u32[]{:S(2)}, u32[]{:S(2)}) collective-permute-start(bf16[8,128,512]{2,1,0:T(8,128)(2,1)S(1)} %pad_maximum_fusion.3), channel_id=1, source_target_pairs={{0,4},{1,3},{2,6},{3,1},{4,0},{5,7},{6,2},{7,5},{8,12},{9,11},{10,... | collective-permute-start | bytes 3145736 | tf_op jit(solution)/shard_map/ppermute | solution.py:77
  152.6 22.4 %collective-permute-start.36 = (bf16[8,128,512]{2,1,0:T(8,128)(2,1)}, bf16[8,128,512]{2,1,0:T(8,128)(2,1)}, u32[]{:S(2)}, u32[]{:S(2)}) collective-permute-start(bf16[8,128,512]{2,1,0:T(8,128)(2,1)} %collective-permute-done.31.refs_2_), channel_id=1, source_target_pairs={{0,1},{1,0},{2,3},{3,2},{4,5},{5,4},{6,7},{7,6},{8,9},{9,8},{10,11... | collective-permute-start | bytes 3145736 | tf_op jit(solution)/shard_map/ppermute | solution.py:68
  152.8 22.1 %collective-permute-start.34 = (bf16[4,128,512]{2,1,0:T(8,128)(2,1)S(1)}, bf16[4,128,512]{2,1,0:T(8,128)(2,1)S(1)}, u32[]{:S(2)}, u32[]{:S(2)}) collective-permute-start(bf16[4,128,512]{2,1,0:T(8,128)(2,1)S(1)} %slice.218), channel_id=1, source_target_pairs={{0,2},{1,5},{2,0},{3,7},{4,6},{5,1},{6,4},{7,3},{8,10},{9,13},{10,... | collective-permute-start | bytes 1572872 | tf_op jit(solution)/shard_map/ppermute | solution.py:77
  154.0 20.9 %collective-permute-start.35 = (bf16[8,128,512]{2,1,0:T(8,128)(2,1)S(1)}, bf16[8,128,512]{2,1,0:T(8,128)(2,1)S(1)}, u32[]{:S(2)}, u32[]{:S(2)}) collective-permute-start(bf16[8,128,512]{2,1,0:T(8,128)(2,1)S(1)} %pad_maximum_fusion.4), channel_id=1, source_target_pairs={{0,4},{1,3},{2,6},{3,1},{4,0},{5,7},{6,2},{7,5},{8,12},{9,11},{10,... | collective-permute-start | bytes 3145736 | tf_op jit(solution)/shard_map/ppermute | solution.py:77
  177.7 22.2 %collective-permute-start.39 = (bf16[16,128,1024]{2,1,0:T(8,128)(2,1)}, bf16[16,128,1024]{2,1,0:T(8,128)(2,1)}, u32[]{:S(2)}, u32[]{:S(2)}) collective-permute-start(bf16[16,128,1024]{2,1,0:T(8,128)(2,1)} %get-tuple-element.307), channel_id=1, source_target_pairs={{0,1},{1,0},{2,3},{3,2},{4,5},{5,4},{6,7},{7,6},{8,9},{9,8},{10,11... | collective-permute-start | bytes 12582920 | tf_op jit(solution)/shard_map/ppermute | solution.py:68
  177.9 22.1 %collective-permute-start.40 = (bf16[8,128,512]{2,1,0:T(8,128)(2,1)S(1)}, bf16[8,128,512]{2,1,0:T(8,128)(2,1)S(1)}, u32[]{:S(2)}, u32[]{:S(2)}) collective-permute-start(bf16[8,128,512]{2,1,0:T(8,128)(2,1)S(1)} %collective-permute-done.35.refs_2_), channel_id=1, source_target_pairs={{0,1},{1,0},{2,3},{3,2},{4,5},{5,4},{6,7},{7,6},{8,9},{9,8},{10,11... | collective-permute-start | bytes 3145736 | tf_op jit(solution)/shard_map/ppermute | solution.py:68
  178.3 21.6 %collective-permute-start.38 = (bf16[4,128,512]{2,1,0:T(8,128)(2,1)S(1)}, bf16[4,128,512]{2,1,0:T(8,128)(2,1)S(1)}, u32[]{:S(2)}, u32[]{:S(2)}) collective-permute-start(bf16[4,128,512]{2,1,0:T(8,128)(2,1)S(1)} %slice.219), channel_id=1, source_target_pairs={{0,2},{1,5},{2,0},{3,7},{4,6},{5,1},{6,4},{7,3},{8,10},{9,13},{10,... | collective-permute-start | bytes 1572872 | tf_op jit(solution)/shard_map/ppermute | solution.py:77
  204.1 20.9 %collective-permute-start.42 = (bf16[4,128,1024]{2,1,0:T(8,128)(2,1)S(1)}, bf16[4,128,1024]{2,1,0:T(8,128)(2,1)S(1)}, u32[]{:S(2)}, u32[]{:S(2)}) collective-permute-start(bf16[4,128,1024]{2,1,0:T(8,128)(2,1)S(1)} %add_convert_fusion.7), channel_id=1, source_target_pairs={{0,2},{1,5},{2,0},{3,7},{4,6},{5,1},{6,4},{7,3},{8,10},{9,13},{10,... | collective-permute-start | bytes 3145736 | tf_op jit(solution)/shard_map/ppermute | solution.py:77
  224.9 29.6 %collective-permute-start.45 = (bf16[16,128,1024]{2,1,0:T(8,128)(2,1)}, bf16[16,128,1024]{2,1,0:T(8,128)(2,1)}, u32[]{:S(2)}, u32[]{:S(2)}) collective-permute-start(bf16[16,128,1024]{2,1,0:T(8,128)(2,1)} %get-tuple-element.334), channel_id=1, source_target_pairs={{0,1},{1,0},{2,3},{3,2},{4,5},{5,4},{6,7},{7,6},{8,9},{9,8},{10,11... | collective-permute-start | bytes 12582920 | tf_op jit(solution)/shard_map/ppermute | solution.py:68
  228.5 21.0 %collective-permute-start.44 = (bf16[4,128,1024]{2,1,0:T(8,128)(2,1)S(1)}, bf16[4,128,1024]{2,1,0:T(8,128)(2,1)}, u32[]{:S(2)}, u32[]{:S(2)}) collective-permute-start(bf16[4,128,1024]{2,1,0:T(8,128)(2,1)S(1)} %get-tuple-element.423), channel_id=1, source_target_pairs={{0,4},{1,3},{2,6},{3,1},{4,0},{5,7},{6,2},{7,5},{8,12},{9,11},{10,... | collective-permute-start | bytes 3145736 | tf_op jit(solution)/shard_map/ppermute | solution.py:77
  229.9 24.7 %collective-permute-start.43 = (bf16[4,128,1024]{2,1,0:T(8,128)(2,1)S(1)}, bf16[4,128,1024]{2,1,0:T(8,128)(2,1)S(1)}, u32[]{:S(2)}, u32[]{:S(2)}) collective-permute-start(bf16[4,128,1024]{2,1,0:T(8,128)(2,1)S(1)} %get-tuple-element.424), channel_id=1, source_target_pairs={{0,4},{1,3},{2,6},{3,1},{4,0},{5,7},{6,2},{7,5},{8,12},{9,11},{10,... | collective-permute-start | bytes 3145736 | tf_op jit(solution)/shard_map/ppermute | solution.py:77
  257.5 15.6 %collective-permute-start.46 = (bf16[4,128,1024]{2,1,0:T(8,128)(2,1)}, bf16[4,128,1024]{2,1,0:T(8,128)(2,1)S(1)}, u32[]{:S(2)}, u32[]{:S(2)}) collective-permute-start(bf16[4,128,1024]{2,1,0:T(8,128)(2,1)} %add_convert_fusion.4), channel_id=1, source_target_pairs={{0,2},{1,5},{2,0},{3,7},{4,6},{5,1},{6,4},{7,3},{8,10},{9,13},{10,... | collective-permute-start | bytes 3145736 | tf_op jit(solution)/shard_map/ppermute | solution.py:77
  259.0 14.0 %collective-permute-start.47 = (bf16[4,128,1024]{2,1,0:T(8,128)(2,1)}, bf16[4,128,1024]{2,1,0:T(8,128)(2,1)S(1)}, u32[]{:S(2)}, u32[]{:S(2)}) collective-permute-start(bf16[4,128,1024]{2,1,0:T(8,128)(2,1)} %collective-permute-done.44), channel_id=1, source_target_pairs={{0,1},{1,0},{2,3},{3,2},{4,5},{5,4},{6,7},{7,6},{8,9},{9,8},{10,11... | collective-permute-start | bytes 3145736 | tf_op jit(solution)/shard_map/ppermute | solution.py:68
  276.5 34.5 %all-to-all-start.1 = ((bf16[4,128,1024]{2,1,0:T(8,128)(2,1)}), bf16[4,128,1024]{2,1,0:T(8,128)(2,1)S(1)}, u32[]{:S(2)}, u32[]{:S(2)}) async-start(bf16[4,128,1024]{2,1,0:T(8,128)(2,1)} %add_convert_fusion.1), calls=%async_computation.1 | async-start | bytes 2097152 | tf_op jit(solution)/shard_map/all_to_all | solution.py:81
  284.4 25.7 %collective-permute-start.49 = (bf16[4,128,1024]{2,1,0:T(8,128)(2,1)}, bf16[4,128,1024]{2,1,0:T(8,128)(2,1)S(1)}, u32[]{:S(2)}, u32[]{:S(2)}) collective-permute-start(bf16[4,128,1024]{2,1,0:T(8,128)(2,1)} %get-tuple-element.421), channel_id=1, source_target_pairs={{0,4},{1,3},{2,6},{3,1},{4,0},{5,7},{6,2},{7,5},{8,12},{9,11},{10,... | collective-permute-start | bytes 3145736 | tf_op jit(solution)/shard_map/ppermute | solution.py:77
  285.2 25.8 %collective-permute-start.48 = (bf16[4,128,1024]{2,1,0:T(8,128)(2,1)S(1)}, bf16[4,128,1024]{2,1,0:T(8,128)(2,1)}, u32[]{:S(2)}, u32[]{:S(2)}) collective-permute-start(bf16[4,128,1024]{2,1,0:T(8,128)(2,1)S(1)} %get-tuple-element.422), channel_id=1, source_target_pairs={{0,4},{1,3},{2,6},{3,1},{4,0},{5,7},{6,2},{7,5},{8,12},{9,11},{10,... | collective-permute-start | bytes 3145736 | tf_op jit(solution)/shard_map/ppermute | solution.py:77
  311.1 6.9 %collective-permute-start.50 = (bf16[16,128,512]{2,1,0:T(8,128)(2,1)}, bf16[16,128,512]{2,1,0:T(8,128)(2,1)S(1)}, u32[]{:S(2)}, u32[]{:S(2)}) collective-permute-start(bf16[16,128,512]{2,1,0:T(8,128)(2,1)} %get-tuple-element.354), channel_id=1, source_target_pairs={{0,1},{1,0},{2,3},{3,2},{4,5},{5,4},{6,7},{7,6},{8,9},{9,8},{10,11... | collective-permute-start | bytes 6291464 | tf_op jit(solution)/shard_map/ppermute | solution.py:68
  311.1 6.9 %collective-permute-start.51 = (bf16[4,128,1024]{2,1,0:T(8,128)(2,1)}, bf16[4,128,1024]{2,1,0:T(8,128)(2,1)}, u32[]{:S(2)}, u32[]{:S(2)}) collective-permute-start(bf16[4,128,1024]{2,1,0:T(8,128)(2,1)} %copy-done.41), channel_id=1, source_target_pairs={{0,1},{1,0},{2,3},{3,2},{4,5},{5,4},{6,7},{7,6},{8,9},{9,8},{10,11... | collective-permute-start | bytes 3145736 | tf_op jit(solution)/shard_map/ppermute | solution.py:68
  317.9 13.6 %collective-permute-start.53 = (bf16[16,128,512]{2,1,0:T(8,128)(2,1)}, bf16[16,128,512]{2,1,0:T(8,128)(2,1)}, u32[]{:S(2)}, u32[]{:S(2)}) collective-permute-start(bf16[16,128,512]{2,1,0:T(8,128)(2,1)} %get-tuple-element.368), channel_id=1, source_target_pairs={{0,1},{1,0},{2,3},{3,2},{4,5},{5,4},{6,7},{7,6},{8,9},{9,8},{10,11... | collective-permute-start | bytes 6291464 | tf_op jit(solution)/shard_map/ppermute | solution.py:68
  321.2 10.3 %collective-permute-start.52 = (bf16[4,128,512]{2,1,0:T(8,128)(2,1)}, bf16[4,128,512]{2,1,0:T(8,128)(2,1)}, u32[]{:S(2)}, u32[]{:S(2)}) collective-permute-start(bf16[4,128,512]{2,1,0:T(8,128)(2,1)} %add_convert_fusion.15), channel_id=1, source_target_pairs={{0,2},{1,5},{2,0},{3,7},{4,6},{5,1},{6,4},{7,3},{8,10},{9,13},{10,... | collective-permute-start | bytes 1572872 | tf_op jit(solution)/shard_map/ppermute | solution.py:77
  326.2 30.9 %all-to-all-start.2 = ((bf16[4,128,1024]{2,1,0:T(8,128)(2,1)}), bf16[4,128,1024]{2,1,0:T(8,128)(2,1)}, u32[]{:S(2)}, u32[]{:S(2)}) async-start(bf16[4,128,1024]{2,1,0:T(8,128)(2,1)} %add_convert_fusion), calls=%async_computation.2 | async-start | bytes 2097152 | tf_op jit(solution)/shard_map/all_to_all | solution.py:81
  334.7 22.4 %collective-permute-start.55 = (bf16[4,128,512]{2,1,0:T(8,128)(2,1)}, bf16[4,128,512]{2,1,0:T(8,128)(2,1)}, u32[]{:S(2)}, u32[]{:S(2)}) collective-permute-start(bf16[4,128,512]{2,1,0:T(8,128)(2,1)} %get-tuple-element.427), channel_id=1, source_target_pairs={{0,4},{1,3},{2,6},{3,1},{4,0},{5,7},{6,2},{7,5},{8,12},{9,11},{10,... | collective-permute-start | bytes 1572872 | tf_op jit(solution)/shard_map/ppermute | solution.py:77
  335.6 21.5 %collective-permute-start.54 = (bf16[4,128,512]{2,1,0:T(8,128)(2,1)}, bf16[4,128,512]{2,1,0:T(8,128)(2,1)}, u32[]{:S(2)}, u32[]{:S(2)}) collective-permute-start(bf16[4,128,512]{2,1,0:T(8,128)(2,1)} %get-tuple-element.428), channel_id=1, source_target_pairs={{0,4},{1,3},{2,6},{3,1},{4,0},{5,7},{6,2},{7,5},{8,12},{9,11},{10,... | collective-permute-start | bytes 1572872 | tf_op jit(solution)/shard_map/ppermute | solution.py:77
  339.2 18.0 %collective-permute-start.56 = (bf16[4,128,512]{2,1,0:T(8,128)(2,1)}, bf16[4,128,512]{2,1,0:T(8,128)(2,1)}, u32[]{:S(2)}, u32[]{:S(2)}) collective-permute-start(bf16[4,128,512]{2,1,0:T(8,128)(2,1)} %get-tuple-element.426), channel_id=1, source_target_pairs={{0,2},{1,5},{2,0},{3,7},{4,6},{5,1},{6,4},{7,3},{8,10},{9,13},{10,... | collective-permute-start | bytes 1572872 | tf_op jit(solution)/shard_map/ppermute | solution.py:77
  357.2 16.8 %collective-permute-start.58 = (bf16[4,128,512]{2,1,0:T(8,128)(2,1)}, bf16[4,128,512]{2,1,0:T(8,128)(2,1)}, u32[]{:S(2)}, u32[]{:S(2)}) collective-permute-start(bf16[4,128,512]{2,1,0:T(8,128)(2,1)} %get-tuple-element.425), channel_id=1, source_target_pairs={{0,4},{1,3},{2,6},{3,1},{4,0},{5,7},{6,2},{7,5},{8,12},{9,11},{10,... | collective-permute-start | bytes 1572872 | tf_op jit(solution)/shard_map/ppermute | solution.py:77
  361.8 19.4 %all-to-all-start.3 = ((bf16[4,128,512]{2,1,0:T(8,128)(2,1)}), bf16[4,128,512]{2,1,0:T(8,128)(2,1)}, u32[]{:S(2)}, u32[]{:S(2)}) async-start(bf16[4,128,512]{2,1,0:T(8,128)(2,1)} %add_convert_fusion.9), calls=%async_computation.3 | async-start | bytes 1048576 | tf_op jit(solution)/shard_map/all_to_all | solution.py:81
  367.4 9.4 %collective-permute-start.57 = (bf16[4,128,512]{2,1,0:T(8,128)(2,1)S(1)}, bf16[4,128,512]{2,1,0:T(8,128)(2,1)}, u32[]{:S(2)}, u32[]{:S(2)}) collective-permute-start(bf16[4,128,512]{2,1,0:T(8,128)(2,1)S(1)} %add_convert_fusion.11), channel_id=1, source_target_pairs={{0,4},{1,3},{2,6},{3,1},{4,0},{5,7},{6,2},{7,5},{8,12},{9,11},{10,... | collective-permute-start | bytes 1572872 | tf_op jit(solution)/shard_map/ppermute | solution.py:77
  370.0 4.0 collective-permute-start.61
  385.6 21.1 %all-to-all-start.4 = ((bf16[4,128,512]{2,1,0:T(8,128)(2,1)}), bf16[4,128,512]{2,1,0:T(8,128)(2,1)S(1)}, u32[]{:S(2)}, u32[]{:S(2)}) async-start(bf16[4,128,512]{2,1,0:T(8,128)(2,1)} %add_convert_fusion.8), calls=%async_computation.4 | async-start | bytes 1048576 | tf_op jit(solution)/shard_map/all_to_all | solution.py:81
  390.7 6.1 %collective-permute-start.63 = (f32[4,1024]{1,0:T(4,128)S(1)}, f32[4,1024]{1,0:T(4,128)}, u32[]{:S(2)}, u32[]{:S(2)}) collective-permute-start(f32[4,1024]{1,0:T(4,128)S(1)} %add.200), channel_id=1, source_target_pairs={{0,4},{4,0},{8,12},{12,8},{16,20},{20,16},{24,28},{28,24},{1,5},{5... | collective-permute-start | bytes 49160 | tf_op jit(solution)/shard_map/ppermute | solution.py:87
  397.6 3.7 collective-permute-start.64
  401.4 4.7 %collective-permute-start.65 = (f32[4,1024]{1,0:T(4,128)S(1)}, f32[4,1024]{1,0:T(4,128)S(1)}, u32[]{:S(2)}, u32[]{:S(2)}) collective-permute-start(f32[4,1024]{1,0:T(4,128)S(1)} %add.225), channel_id=1, source_target_pairs={{0,16},{4,20},{8,24},{12,28},{16,0},{20,4},{24,8},{28,12},{1,17},{... | collective-permute-start | bytes 49160 | tf_op jit(solution)/shard_map/ppermute | solution.py:87
  (56 other events, 489.6 us)
